TPU v7x, 32 devices: a whole 2x2x4 slice. The times are simulated.
32 devices in a mesh: dp: 8 (over z, core), tensor: 4 (over y, x).
Axes of the slice: x: 2, y: 2, z: 4, core: 2. Of those that a mesh axis runs over, the one named last changes fastest.
Arguments:
- tokens: bfloat16 [2, 4096, 2048], P(None, ('dp', 'tensor')), may hold values from -6 to 6
- cotangent: bfloat16 [2, 4096, 2048], P(None, ('dp', 'tensor')), may hold values from -6 to 6
- mixer: bfloat16 [2048, 6144], P('dp', 'tensor'), may hold values from -0.125 to 0.125
- merger: bfloat16 [2048, 2048], P('tensor', 'dp'), may hold values from -1.5 to 1.5
- expand: bfloat16 [2048, 8192], P('dp', 'tensor'), may hold values from -0.125 to 0.125
- shrink: bfloat16 [8192, 2048], P('tensor', 'dp'), may hold values from -0.0625 to 0.0625
- attend_gain: bfloat16 [2048], replicated, may hold values from 0.5 to 1.5
- attend_bias: bfloat16 [2048], replicated, may hold values from -0.59765625 to 0.59765625
- feed_gain: bfloat16 [2048], replicated, may hold values from 0.5 to 1.5
- feed_bias: bfloat16 [2048], replicated, may hold values from -0.59765625 to 0.59765625
- width_router: bfloat16 [2048, 4], replicated, may hold values from -0.09375 to 0.09375
- head_router: bfloat16 [2048, 4], replicated, may hold values from -0.8984375 to 0.8984375
- lengths: int32 [2, 32], P(None, 'dp'), may hold values from 0 to 512, as said below
- head_choice: int32 [2, 32], P(None, 'dp'), may hold values from 0 to 3
- width_bucket: int32 [2, 4096], P(None, 'dp'), may hold values from 0 to 3
Outputs:
- block_output: bfloat16 [2, 4096, 2048], P(None, ('dp', 'tensor'))
- tokens_gradient: float32 [2, 4096, 2048], P(None, ('dp', 'tensor'))
- mixer_gradient: float32 [2048, 6144], P('dp', 'tensor')
- merger_gradient: float32 [2048, 2048], P('tensor', 'dp')
- expand_gradient: float32 [2048, 8192], P('dp', 'tensor')
- shrink_gradient: float32 [8192, 2048], P('tensor', 'dp')
- attend_gain_gradient: float32 [2048], replicated
- attend_bias_gradient: float32 [2048], replicated
- feed_gain_gradient: float32 [2048], replicated
- feed_bias_gradient: float32 [2048], replicated
- width_router_gradient: float32 [2048, 4], replicated
- head_router_gradient: float32 [2048, 4], replicated
- width_usage: float32 [4], replicated
- head_usage: float32 [4], replicated
Inputs may be any that keep to these rules, and one draw needn't show every extreme that they name: For each micro-batch and each of the 8 buffers the 4 lengths sum to between 256 and 512; in each micro-batch one buffer holds a single sequence of 512 tokens.
All inputs are finite; a program needn't handle non-finite values.
Results may differ from a plain program's by a relative error of at most 0.012.
The roundings to bfloat16 on the way count: a program that leaves them out, or rounds other values in their place, can miss the bound.
Values may be sent and summed in bfloat16 or wider, within the bound.
A program may use at most 256 MiB of HBM per device.

v0:
```python
import jax
import jax.numpy as jnp
from jax import lax
from jax.sharding import PartitionSpec as P

H = 16
HD = 128
FF = 8192
NB = 4
NHC = 4


EPSILON = 1e-05
HIGHEST = lax.Precision.HIGHEST
MASKED = -1e30


def contract_rows(left, right):
    return lax.dot_general(
        left, right, (((0,), (0,)), ((), ())), preferred_element_type=jnp.float32
    )


def contract_cols(left, right):
    return lax.dot_general(
        left, right, (((1,), (1,)), ((), ())), preferred_element_type=jnp.float32
    )


def layout(lengths, slots_total):
    slot_count = lengths.shape[0]
    ends = jnp.cumsum(lengths, dtype=jnp.int32)
    starts = ends - lengths
    filled = ends[-1]
    slots = jnp.arange(slots_total, dtype=jnp.int32)
    member = jnp.sum((ends[None, :] <= slots[:, None]).astype(jnp.int32), axis=1, dtype=jnp.int32)
    begins = jnp.concatenate([starts, filled[None]])
    onehot = member[:, None] == jnp.arange(slot_count + 1, dtype=jnp.int32)[None, :]
    place = slots - jnp.sum(jnp.where(onehot, begins[None, :], 0), axis=1, dtype=jnp.int32)
    return (member, place, slots < filled, onehot[:, :slot_count])


def normalize(value):
    centred = value - jnp.mean(value, axis=-1, keepdims=True)
    inverse = lax.rsqrt(jnp.mean(centred * centred, axis=-1, keepdims=True) + EPSILON)
    return (centred * inverse, inverse)


def norm_back(back, normed, inverse, gain):
    scaled = back * gain
    inner = jnp.mean(scaled, axis=-1, keepdims=True)
    along = jnp.mean(scaled * normed, axis=-1, keepdims=True)
    return inverse * (scaled - inner - normed * along)


def rotary_tables(place, width):
    half = width // 2
    rates = jnp.power(10000.0, -2.0 * jnp.arange(half, dtype=jnp.float32) / width)
    angles = place.astype(jnp.float32)[:, None] * rates[None, :]
    cosine = jnp.cos(angles)
    sine = jnp.sin(angles)
    return (jnp.concatenate([cosine, cosine], axis=1), jnp.concatenate([sine, sine], axis=1))


def rotate(value, cosine, sine):
    half = value.shape[-1] // 2
    turned = jnp.concatenate([-value[..., half:], value[..., :half]], axis=-1)
    return value * cosine + turned * sine


def rotate_back(grad_value, cosine, sine):
    moved = grad_value * sine
    half = moved.shape[-1] // 2
    return grad_value * cosine + jnp.concatenate([moved[..., half:], -moved[..., :half]], axis=-1)


def softmax_rows(logits):
    powers = jnp.exp(logits - jnp.max(logits, axis=-1, keepdims=True))
    return powers / jnp.sum(powers, axis=-1, keepdims=True)


def visible(member, slots):
    return (member[:, None] == member[None, :]) & (slots[:, None] >= slots[None, :])


def block_scores(query, keys, member, slots):
    scale = query.shape[-1] ** (-0.5)
    scores = jnp.einsum("qhd,khd->hqk", query, keys, preferred_element_type=jnp.float32) * scale
    return jnp.where(visible(member, slots)[None], scores, MASKED)


def attend_forward(query, keys, values, member):
    total = keys.shape[0]
    slots = jnp.arange(total, dtype=jnp.int32)
    scores = block_scores(query, keys, member, slots)
    peak = jnp.max(scores, axis=-1, keepdims=True)
    powers = jnp.exp(scores - peak)
    mass = jnp.sum(powers, axis=-1, keepdims=True)
    share = (powers / mass).astype(jnp.bfloat16)
    pieces = jnp.einsum("hqk,khd->qhd", share, values, preferred_element_type=jnp.float32)
    totals = peak + jnp.log(mass)
    return (pieces, totals)


def attend_backward(query, keys, values, member, log_total, heads_back):
    total = keys.shape[0]
    scale = query.shape[-1] ** (-0.5)
    slots = jnp.arange(total, dtype=jnp.int32)
    scores = block_scores(query, keys, member, slots)
    share = jnp.exp(scores - log_total)
    share_back = jnp.einsum("qhd,khd->hqk", heads_back, values, preferred_element_type=jnp.float32)
    inner = jnp.sum(share * share_back, axis=-1, keepdims=True)
    score_back = (share * (share_back - inner)).astype(jnp.bfloat16)
    query_parts = (
        jnp.einsum("hqk,khd->qhd", score_back, keys, preferred_element_type=jnp.float32) * scale
    )
    keys_back = (
        jnp.einsum("hqk,qhd->khd", score_back, query, preferred_element_type=jnp.float32) * scale
    )
    values_back = jnp.einsum(
        "hqk,qhd->khd", share.astype(jnp.bfloat16), heads_back, preferred_element_type=jnp.float32
    )
    return (query_parts, keys_back, values_back)


def local(
    tokens,
    cotangent,
    mixer,
    merger,
    expand,
    shrink,
    attend_gain,
    attend_bias,
    feed_gain,
    feed_bias,
    width_router,
    head_router,
    lengths,
    head_choice,
    width_bucket,
):
    rank = lax.axis_index("tensor")
    micro, rows, width = tokens.shape
    total = width_bucket.shape[1]
    heads_local = merger.shape[0] // HD
    units_local = expand.shape[1]
    first_start = rank * rows
    head_ids = rank * heads_local + jnp.arange(heads_local, dtype=jnp.int32)
    unit_ids = rank * units_local + jnp.arange(units_local, dtype=jnp.int32)
    gain_one = attend_gain.astype(jnp.float32)
    bias_one = attend_bias.astype(jnp.float32)
    gain_two = feed_gain.astype(jnp.float32)
    bias_two = feed_bias.astype(jnp.float32)
    router_width = width_router.astype(jnp.float32)
    router_head = head_router.astype(jnp.float32)
    sums = tuple((jnp.zeros(piece.shape, jnp.float32) for piece in (mixer, merger, expand, shrink)))
    gain_one_sum = jnp.zeros((width,), jnp.float32)
    bias_one_sum = jnp.zeros((width,), jnp.float32)
    gain_two_sum = jnp.zeros((width,), jnp.float32)
    bias_two_sum = jnp.zeros((width,), jnp.float32)
    width_router_sum = jnp.zeros(width_router.shape, jnp.float32)
    head_router_sum = jnp.zeros(head_router.shape, jnp.float32)
    width_use = jnp.zeros((NB,), jnp.float32)
    head_use = jnp.zeros((NHC,), jnp.float32)
    outputs = []
    input_backs = []
    for micro_index in range(micro):
        forward_weights = (
            lax.all_gather(mixer, "dp", axis=0, tiled=True),
            lax.all_gather(merger, "dp", axis=1, tiled=True),
            lax.all_gather(expand, "dp", axis=0, tiled=True),
            lax.all_gather(shrink, "dp", axis=1, tiled=True),
        )
        mix_weight, out_weight, up_weight, down_weight = forward_weights
        member, place, live, seqmask = layout(lengths[micro_index], total)
        seq_float = seqmask.astype(jnp.float32)
        own_seq = lax.dynamic_slice_in_dim(seq_float, first_start, rows, 0)
        own_live = lax.dynamic_slice_in_dim(live.astype(jnp.float32), first_start, rows, 0)
        buckets = width_bucket[micro_index]
        own_buckets = lax.dynamic_slice_in_dim(buckets, first_start, rows, 0)
        choices = head_choice[micro_index]
        inputs = tokens[micro_index].astype(jnp.float32)
        first_normed, first_inverse = normalize(inputs)
        first_low = (first_normed * gain_one + bias_one).astype(jnp.bfloat16)
        first_rows = lax.all_gather(first_low, "tensor", axis=0, tiled=True)
        divisor = jnp.maximum(jnp.sum(seq_float, axis=0), 1.0)
        means = (
            jnp.dot(
                seq_float.T.astype(jnp.bfloat16), first_rows, preferred_element_type=jnp.float32
            )
            / divisor[:, None]
        )
        head_share = softmax_rows(jnp.dot(means, router_head, precision=HIGHEST))
        choice_hot = (choices[:, None] == jnp.arange(NHC, dtype=jnp.int32)[None, :]).astype(
            jnp.float32
        )
        picked_head = jnp.sum(head_share * choice_hot, axis=1)
        seq_gate = NHC * picked_head
        own_gate = jnp.sum(own_seq * seq_gate[None, :], axis=1)
        heads_used = jnp.sum(
            jnp.where(seqmask, H // NHC * (choices[None, :] + 1), 0), axis=1, dtype=jnp.int32
        )
        head_on = (head_ids[None, :] < heads_used[:, None]).astype(jnp.bfloat16)
        mixed = jnp.dot(first_rows, mix_weight, preferred_element_type=jnp.float32).reshape(
            total, heads_local, 3, HD
        )
        cosine, sine = rotary_tables(place, HD)
        cosine = cosine[:, None, :]
        sine = sine[:, None, :]
        query = rotate(mixed[:, :, 0], cosine, sine).astype(jnp.bfloat16)
        keys = rotate(mixed[:, :, 1], cosine, sine).astype(jnp.bfloat16)
        values = mixed[:, :, 2].astype(jnp.bfloat16)
        attended, log_total = attend_forward(query, keys, values, member)
        head_rows = (attended.astype(jnp.bfloat16) * head_on[:, :, None]).reshape(
            total, heads_local * HD
        )
        attention_part = jnp.dot(head_rows, out_weight, preferred_element_type=jnp.float32)
        attention_own = lax.psum_scatter(attention_part, "tensor", scatter_dimension=0, tiled=True)
        hidden = inputs + own_gate[:, None] * attention_own
        second_normed, second_inverse = normalize(hidden)
        second_low = (second_normed * gain_two + bias_two).astype(jnp.bfloat16)
        second_value = second_low.astype(jnp.float32)
        width_share = softmax_rows(
            jnp.dot(second_low, width_router, preferred_element_type=jnp.float32)
        )
        bucket_hot = (own_buckets[:, None] == jnp.arange(NB, dtype=jnp.int32)[None, :]).astype(
            jnp.float32
        )
        picked_width = jnp.sum(width_share * bucket_hot, axis=1)
        width_gate = NB * picked_width
        second_rows = lax.all_gather(second_low, "tensor", axis=0, tiled=True)
        before = jnp.dot(second_rows, up_weight, preferred_element_type=jnp.float32)
        unit_on = (unit_ids[None, :] < FF // NB * (buckets[:, None] + 1)).astype(jnp.float32)
        rectified = jnp.maximum(before, 0.0) * unit_on
        active = (rectified * rectified).astype(jnp.bfloat16)
        branch_part = jnp.dot(active, down_weight, preferred_element_type=jnp.float32)
        branch_own = lax.psum_scatter(branch_part, "tensor", scatter_dimension=0, tiled=True)
        outputs.append(
            (own_live[:, None] * (hidden + width_gate[:, None] * branch_own)).astype(jnp.bfloat16)
        )
        backward_weights = (
            lax.all_gather(mixer, "dp", axis=0, tiled=True),
            lax.all_gather(merger, "dp", axis=1, tiled=True),
            lax.all_gather(expand, "dp", axis=0, tiled=True),
            lax.all_gather(shrink, "dp", axis=1, tiled=True),
        )
        mix_weight, out_weight, up_weight, down_weight = backward_weights
        outer = cotangent[micro_index].astype(jnp.float32) * own_live[:, None]
        width_gate_back = jnp.sum(outer * branch_own, axis=1)
        branch_back = (width_gate[:, None] * outer).astype(jnp.bfloat16)
        branch_rows = lax.all_gather(branch_back, "tensor", axis=0, tiled=True)
        active_back = contract_cols(branch_rows, down_weight)
        down_term = contract_rows(active, branch_rows)
        before_back = (2.0 * rectified * active_back).astype(jnp.bfloat16)
        up_term = contract_rows(second_rows, before_back)
        second_part = contract_cols(before_back, up_weight)
        second_back = lax.psum_scatter(second_part, "tensor", scatter_dimension=0, tiled=True)
        width_logit_back = (
            NB * picked_width[:, None] * (bucket_hot - width_share) * width_gate_back[:, None]
        )
        width_router_sum = width_router_sum + jnp.dot(
            second_value.T, width_logit_back, precision=HIGHEST
        )
        second_back = second_back + jnp.dot(width_logit_back, router_width.T, precision=HIGHEST)
        gain_two_sum = gain_two_sum + jnp.sum(second_back * second_normed, axis=0)
        bias_two_sum = bias_two_sum + jnp.sum(second_back, axis=0)
        hidden_back = outer + norm_back(second_back, second_normed, second_inverse, gain_two)
        gate_back = jnp.sum(hidden_back * attention_own, axis=1)
        attention_back = (own_gate[:, None] * hidden_back).astype(jnp.bfloat16)
        attention_rows_back = lax.all_gather(attention_back, "tensor", axis=0, tiled=True)
        out_term = contract_rows(head_rows, attention_rows_back)
        heads_back = (
            contract_cols(attention_rows_back, out_weight).reshape(total, heads_local, HD)
            * head_on[:, :, None]
        ).astype(jnp.bfloat16)
        query_back, keys_back, values_back = attend_backward(
            query, keys, values, member, log_total, heads_back
        )
        mixed_back = jnp.stack(
            [
                rotate_back(query_back, cosine, sine),
                rotate_back(keys_back, cosine, sine),
                values_back,
            ],
            axis=2,
        )
        mixed_back = mixed_back.reshape(total, 3 * heads_local * HD).astype(jnp.bfloat16)
        mix_term = contract_rows(first_rows, mixed_back)
        first_part = contract_cols(mixed_back, mix_weight)
        seq_gate_part = jnp.sum(own_seq * gate_back[:, None], axis=0)
        seq_gate_back = lax.psum(seq_gate_part, "tensor")
        head_logit_back = (
            NHC * picked_head[:, None] * (choice_hot - head_share) * seq_gate_back[:, None]
        )
        own_spread = jnp.dot(own_seq, head_logit_back / divisor[:, None], precision=HIGHEST)
        first_back = lax.psum_scatter(first_part, "tensor", scatter_dimension=0, tiled=True)
        first_back = first_back + jnp.dot(own_spread, router_head.T, precision=HIGHEST)
        head_router_sum = head_router_sum + jnp.dot(
            first_low.astype(jnp.float32).T, own_spread, precision=HIGHEST
        )
        gain_one_sum = gain_one_sum + jnp.sum(first_back * first_normed, axis=0)
        bias_one_sum = bias_one_sum + jnp.sum(first_back, axis=0)
        input_backs.append(
            hidden_back + norm_back(first_back, first_normed, first_inverse, gain_one)
        )
        width_use = width_use + jnp.sum(bucket_hot * own_live[:, None], axis=0)
        head_use = head_use + jnp.sum(own_seq[:, :, None] * choice_hot[None, :, :], axis=(0, 1))
        shares = (
            lax.psum_scatter(mix_term, "dp", scatter_dimension=0, tiled=True),
            lax.psum_scatter(out_term, "dp", scatter_dimension=1, tiled=True),
            lax.psum_scatter(up_term, "dp", scatter_dimension=0, tiled=True),
            lax.psum_scatter(down_term, "dp", scatter_dimension=1, tiled=True),
        )
        sums = tuple((left + right for left, right in zip(sums, shares)))
    stats = lax.psum(
        (
            gain_one_sum,
            bias_one_sum,
            gain_two_sum,
            bias_two_sum,
            width_router_sum,
            head_router_sum,
            width_use,
            head_use,
        ),
        ("dp", "tensor"),
    )
    return (
        jnp.stack(outputs, axis=0),
        jnp.stack(input_backs, axis=0),
        sums[0],
        sums[1],
        sums[2],
        sums[3],
        stats[0],
        stats[1],
        stats[2],
        stats[3],
        stats[4],
        stats[5],
        stats[6],
        stats[7],
    )


def solution(mesh):
    return jax.shard_map(
        local,
        mesh=mesh,
        in_specs=(
            P(None, ("dp", "tensor"), None),
            P(None, ("dp", "tensor"), None),
            P("dp", "tensor"),
            P("tensor", "dp"),
            P("dp", "tensor"),
            P("tensor", "dp"),
            P(),
            P(),
            P(),
            P(),
            P(),
            P(),
            P(None, "dp"),
            P(None, "dp"),
            P(None, "dp"),
        ),
        out_specs=(
            P(None, ("dp", "tensor"), None),
            P(None, ("dp", "tensor"), None),
            P("dp", "tensor"),
            P("tensor", "dp"),
            P("dp", "tensor"),
            P("tensor", "dp"),
            P(),
            P(),
            P(),
            P(),
            P(),
            P(),
            P(),
            P(),
        ),
        check_vma=False,
    )
```

profile of v0, /device:TPU:0, one launch (start us, length us, event | category | flops | bytes accessed | tf_op | source)
XLA Modules:
  0.0 1701.9 jit_solution(9767891209946445668)
XLA Ops:
  8.7 1.6 fusion.63
  11.8 2.6 fusion.56
  22.7 29.9 %all-gather.25.cloned.1.call-done = bf16[512,2048]{1,0:T(8,128)(2,1)} async-done(((bf16[128,2048]{1,0:T(8,128)(2,1)}), bf16[512,2048]{1,0:T(8,128)(2,1)}) %all-gather.25.cloned.1.call-update) | async-done | bytes 2097168 | tf_op jit(solution)/shard_map/all_gather | solution.py:186
  52.6 66.4 %all-gather.15.cloned.1.call-done = bf16[2048,1536]{1,0:T(8,128)(2,1)} async-done(((bf16[256,1536]{1,0:T(8,128)(2,1)}), bf16[2048,1536]{1,0:T(8,128)(2,1)}) %all-gather.15.cloned.1.call-update) | async-done | bytes 6291472 | tf_op jit(solution)/shard_map/all_gather | solution.py:170
  119.0 6.2 fusion.176
  130.2 19.9 %all-gather.17.cloned.1.call-done = bf16[512,2048]{1,0:T(8,128)(2,1)} async-done(((bf16[512,256]{1,0:T(8,128)(2,1)}), bf16[512,2048]{1,0:T(8,128)(2,1)}) %all-gather.17.cloned.1.call-update) | async-done | bytes 2097168 | tf_op jit(solution)/shard_map/all_gather | solution.py:171
  150.1 4.8 fusion.177
  157.0 29.8 %all-gather.13.cloned.1.call-done = bf16[512,2048]{1,0:T(8,128)(2,1)} async-done(((bf16[128,2048]{1,0:T(8,128)(2,1)}), bf16[512,2048]{1,0:T(8,128)(2,1)}) %all-gather.13.cloned.1.call-update) | async-done | bytes 2097168 | tf_op jit(solution)/shard_map/all_gather | solution.py:186
  186.8 6.2 fusion.173
  198.8 3.2 fusion.174
  205.0 2.2 convolution_divide_fusion.1
  208.1 34.3 %reduce-scatter.17.cloned.1.call-done = f32[128,2048]{1,0:T(8,128)} async-done(((f32[512,2048]{1,0:T(8,128)}), f32[128,2048]{1,0:T(8,128)}) %reduce-scatter.17.cloned.1.call-update) | async-done | bytes 1048592 | tf_op jit(solution)/shard_map/reduce_scatter | solution.py:219
  242.4 55.8 %reduce-scatter.13.cloned.1.call-done = f32[128,2048]{1,0:T(8,128)} async-done(((f32[512,2048]{1,0:T(8,128)}), f32[128,2048]{1,0:T(8,128)}) %reduce-scatter.13.cloned.1.call-update) | async-done | bytes 1048592 | tf_op jit(solution)/shard_map/reduce_scatter | solution.py:219
  298.2 2.0 fusion.155
  304.1 77.8 %all-gather.21.cloned.1.call-done = bf16[2048,2048]{1,0:T(8,128)(2,1)} async-done(((bf16[256,2048]{1,0:T(8,128)(2,1)}), bf16[2048,2048]{1,0:T(8,128)(2,1)}) %all-gather.21.cloned.1.call-update) | async-done | bytes 8388624 | tf_op jit(solution)/shard_map/all_gather | solution.py:172
  381.9 35.7 %all-gather.19.cloned.1.call-done = bf16[512,2048]{1,0:T(8,128)(2,1)} async-done(((bf16[128,2048]{1,0:T(8,128)(2,1)}), bf16[512,2048]{1,0:T(8,128)(2,1)}) %all-gather.19.cloned.1.call-update) | async-done | bytes 2097168 | tf_op jit(solution)/shard_map/all_gather | solution.py:232
  417.6 10.6 fusion.175
  428.2 73.5 %all-gather.23.cloned.1.call-done = bf16[2048,2048]{1,0:T(8,128)(2,1)} async-done(((bf16[2048,256]{1,0:T(8,128)(2,1)}), bf16[2048,2048]{1,0:T(8,128)(2,1)}) %all-gather.23.cloned.1.call-update) | async-done | bytes 8388624 | tf_op jit(solution)/shard_map/all_gather | solution.py:173
  501.7 11.2 fusion.150
  513.0 23.9 %all-gather.27.cloned.1.call-done = bf16[512,2048]{1,0:T(8,128)(2,1)} async-done(((bf16[128,2048]{1,0:T(8,128)(2,1)}), bf16[512,2048]{1,0:T(8,128)(2,1)}) %all-gather.27.cloned.1.call-update) | async-done | bytes 2097168 | tf_op jit(solution)/shard_map/all_gather | solution.py:232
  536.9 7.6 fusion.178
  544.5 2.0 copy-done.11
  546.6 9.7 fusion.151
  559.8 32.9 %reduce-scatter.15.cloned.1.call-done = f32[128,2048]{1,0:T(8,128)} async-done(((f32[512,2048]{1,0:T(8,128)}), f32[128,2048]{1,0:T(8,128)}) %reduce-scatter.15.cloned.1.call-update) | async-done | bytes 1048592 | tf_op jit(solution)/shard_map/reduce_scatter | solution.py:238
  592.6 55.8 %reduce-scatter.19.cloned.1.call-done = f32[128,2048]{1,0:T(8,128)} async-done(((f32[512,2048]{1,0:T(8,128)}), f32[128,2048]{1,0:T(8,128)}) %reduce-scatter.19.cloned.1.call-update) | async-done | bytes 1048592 | tf_op jit(solution)/shard_map/reduce_scatter | solution.py:238
  648.5 3.9 fusion.85
  653.2 34.7 %all-gather.33.cloned.1.call-done = bf16[512,2048]{1,0:T(8,128)(2,1)} async-done(((bf16[128,2048]{1,0:T(8,128)(2,1)}), bf16[512,2048]{1,0:T(8,128)(2,1)}) %all-gather.33.cloned.1.call-update) | async-done | bytes 2097168 | tf_op jit(solution)/shard_map/all_gather | solution.py:252
  687.8 9.8 multiply_convert_fusion.1
  699.0 9.7 fusion.182
  708.8 16.7 all-gather.29.cloned.1.call-done
  725.5 9.8 multiply_convert_fusion.3
  736.6 9.7 fusion.179
  746.6 34.4 %reduce-scatter.25.cloned.1.call-done = f32[128,2048]{1,0:T(8,128)} async-done(((f32[512,2048]{1,0:T(8,128)}), f32[128,2048]{1,0:T(8,128)}) %reduce-scatter.25.cloned.1.call-update) | async-done | bytes 1048592 | tf_op jit(solution)/shard_map/reduce_scatter | solution.py:258
  781.0 1.9 convolution_add_fusion.5
  782.9 53.9 %reduce-scatter.21.cloned.1.call-done = f32[128,2048]{1,0:T(8,128)} async-done(((f32[512,2048]{1,0:T(8,128)}), f32[128,2048]{1,0:T(8,128)}) %reduce-scatter.21.cloned.1.call-update) | async-done | bytes 1048592 | tf_op jit(solution)/shard_map/reduce_scatter | solution.py:258
  836.8 2.8 multiply_reduce_fusion.3
  839.7 3.3 multiply_convert_fusion.9
  845.6 34.8 %all-gather.35.cloned.1.call-done = bf16[512,2048]{1,0:T(8,128)(2,1)} async-done(((bf16[128,2048]{1,0:T(8,128)(2,1)}), bf16[512,2048]{1,0:T(8,128)(2,1)}) %all-gather.35.cloned.1.call-update) | async-done | bytes 2097168 | tf_op jit(solution)/shard_map/all_gather | solution.py:271
  880.4 3.6 fusion.183
  884.1 2.2 multiply_reduce_fusion
  893.2 5.1 fusion.184
  898.7 19.3 %all-gather.31.cloned.1.call-done = bf16[512,2048]{1,0:T(8,128)(2,1)} async-done(((bf16[128,2048]{1,0:T(8,128)(2,1)}), bf16[512,2048]{1,0:T(8,128)(2,1)}) %all-gather.31.cloned.1.call-update) | async-done | bytes 2097168 | tf_op jit(solution)/shard_map/all_gather | solution.py:271
  918.0 3.0 fusion.180
  921.1 2.2 multiply_reduce_fusion.1
  930.4 5.1 fusion.181
  935.6 1.5 copy-done.43
  938.9 3.2 convolution_add_fusion.3
  946.3 14.0 fusion.149
  960.3 9.1 all-reduce.1
  973.9 1.9 convolution_add_fusion.4
  975.8 53.9 %reduce-scatter.23.cloned.1.call-done = f32[128,2048]{1,0:T(8,128)} async-done(((f32[512,2048]{1,0:T(8,128)}), f32[128,2048]{1,0:T(8,128)}) %reduce-scatter.23.cloned.1.call-update) | async-done | bytes 1048592 | tf_op jit(solution)/shard_map/reduce_scatter | solution.py:297
  1029.7 3.5 fusion.62
  1034.5 18.5 %convolution_add_fusion.1 = f32[2048,2048]{1,0:T(8,128)} fusion(f32[2048,2048]{1,0:T(8,128)} %fusion.149, bf16[512,2048]{1,0:T(8,128)(2,1)} %all-gather.33.cloned.1.call-done, f32[512,2048]{1,0:T(8,128)} %copy-done.11, s32[2048]{0:T(1024)S(1)} %iota_add_fusion, s32[512]{0:T(512)S(1)} %bitcast.296), kind=kOutput, calls=%fused_computation.1 | convolution fusion | flops 4304404480 | bytes 39856128 | tf_op jit(solution)/shard_map/dot_general | solution.py:19
  1053.3 7.0 fusion.187
  1060.2 13.2 convolution_add_fusion.2
  1073.8 5.8 fusion.185
  1079.6 6.8 convolution_add_fusion
  1086.4 2.4 pad_maximum_fusion.3
  1088.9 2.3 fusion.61
  1091.2 1.5 pad_maximum_fusion
  1092.8 119.3 %all-reduce.4.cloned.1.call-done = (f32[2048]{0:T(1024)}, f32[2048]{0:T(1024)}, f32[2048]{0:T(1024)}, f32[2048]{0:T(1024)}, f32[2048,4]{0,1:T(4,128)}, /*index=5*/f32[2048,4]{0,1:T(4,128)}, f32[4]{0:T(128)}, f32[4]{0:T(128)}) async-done(((f32[2048]{0:T(1024)}, f32[2048]{0:T(1024)}, f32[2048]{0:T(1024)}, f32[2048]{0:T(1024)}, f32[2048,4]{0,1:T(4,128)}, /*index=5*/f32[2048,4]{0,1:T(4,128)}, f32[4]{0:T(128)}, ...) | async-done | bytes 98352 | tf_op jit(solution)/shard_map/psum | solution.py:316
  1212.1 172.4 %reduce-scatter.35.cloned.1.call-done = f32[2048,256]{1,0:T(8,128)} async-done(((f32[2048,2048]{1,0:T(8,128)}), f32[2048,256]{1,0:T(8,128)}) %reduce-scatter.35.cloned.1.call-update) | async-done | bytes 2097168 | tf_op jit(solution)/shard_map/reduce_scatter | solution.py:313
  1384.5 169.6 %reduce-scatter.33.cloned.1.call-done = f32[256,2048]{1,0:T(8,128)} async-done(((f32[2048,2048]{1,0:T(8,128)}), f32[256,2048]{1,0:T(8,128)}) %reduce-scatter.33.cloned.1.call-update) | async-done | bytes 2097168 | tf_op jit(solution)/shard_map/reduce_scatter | solution.py:312
  1554.1 130.6 %reduce-scatter.29.cloned.1.call-done = f32[256,1536]{1,0:T(8,128)} async-done(((f32[2048,1536]{1,0:T(8,128)}), f32[256,1536]{1,0:T(8,128)}) %reduce-scatter.29.cloned.1.call-update) | async-done | bytes 1572880 | tf_op jit(solution)/shard_map/reduce_scatter | solution.py:310
  (433 shorter events, 77.4 us)
Async XLA Ops:
  7.2 550.7 %copy-start = (bf16[2048,4]{0,1:T(4,128)(2,1)S(1)}, bf16[2048,4]{0,1:T(4,128)(2,1)}, u32[]{:S(2)}) copy-start(bf16[2048,4]{0,1:T(4,128)(2,1)} %param.25) | copy-start | bytes 49156
  7.2 45.4 %all-gather.25.cloned.1.call-start = ((), (), s32[]{:S(2)}) async-start(), calls=%async_computation.20 | async-start | bytes 2621440 | tf_op jit(solution)/shard_map/all_gather | solution.py:186
  14.4 104.6 %all-gather.15.cloned.1.call-start = ((), (), s32[]{:S(2)}) async-start(), calls=%async_computation.13 | async-start | bytes 7077888 | tf_op jit(solution)/shard_map/all_gather | solution.py:170
  15.2 135.0 %all-gather.17.cloned.1.call-start = ((), (), s32[]{:S(2)}) async-start(), calls=%async_computation.14 | async-start | bytes 2359296 | tf_op jit(solution)/shard_map/all_gather | solution.py:171
  15.9 170.9 %all-gather.13.cloned.1.call-start = ((), (), s32[]{:S(2)}) async-start(), calls=%async_computation.12 | async-start | bytes 2621440 | tf_op jit(solution)/shard_map/all_gather | solution.py:186
  16.5 225.9 %reduce-scatter.17.cloned.1.call-start = ((), (), s32[]{:S(2)}) async-start(), calls=%async_computation.21 | async-start | bytes 5242880 | tf_op jit(solution)/shard_map/reduce_scatter | solution.py:219
  20.1 187.3 %copy-start.66 = (s32[4]{0:T(128)}, s32[4]{0:T(128)S(1)}, u32[]{:S(2)}) copy-start(s32[4]{0:T(128)S(1)} %get-tuple-element.143) | copy-start | bytes 52
  20.1 187.4 %copy-start.68 = (s32[4]{0:T(128)}, s32[4]{0:T(128)S(1)}, u32[]{:S(2)}) copy-start(s32[4]{0:T(128)S(1)} %get-tuple-element.140) | copy-start | bytes 52
  130.2 24.8 %copy-start.40 = (bf16[512,4,128]{0,2,1:T(8,128)(2,1)}, bf16[512,4,128]{0,2,1:T(8,128)(2,1)S(1)}, u32[]{:S(2)}) copy-start(bf16[512,4,128]{0,2,1:T(8,128)(2,1)S(1)} %fusion.44) | copy-start | bytes 1572868
  155.0 143.2 %reduce-scatter.13.cloned.1.call-start = ((), (), s32[]{:S(2)}) async-start(), calls=%async_computation.15 | async-start | bytes 5242880 | tf_op jit(solution)/shard_map/reduce_scatter | solution.py:219
  202.0 96.2 %copy-start.6 = (bf16[2,128,2048]{2,1,0:T(8,128)(2,1)S(1)}, bf16[2,128,2048]{2,1,0:T(8,128)(2,1)}, u32[]{:S(2)}) copy-start(bf16[2,128,2048]{2,1,0:T(8,128)(2,1)} %param.15) | copy-start | bytes 3145732
  202.1 179.8 %all-gather.21.cloned.1.call-start = ((), (), s32[]{:S(2)}) async-start(), calls=%async_computation.17 | async-start | bytes 9437184 | tf_op jit(solution)/shard_map/all_gather | solution.py:172
  202.8 214.8 %all-gather.19.cloned.1.call-start = ((), (), s32[]{:S(2)}) async-start(), calls=%async_computation.16 | async-start | bytes 2621440 | tf_op jit(solution)/shard_map/all_gather | solution.py:232
  205.0 95.5 %copy-start.60 = (f32[4,4]{0,1:T(4,128)}, f32[4,4]{0,1:T(4,128)S(1)}, u32[]{:S(2)}) copy-start(f32[4,4]{0,1:T(4,128)S(1)} %get-tuple-element.159) | copy-start | bytes 196
  207.4 94.8 %copy-start.62 = (f32[4,4]{0,1:T(4,128)}, f32[4,4]{0,1:T(4,128)S(1)}, u32[]{:S(2)}) copy-start(f32[4,4]{0,1:T(4,128)S(1)} %get-tuple-element.155) | copy-start | bytes 196
  207.4 90.8 %copy-start.97 = (f32[4]{0:T(128)}, f32[4]{0:T(128)S(1)}, u32[]{:S(2)}) copy-start(f32[4]{0:T(128)S(1)} %fusion.111) | copy-start | bytes 52
  207.5 90.7 %copy-start.107 = (f32[4]{0:T(128)}, f32[4]{0:T(128)S(1)}, u32[]{:S(2)}) copy-start(f32[4]{0:T(128)S(1)} %broadcast_multiply_fusion.10) | copy-start | bytes 52
  207.9 94.3 %copy-start.109 = (f32[4]{0:T(128)}, f32[4]{0:T(128)S(1)}, u32[]{:S(2)}) copy-start(f32[4]{0:T(128)S(1)} %broadcast_multiply_fusion.11) | copy-start | bytes 52
  208.0 94.2 %copy-start.64 = (f32[128]{0:T(128)}, f32[128]{0:T(128)S(1)}, u32[]{:S(2)}) copy-start(f32[128]{0:T(128)S(1)} %get-tuple-element.64) | copy-start | bytes 1540
  208.1 94.1 %copy-start.78 = (f32[128]{0:T(128)}, f32[128]{0:T(128)S(1)}, u32[]{:S(2)}) copy-start(f32[128]{0:T(128)S(1)} %get-tuple-element.59) | copy-start | bytes 1540
  302.3 199.5 %all-gather.23.cloned.1.call-start = ((), (), s32[]{:S(2)}) async-start(), calls=%async_computation.18 | async-start | bytes 9437184 | tf_op jit(solution)/shard_map/all_gather | solution.py:173
  303.0 233.9 %all-gather.27.cloned.1.call-start = ((), (), s32[]{:S(2)}) async-start(), calls=%async_computation.22 | async-start | bytes 2621440 | tf_op jit(solution)/shard_map/all_gather | solution.py:232
  303.6 289.0 %reduce-scatter.15.cloned.1.call-start = ((), (), s32[]{:S(2)}) async-start(), calls=%async_computation.19 | async-start | bytes 5242880 | tf_op jit(solution)/shard_map/reduce_scatter | solution.py:238
  304.1 421.4 %copy-start.89 = (s32[1,512]{1,0:T(1,128)}, s32[1,512]{1,0:T(1,128)S(1)}, u32[]{:S(2)}) copy-start(s32[1,512]{1,0:T(1,128)S(1)} %get-tuple-element.129) | copy-start | bytes 6148
  513.0 135.5 %reduce-scatter.19.cloned.1.call-start = ((), (), s32[]{:S(2)}) async-start(), calls=%async_computation.23 | async-start | bytes 5242880 | tf_op jit(solution)/shard_map/reduce_scatter | solution.py:238
  556.3 131.6 %all-gather.33.cloned.1.call-start = ((), (), s32[]{:S(2)}) async-start(), calls=%async_computation.28 | async-start | bytes 2621440 | tf_op jit(solution)/shard_map/all_gather | solution.py:252
  557.2 95.2 %copy-start.76 = (f32[128]{0:T(128)}, f32[128]{0:T(128)S(1)}, u32[]{:S(2)}) copy-start(f32[128]{0:T(128)S(1)} %dynamic_slice.25) | copy-start | bytes 1540
  557.9 94.5 %copy-start.77 = (f32[128]{0:T(128)}, f32[128]{0:T(128)S(1)}, u32[]{:S(2)}) copy-start(f32[128]{0:T(128)S(1)} %dynamic_slice.22) | copy-start | bytes 1540
  557.9 223.1 %copy-start.74 = (s32[128]{0:T(128)}, s32[128]{0:T(128)S(1)}, u32[]{:S(2)}) copy-start(s32[128]{0:T(128)S(1)} %fusion.140) | copy-start | bytes 1540
  559.8 221.2 %copy-start.70 = (f32[128]{0:T(128)}, f32[128]{0:T(128)S(1)}, u32[]{:S(2)}) copy-start(f32[128]{0:T(128)S(1)} %broadcast_multiply_fusion.8) | copy-start | bytes 1540
  652.3 128.7 %copy-start.72 = (f32[128]{0:T(128)}, f32[128]{0:T(128)S(1)}, u32[]{:S(2)}) copy-start(f32[128]{0:T(128)S(1)} %get-tuple-element.33) | copy-start | bytes 1540
  652.4 73.1 %all-gather.29.cloned.1.call-start = ((), (), s32[]{:S(2)}) async-start(), calls=%async_computation.24 | async-start | bytes 2621440 | tf_op jit(solution)/shard_map/all_gather | solution.py:252
  653.0 128.0 %reduce-scatter.25.cloned.1.call-start = ((), (), s32[]{:S(2)}) async-start(), calls=%async_computation.29 | async-start | bytes 5242880 | tf_op jit(solution)/shard_map/reduce_scatter | solution.py:258
  708.8 128.1 %reduce-scatter.21.cloned.1.call-start = ((), (), s32[]{:S(2)}) async-start(), calls=%async_computation.25 | async-start | bytes 5242880 | tf_op jit(solution)/shard_map/reduce_scatter | solution.py:258
  746.3 134.1 %all-gather.35.cloned.1.call-start = ((), (), s32[]{:S(2)}) async-start(), calls=%async_computation.30 | async-start | bytes 2621440 | tf_op jit(solution)/shard_map/all_gather | solution.py:271
  844.9 73.1 %all-gather.31.cloned.1.call-start = ((), (), s32[]{:S(2)}) async-start(), calls=%async_computation.26 | async-start | bytes 2621440 | tf_op jit(solution)/shard_map/all_gather | solution.py:271
  845.5 128.4 %reduce-scatter.27.cloned.1.call-start = ((), (), s32[]{:S(2)}) async-start(), calls=%async_computation.31 | async-start | bytes 5242880 | tf_op jit(solution)/shard_map/reduce_scatter | solution.py:297
  898.3 131.4 %reduce-scatter.23.cloned.1.call-start = ((), (), s32[]{:S(2)}) async-start(), calls=%async_computation.27 | async-start | bytes 5242880 | tf_op jit(solution)/shard_map/reduce_scatter | solution.py:297
  935.5 157.2 %reduce-scatter.31.cloned.1.call-start = ((), (), s32[]{:S(2)}) async-start(), calls=%async_computation.33 | async-start | bytes 4718592 | tf_op jit(solution)/shard_map/reduce_scatter | solution.py:311
  942.3 269.9 %all-reduce.4.cloned.1.call-start = ((), (), s32[]{:S(2)}) async-start(), calls=%async_computation.36 | async-start | bytes 198656 | tf_op jit(solution)/shard_map/psum | solution.py:316
  946.1 24.5 %copy-start.63 = (f32[4,4]{0,1:T(4,128)S(1)}, f32[4,4]{0,1:T(4,128)}, u32[]{:S(2)}) copy-start(f32[4,4]{0,1:T(4,128)} %copy-done.62) | copy-start | bytes 196
  946.1 24.5 %copy-start.96 = (f32[4]{0:T(128)S(1)}, f32[4]{0:T(128)}, u32[]{:S(2)}) copy-start(f32[4]{0:T(128)} %copy-done.95) | copy-start | bytes 52
  946.1 24.5 %copy-start.98 = (f32[4]{0:T(128)S(1)}, f32[4]{0:T(128)}, u32[]{:S(2)}) copy-start(f32[4]{0:T(128)} %copy-done.97) | copy-start | bytes 52
  946.1 24.5 %copy-start.104 = (f32[4]{0:T(128)S(1)}, f32[4]{0:T(128)}, u32[]{:S(2)}) copy-start(f32[4]{0:T(128)} %copy-done.103) | copy-start | bytes 52
  946.1 24.4 %copy-start.110 = (f32[4]{0:T(128)S(1)}, f32[4]{0:T(128)}, u32[]{:S(2)}) copy-start(f32[4]{0:T(128)} %copy-done.109) | copy-start | bytes 52
  946.1 25.2 %copy-start.61 = (f32[4,4]{0,1:T(4,128)S(1)}, f32[4,4]{0,1:T(4,128)}, u32[]{:S(2)}) copy-start(f32[4,4]{0,1:T(4,128)} %copy-done.60) | copy-start | bytes 196
  946.2 25.2 %copy-start.92 = (f32[4]{0:T(128)S(1)}, f32[4]{0:T(128)}, u32[]{:S(2)}) copy-start(f32[4]{0:T(128)} %copy-done.91) | copy-start | bytes 52
  946.2 25.2 %copy-start.94 = (f32[4]{0:T(128)S(1)}, f32[4]{0:T(128)}, u32[]{:S(2)}) copy-start(f32[4]{0:T(128)} %copy-done.93) | copy-start | bytes 52
  946.2 25.2 %copy-start.102 = (f32[4]{0:T(128)S(1)}, f32[4]{0:T(128)}, u32[]{:S(2)}) copy-start(f32[4]{0:T(128)} %copy-done.101) | copy-start | bytes 52
  946.2 25.2 %copy-start.108 = (f32[4]{0:T(128)S(1)}, f32[4]{0:T(128)}, u32[]{:S(2)}) copy-start(f32[4]{0:T(128)} %copy-done.107) | copy-start | bytes 52
  946.2 26.0 %copy-start.27 = (bf16[128,2048]{1,0:T(8,128)(2,1)S(1)}, bf16[128,2048]{1,0:T(8,128)(2,1)}, u32[]{:S(2)}) copy-start(bf16[128,2048]{1,0:T(8,128)(2,1)} %get-tuple-element.70) | copy-start | bytes 1572868
  946.2 26.3 %copy-start.26 = (bf16[128,2048]{1,0:T(8,128)(2,1)S(1)}, bf16[128,2048]{1,0:T(8,128)(2,1)}, u32[]{:S(2)}) copy-start(bf16[128,2048]{1,0:T(8,128)(2,1)} %get-tuple-element.71) | copy-start | bytes 1572868
  946.2 27.7 %copy-start.55 = (bf16[2048,4]{0,1:T(4,128)(2,1)S(1)}, bf16[2048,4]{0,1:T(4,128)(2,1)}, u32[]{:S(2)}) copy-start(bf16[2048,4]{0,1:T(4,128)(2,1)} %param.26) | copy-start | bytes 49156
  946.2 83.4 %copy-start.7 = (bf16[2,128,2048]{2,1,0:T(8,128)(2,1)S(1)}, bf16[2,128,2048]{2,1,0:T(8,128)(2,1)}, u32[]{:S(2)}) copy-start(bf16[2,128,2048]{2,1,0:T(8,128)(2,1)} %param.15) | copy-start | bytes 3145732
  946.2 83.4 %copy-start.53 = (f32[2048]{0:T(1024)S(1)}, f32[2048]{0:T(1024)}, u32[]{:S(2)}) copy-start(f32[2048]{0:T(1024)} %copy-done.52) | copy-start | bytes 24580
  946.3 83.4 %copy-start.57 = (f32[128]{0:T(128)S(1)}, f32[128]{0:T(128)}, u32[]{:S(2)}) copy-start(f32[128]{0:T(128)} %copy-done.56) | copy-start | bytes 1540
  946.3 83.4 %copy-start.59 = (f32[128]{0:T(128)S(1)}, f32[128]{0:T(128)}, u32[]{:S(2)}) copy-start(f32[128]{0:T(128)} %copy-done.58) | copy-start | bytes 1540
  946.3 83.4 %copy-start.86 = (f32[128]{0:T(128)S(1)}, f32[128]{0:T(128)}, u32[]{:S(2)}) copy-start(f32[128]{0:T(128)} %copy-done.85) | copy-start | bytes 1540
  946.3 83.4 %copy-start.88 = (f32[128]{0:T(128)S(1)}, f32[128]{0:T(128)}, u32[]{:S(2)}) copy-start(f32[128]{0:T(128)} %copy-done.87) | copy-start | bytes 1540
  975.8 77.2 %copy-start.37 = (f32[128,2048]{1,0:T(8,128)}, f32[128,2048]{1,0:T(8,128)S(1)}, u32[]{:S(2)}) copy-start(f32[128,2048]{1,0:T(8,128)S(1)} %convolution_add_fusion.4) | copy-start | bytes 3145732
  1034.5 350.1 %reduce-scatter.35.cloned.1.call-start = ((), (), s32[]{:S(2)}) async-start(), calls=%async_computation.35 | async-start | bytes 18874368 | tf_op jit(solution)/shard_map/reduce_scatter | solution.py:313
  1053.0 501.1 %reduce-scatter.33.cloned.1.call-start = ((), (), s32[]{:S(2)}) async-start(), calls=%async_computation.34 | async-start | bytes 18874368 | tf_op jit(solution)/shard_map/reduce_scatter | solution.py:312
  1073.4 611.2 %reduce-scatter.29.cloned.1.call-start = ((), (), s32[]{:S(2)}) async-start(), calls=%async_computation.32 | async-start | bytes 14155776 | tf_op jit(solution)/shard_map/reduce_scatter | solution.py:310
  1088.9 606.0 %copy-start.1 = (bf16[2048,4]{0,1:T(4,128)(2,1)S(1)}, bf16[2048,4]{0,1:T(4,128)(2,1)}, u32[]{:S(2)}) copy-start(bf16[2048,4]{0,1:T(4,128)(2,1)} %param.25) | copy-start | bytes 49156
  (77 other events, 246.0 us)
Sparse Core Ops, SparseCore 0:
  14.5 38.0 all-gather.24
  54.2 64.7 all-gather.14
  120.6 29.4 all-gather.16
  152.4 34.3 all-gather.12
  189.6 52.6 reduce-scatter.16
  245.4 52.6 reduce-scatter.12
  299.8 82.0 all-gather.20
  383.7 33.8 all-gather.18
  419.2 82.4 all-gather.22
  503.4 33.4 all-gather.26
  539.9 52.6 reduce-scatter.14
  595.7 52.6 reduce-scatter.18
  652.5 35.2 all-gather.32
  690.1 35.2 all-gather.28
  728.3 52.6 reduce-scatter.24
  784.1 52.6 reduce-scatter.20
  845.0 35.2 all-gather.34
  882.7 35.2 all-gather.30
  921.0 52.8 reduce-scatter.26
  977.0 52.6 reduce-scatter.22
  1032.6 50.0 reduce-scatter.30
  1090.2 121.8 all-reduce.3
  1215.2 169.3 reduce-scatter.34
  1387.4 166.6 reduce-scatter.32
  1557.1 127.5 reduce-scatter.28
where the time goes:
time: 1710 us; the launch traced here: 1700 us
  waiting for transfers between devices  1380 us (81%)
  matrix products  215 us (13%)
  other arithmetic  47.9 us (3%)
  local copies, waits for them, and re-layouts  29.4 us (2%)
    reduce_scatter x1, waiting for transfers between devices, local(): lax.psum_scatter(down_term, 'dp', scatter_dimension=1, tiled=True)  172 us
    reduce_scatter x1, waiting for transfers between devices, local(): lax.psum_scatter(up_term, 'dp', scatter_dimension=0, tiled=True)  170 us
    reduce_scatter x1, waiting for transfers between devices, local(): lax.psum_scatter(mix_term, 'dp', scatter_dimension=0, tiled=True)  131 us
    psum x1, waiting for transfers between devices, local(): lax.psum((gain_one_sum, bias_one_sum, gain_two_sum, bias_two_sum, width_r...  119 us
    reduce_scatter x2, waiting for transfers between devices, local(): lax.psum_scatter(attention_part, 'tensor', scatter_dimension=0, tiled=True)  90.1 us
    reduce_scatter x2, waiting for transfers between devices, local(): lax.psum_scatter(branch_part, 'tensor', scatter_dimension=0, tiled=True)  88.7 us
    reduce_scatter x2, waiting for transfers between devices, local(): lax.psum_scatter(second_part, 'tensor', scatter_dimension=0, tiled=True)  88.4 us
    all_gather x1, waiting for transfers between devices, local(): lax.all_gather(expand, 'dp', axis=0, tiled=True)  77.8 us
  transfers between devices with their start and end apart: 25, of which 24 were waited for; matrix products, arithmetic and copies ran while one was open for 15% of the time, Pallas kernels for 0%

commit v1 on v0

v1 whole, which is shorter than its diff:
```python
import jax
import jax.numpy as jnp
from jax import lax
from jax.sharding import PartitionSpec as P

H = 16
HD = 128
FF = 8192
NB = 4
NHC = 4


EPSILON = 1e-05
HIGHEST = lax.Precision.HIGHEST
MASKED = -1e30
BF16 = jnp.bfloat16
F32 = jnp.float32


def contract_rows(left, right):
    return lax.dot_general(left, right, (((0,), (0,)), ((), ())), preferred_element_type=F32)


def contract_cols(left, right):
    return lax.dot_general(left, right, (((1,), (1,)), ((), ())), preferred_element_type=F32)


def swap_low(value, size):
    return lax.ppermute(value, "tensor", [(i, i ^ 1) for i in range(size)])


def from_high(value, size, step):
    high = size // 2
    pairs = [(((h + step) % high) * 2 + l, h * 2 + l) for h in range(high) for l in range(2)]
    return lax.ppermute(value, "tensor", pairs)


def to_high(value, size, step):
    high = size // 2
    pairs = [(h * 2 + l, ((h + step) % high) * 2 + l) for h in range(high) for l in range(2)]
    return lax.ppermute(value, "tensor", pairs)


def arrival_parts(rank, size):
    high = size // 2
    hi, lo = rank // 2, rank % 2
    first = [((hi + s) % high) * 2 + (lo + l) % 2 for s in range(high) for l in range(2)]
    second = [((hi + s) % high) * 2 + (lo + l) % 2 for l in range(2) for s in range(high)]
    return first, second


def gather_rows(own, size):
    half = own.shape[0] // 2
    high = size // 2
    first, second = own[:half], own[half:]
    first = jnp.concatenate([first, swap_low(first, size)], axis=0)
    second = jnp.concatenate(
        [second] + [from_high(second, size, s) for s in range(1, high)], axis=0
    )
    blocks = [first] + [from_high(first, size, s) for s in range(1, high)]
    blocks += [second, swap_low(second, size)]
    return jnp.concatenate(blocks, axis=0)


def scatter_rows(part, size):
    half = part.shape[0] // (2 * size)
    high = size // 2
    first, second = part[: half * size], part[half * size :]
    first_sum = first[: 2 * half].astype(F32)
    for s in range(1, high):
        sent = to_high(first[2 * half * s : 2 * half * (s + 1)], size, s)
        first_sum = first_sum + sent.astype(F32)
    second_sum = second[: high * half].astype(F32)
    second_sum = second_sum + swap_low(second[high * half :], size).astype(F32)
    first_own = first_sum[:half] + swap_low(first_sum[half:].astype(BF16), size).astype(F32)
    second_own = second_sum[:half]
    for s in range(1, high):
        sent = to_high(second_sum[half * s : half * (s + 1)].astype(BF16), size, s)
        second_own = second_own + sent.astype(F32)
    return jnp.concatenate([first_own, second_own], axis=0)


def butterfly(value, axis, size):
    step = 1
    while step < size:
        value = value + lax.ppermute(value, axis, [(i, i ^ step) for i in range(size)])
        step *= 2
    return value


def normalize(value):
    centred = value - jnp.mean(value, axis=-1, keepdims=True)
    inverse = lax.rsqrt(jnp.mean(centred * centred, axis=-1, keepdims=True) + EPSILON)
    return (centred * inverse, inverse)


def norm_back(back, normed, inverse, gain):
    scaled = back * gain
    inner = jnp.mean(scaled, axis=-1, keepdims=True)
    along = jnp.mean(scaled * normed, axis=-1, keepdims=True)
    return inverse * (scaled - inner - normed * along)


def rotary_tables(place, width):
    half = width // 2
    rates = jnp.power(10000.0, -2.0 * jnp.arange(half, dtype=F32) / width)
    angles = place.astype(F32)[:, None] * rates[None, :]
    cosine = jnp.cos(angles)
    sine = jnp.sin(angles)
    return (jnp.concatenate([cosine, cosine], axis=1), jnp.concatenate([sine, sine], axis=1))


def rotate(value, cosine, sine):
    half = value.shape[-1] // 2
    turned = jnp.concatenate([-value[..., half:], value[..., :half]], axis=-1)
    return value * cosine + turned * sine


def rotate_back(grad_value, cosine, sine):
    moved = grad_value * sine
    half = moved.shape[-1] // 2
    return grad_value * cosine + jnp.concatenate([moved[..., half:], -moved[..., :half]], axis=-1)


def softmax_rows(logits):
    powers = jnp.exp(logits - jnp.max(logits, axis=-1, keepdims=True))
    return powers / jnp.sum(powers, axis=-1, keepdims=True)


def place_rows(lengths, slots):
    slot_count = lengths.shape[0]
    ends = jnp.cumsum(lengths, dtype=jnp.int32)
    starts = ends - lengths
    filled = ends[-1]
    member = jnp.sum((ends[None, :] <= slots[:, None]).astype(jnp.int32), axis=1, dtype=jnp.int32)
    begins = jnp.concatenate([starts, filled[None]])
    onehot = member[:, None] == jnp.arange(slot_count + 1, dtype=jnp.int32)[None, :]
    place = slots - jnp.sum(jnp.where(onehot, begins[None, :], 0), axis=1, dtype=jnp.int32)
    return (member, place, slots < filled, onehot[:, :slot_count])


def block_scores(query, keys, member, slots):
    scale = query.shape[-1] ** (-0.5)
    seen = (member[:, None] == member[None, :]) & (slots[:, None] >= slots[None, :])
    scores = jnp.einsum("qhd,khd->hqk", query, keys, preferred_element_type=F32) * scale
    return jnp.where(seen[None], scores, MASKED)


def attend_forward(query, keys, values, member, slots):
    scores = block_scores(query, keys, member, slots)
    peak = jnp.max(scores, axis=-1, keepdims=True)
    powers = jnp.exp(scores - peak)
    mass = jnp.sum(powers, axis=-1, keepdims=True)
    share = (powers / mass).astype(BF16)
    pieces = jnp.einsum("hqk,khd->qhd", share, values, preferred_element_type=F32)
    return (pieces, peak + jnp.log(mass))


def attend_backward(query, keys, values, member, slots, log_total, heads_back):
    scale = query.shape[-1] ** (-0.5)
    scores = block_scores(query, keys, member, slots)
    share = jnp.exp(scores - log_total)
    share_back = jnp.einsum("qhd,khd->hqk", heads_back, values, preferred_element_type=F32)
    inner = jnp.sum(share * share_back, axis=-1, keepdims=True)
    score_back = (share * (share_back - inner)).astype(BF16)
    query_back = jnp.einsum("hqk,khd->qhd", score_back, keys, preferred_element_type=F32) * scale
    keys_back = jnp.einsum("hqk,qhd->khd", score_back, query, preferred_element_type=F32) * scale
    values_back = jnp.einsum(
        "hqk,qhd->khd", share.astype(BF16), heads_back, preferred_element_type=F32
    )
    return (query_back, keys_back, values_back)


def after(value, *others):
    return lax.optimization_barrier((value,) + others)[0]


def gather_weights(piece):
    return lax.all_gather(piece, "dp", axis=0, tiled=False)


def local(
    dp_size,
    size,
    tokens,
    cotangent,
    mixer,
    merger,
    expand,
    shrink,
    attend_gain,
    attend_bias,
    feed_gain,
    feed_bias,
    width_router,
    head_router,
    lengths,
    head_choice,
    width_bucket,
):
    rank = lax.axis_index("tensor")
    micro, rows, width = tokens.shape
    total = width_bucket.shape[1]
    half = rows // 2
    heads_local = merger.shape[0] // HD
    units_local = expand.shape[1]
    head_ids = rank * heads_local + jnp.arange(heads_local, dtype=jnp.int32)
    unit_ids = rank * units_local + jnp.arange(units_local, dtype=jnp.int32)
    gain_one = attend_gain.astype(F32)
    bias_one = attend_bias.astype(F32)
    gain_two = feed_gain.astype(F32)
    bias_two = feed_bias.astype(F32)
    router_width = width_router.astype(F32)
    router_head = head_router.astype(F32)

    mix_weight = gather_weights(mixer)
    out_weight = gather_weights(after(merger, mix_weight))
    up_weight = gather_weights(after(expand, out_weight))
    down_weight = gather_weights(after(shrink, up_weight))
    mix_weight = mix_weight.reshape(width, -1)
    up_weight = up_weight.reshape(width, -1)

    first_ranks, second_ranks = arrival_parts(rank, size)
    row_starts = [r * rows for r in first_ranks] + [r * rows + half for r in second_ranks]
    slots = jnp.concatenate([start + jnp.arange(half, dtype=jnp.int32) for start in row_starts])
    own_slots = rank * rows + jnp.arange(rows, dtype=jnp.int32)

    state = []
    for m in range(micro):
        s = {}
        state.append(s)
        s["member"], s["place"], _, s["seqmask"] = place_rows(lengths[m], slots)
        _, _, own_live, own_seq = place_rows(lengths[m], own_slots)
        s["own_live"] = own_live.astype(F32)
        s["own_seq"] = own_seq.astype(F32)
        s["buckets"] = jnp.concatenate(
            [lax.dynamic_slice_in_dim(width_bucket[m], start, half, 0) for start in row_starts]
        )
        own_buckets = lax.dynamic_slice_in_dim(width_bucket[m], rank * rows, rows, 0)
        s["bucket_hot"] = (
            own_buckets[:, None] == jnp.arange(NB, dtype=jnp.int32)[None, :]
        ).astype(F32)
        choices = head_choice[m]
        s["choice_hot"] = (
            choices[:, None] == jnp.arange(NHC, dtype=jnp.int32)[None, :]
        ).astype(F32)
        s["cosine"], s["sine"] = [t[:, None, :] for t in rotary_tables(s["place"], HD)]
        heads_used = jnp.sum(
            jnp.where(s["seqmask"], H // NHC * (choices[None, :] + 1), 0), axis=1, dtype=jnp.int32
        )
        s["head_on"] = (head_ids[None, :] < heads_used[:, None]).astype(BF16)
        s["unit_on"] = (unit_ids[None, :] < FF // NB * (s["buckets"][:, None] + 1)).astype(F32)
        s["inputs"] = tokens[m].astype(F32)
        s["outer"] = cotangent[m].astype(F32) * s["own_live"][:, None]
        s["first_normed"], s["first_inverse"] = normalize(s["inputs"])
        s["first_low"] = (s["first_normed"] * gain_one + bias_one).astype(BF16)

    for s in state:
        s["first_rows"] = gather_rows(s["first_low"], size)

    for s in state:
        seq_float = s["seqmask"].astype(F32)
        s["divisor"] = jnp.maximum(jnp.sum(seq_float, axis=0), 1.0)
        sums = jnp.dot(seq_float.T.astype(BF16), s["first_rows"], preferred_element_type=F32)
        means = sums / s["divisor"][:, None]
        s["head_share"] = softmax_rows(jnp.dot(means, router_head, precision=HIGHEST))
        s["picked_head"] = jnp.sum(s["head_share"] * s["choice_hot"], axis=1)
        s["own_gate"] = jnp.sum(s["own_seq"] * (NHC * s["picked_head"])[None, :], axis=1)

    for s in state:
        mixed = jnp.dot(s["first_rows"], mix_weight, preferred_element_type=F32).reshape(
            total, heads_local, 3, HD
        )
        s["query"] = rotate(mixed[:, :, 0], s["cosine"], s["sine"]).astype(BF16)
        s["keys"] = rotate(mixed[:, :, 1], s["cosine"], s["sine"]).astype(BF16)
        s["values"] = mixed[:, :, 2].astype(BF16)
        attended, s["log_total"] = attend_forward(
            s["query"], s["keys"], s["values"], s["member"], slots
        )
        s["head_rows"] = (attended.astype(BF16) * s["head_on"][:, :, None]).reshape(
            total, heads_local * HD
        )
        part = lax.dot_general(
            s["head_rows"], out_weight, (((1,), (1,)), ((), ())), preferred_element_type=F32
        )
        s["attention_own"] = scatter_rows(part.astype(BF16).reshape(total, width), size)

    for s in state:
        hidden = s["inputs"] + s["own_gate"][:, None] * s["attention_own"]
        s["hidden"] = hidden
        s["second_normed"], s["second_inverse"] = normalize(hidden)
        s["second_low"] = (s["second_normed"] * gain_two + bias_two).astype(BF16)
        s["width_share"] = softmax_rows(
            jnp.dot(s["second_low"], width_router, preferred_element_type=F32)
        )
        s["picked_width"] = jnp.sum(s["width_share"] * s["bucket_hot"], axis=1)
        s["width_gate"] = NB * s["picked_width"]
        s["second_rows"] = gather_rows(s["second_low"], size)
    for s in state:
        branch_back = (s["width_gate"][:, None] * s["outer"]).astype(BF16)
        s["branch_rows"] = gather_rows(branch_back, size)

    for s in state:
        before = jnp.dot(s["second_rows"], up_weight, preferred_element_type=F32)
        s["rectified"] = jnp.maximum(before, 0.0) * s["unit_on"]
        s["active"] = (s["rectified"] * s["rectified"]).astype(BF16)

    def over_micro(left, right):
        return sum(contract_rows(s[left], s[right]) for s in state).astype(BF16)

    def columns_first(term):
        return jnp.swapaxes(term.reshape(term.shape[0], dp_size, -1), 0, 1)

    def share_out(term):
        return lax.psum_scatter(term, "dp", scatter_dimension=0, tiled=False).astype(F32)

    down_sum = share_out(columns_first(over_micro("active", "branch_rows")))

    outputs = []
    for s in state:
        part = lax.dot_general(
            s["active"], down_weight, (((1,), (1,)), ((), ())), preferred_element_type=F32
        )
        branch_own = scatter_rows(part.astype(BF16).reshape(total, width), size)
        outputs.append(
            (
                s["own_live"][:, None] * (s["hidden"] + s["width_gate"][:, None] * branch_own)
            ).astype(BF16)
        )
        s["width_gate_back"] = jnp.sum(s["outer"] * branch_own, axis=1)
    for s in state:
        branch_rows = s["branch_rows"].reshape(total, dp_size, -1)
        active_back = lax.dot_general(
            branch_rows, down_weight, (((1, 2), (0, 2)), ((), ())), preferred_element_type=F32
        )
        s["before_back"] = (2.0 * s["rectified"] * active_back).astype(BF16)
    up_sum = share_out(
        after(over_micro("second_rows", "before_back"), down_sum).reshape(dp_size, -1, units_local)
    )

    gain_two_sum = 0.0
    bias_two_sum = 0.0
    width_router_sum = 0.0
    for s in state:
        second_part = contract_cols(s["before_back"], up_weight)
        second_back = scatter_rows(second_part.astype(BF16), size)
        width_logit_back = (
            NB
            * s["picked_width"][:, None]
            * (s["bucket_hot"] - s["width_share"])
            * s["width_gate_back"][:, None]
        )
        width_router_sum = width_router_sum + jnp.dot(
            width_logit_back.T, s["second_low"].astype(F32), precision=HIGHEST
        )
        second_back = second_back + jnp.dot(width_logit_back, router_width.T, precision=HIGHEST)
        gain_two_sum = gain_two_sum + jnp.sum(second_back * s["second_normed"], axis=0)
        bias_two_sum = bias_two_sum + jnp.sum(second_back, axis=0)
        s["hidden_back"] = s["outer"] + norm_back(
            second_back, s["second_normed"], s["second_inverse"], gain_two
        )
        gate_back = jnp.sum(s["hidden_back"] * s["attention_own"], axis=1)
        seq_gate_part = jnp.sum(s["own_seq"] * gate_back[:, None], axis=0)
        s["seq_gate_back"] = butterfly(seq_gate_part, "tensor", size)
        attention_back = (s["own_gate"][:, None] * s["hidden_back"]).astype(BF16)
        s["attention_rows_back"] = gather_rows(attention_back, size)

    out_sum = share_out(after(columns_first(over_micro("head_rows", "attention_rows_back")), up_sum))

    for s in state:
        rows_back = s["attention_rows_back"].reshape(total, dp_size, -1)
        heads_back = lax.dot_general(
            rows_back, out_weight, (((1, 2), (0, 2)), ((), ())), preferred_element_type=F32
        )
        heads_back = (
            heads_back.reshape(total, heads_local, HD) * s["head_on"][:, :, None]
        ).astype(BF16)
        query_back, keys_back, values_back = attend_backward(
            s["query"], s["keys"], s["values"], s["member"], slots, s["log_total"], heads_back
        )
        mixed_back = jnp.stack(
            [
                rotate_back(query_back, s["cosine"], s["sine"]),
                rotate_back(keys_back, s["cosine"], s["sine"]),
                values_back,
            ],
            axis=2,
        )
        s["mixed_back"] = mixed_back.reshape(total, 3 * heads_local * HD).astype(BF16)

    mix_sum = share_out(
        after(over_micro("first_rows", "mixed_back"), out_sum).reshape(dp_size, -1, mixer.shape[1])
    )

    input_backs = []
    gain_one_sum = 0.0
    bias_one_sum = 0.0
    head_router_sum = 0.0
    width_use = 0.0
    head_use = 0.0
    for s in state:
        first_part = contract_cols(s["mixed_back"], mix_weight)
        first_back = scatter_rows(first_part.astype(BF16), size)
        head_logit_back = (
            NHC
            * s["picked_head"][:, None]
            * (s["choice_hot"] - s["head_share"])
            * s["seq_gate_back"][:, None]
        )
        own_spread = jnp.dot(
            s["own_seq"], head_logit_back / s["divisor"][:, None], precision=HIGHEST
        )
        first_back = first_back + jnp.dot(own_spread, router_head.T, precision=HIGHEST)
        head_router_sum = head_router_sum + jnp.dot(
            own_spread.T, s["first_low"].astype(F32), precision=HIGHEST
        )
        gain_one_sum = gain_one_sum + jnp.sum(first_back * s["first_normed"], axis=0)
        bias_one_sum = bias_one_sum + jnp.sum(first_back, axis=0)
        input_backs.append(
            s["hidden_back"] + norm_back(first_back, s["first_normed"], s["first_inverse"], gain_one)
        )
        width_use = width_use + jnp.sum(s["bucket_hot"] * s["own_live"][:, None], axis=0)
        head_use = head_use + jnp.sum(
            s["own_seq"][:, :, None] * s["choice_hot"][None, :, :], axis=(0, 1)
        )

    use_row = jnp.zeros((1, width), F32)
    use_row = use_row.at[0, :NB].set(width_use).at[0, NB : NB + NHC].set(head_use)
    stats = jnp.concatenate(
        [
            gain_one_sum[None],
            bias_one_sum[None],
            gain_two_sum[None],
            bias_two_sum[None],
            width_router_sum,
            head_router_sum,
            use_row,
        ],
        axis=0,
    )
    stats = butterfly(butterfly(stats, "tensor", size), "dp", dp_size)
    return (
        jnp.stack(outputs, axis=0),
        jnp.stack(input_backs, axis=0),
        mix_sum,
        out_sum,
        up_sum,
        down_sum,
        stats[0],
        stats[1],
        stats[2],
        stats[3],
        stats[4 : 4 + NB].T,
        stats[4 + NB : 4 + NB + NHC].T,
        stats[4 + NB + NHC, :NB],
        stats[4 + NB + NHC, NB : NB + NHC],
    )


def solution(mesh):
    def run(*args):
        return local(mesh.shape["dp"], mesh.shape["tensor"], *args)

    rows = P(None, ("dp", "tensor"), None)
    tall, wide = P("dp", "tensor"), P("tensor", "dp")
    weights = (tall, wide, tall, wide)
    return jax.shard_map(
        run,
        mesh=mesh,
        in_specs=(rows, rows) + weights + (P(),) * 6 + (P(None, "dp"),) * 3,
        out_specs=(rows, rows) + weights + (P(),) * 8,
        check_vma=False,
    )
```

time: 1710 us -> 744 us (0.44)
  waiting for transfers between devices: 1380 us -> 279 us
  starting transfers between devices: 3.06 us -> 79.1 us
  local copies, waits for them, and re-layouts: 29.4 us -> 85.8 us
  other arithmetic: 47.9 us -> 86.2 us
  matrix products: 215 us -> 188 us
    reduce_scatter x12 -> x4, waiting for transfers between devices: 794 us -> 43.4 us  [share_out(): lax.psum_scatter(term, 'dp', scatter_dimension=0, tiled=False).astype(F32)]
    all_gather x12 -> x4, waiting for transfers between devices: 462 us -> 76.8 us  [gather_weights(): return lax.all_gather(piece, 'dp', axis=0, tiled=False)]
    ppermute x0 -> x73, waiting for transfers between devices: none -> 157 us  [the longest x16 55.5 us: from_high(): return lax.ppermute(value, 'tensor', pairs)]
    psum x1 -> x0, waiting for transfers between devices: 119 us -> none  [local(): lax.psum((gain_one_sum, bias_one_sum, gain_two_sum, bias_two_sum, width_r...]
    ppermute x0 -> x73, starting transfers between devices: none -> 78.8 us  [the longest x32 36.7 us: swap_low(): return lax.ppermute(value, 'tensor', [(i, i ^ 1) for i in range(size)])]
    dot_general x8 -> x4, matrix products: 55.9 us -> 29.7 us  [contract_cols(): lax.dot_general(left, right, (((1,), (1,)), ((), ())), preferred_element_...]
    convert_element_type x18 -> x32, other arithmetic: 15.4 us -> 36.8 us  [the longest x4 9.73 us: share_out(): lax.psum_scatter(term, 'dp', scatter_dimension=0, tiled=False).astype(F32)]
    slice x2 -> x44, local copies, waits for them, and re-layouts: 1.17 us -> 21.8 us  [the longest x12 11.8 us: scatter_rows(): sent = to_high(first[2 * half * s:2 * half * (s + 1)], size, s)]
  transfers between devices with their start and end apart: 25 -> 81, of which waited for: 24 -> 49; matrix products, arithmetic and copies ran while one was open for 15% -> 39% of each run, Pallas kernels for 0% -> 0%
where the time goes in v1:
time: 744 us; the launch traced here: 736 us
  waiting for transfers between devices  279 us (38%)
  matrix products  188 us (25%)
  other arithmetic  86.2 us (12%)
  local copies, waits for them, and re-layouts  85.8 us (12%)
  starting transfers between devices  79.1 us (11%)
  between operations  18 us (2%)
    all_gather x4, waiting for transfers between devices, gather_weights(): return lax.all_gather(piece, 'dp', axis=0, tiled=False)  76.8 us
    dot_general x8, matrix products, contract_rows(): lax.dot_general(left, right, (((0,), (0,)), ((), ())), preferred_element_...  63.1 us
    ppermute x16, waiting for transfers between devices, from_high(): return lax.ppermute(value, 'tensor', pairs)  55.5 us
    reduce_scatter x4, waiting for transfers between devices, share_out(): lax.psum_scatter(term, 'dp', scatter_dimension=0, tiled=False).astype(F32)  43.4 us
    ppermute x16, waiting for transfers between devices, to_high(): return lax.ppermute(value, 'tensor', pairs)  42 us
    ppermute x32, waiting for transfers between devices, swap_low(): return lax.ppermute(value, 'tensor', [(i, i ^ 1) for i in range(size)])  37.2 us
    ppermute x32, starting transfers between devices, swap_low(): return lax.ppermute(value, 'tensor', [(i, i ^ 1) for i in range(size)])  36.7 us
    dot_general x4, matrix products, contract_cols(): lax.dot_general(left, right, (((1,), (1,)), ((), ())), preferred_element_...  29.7 us
  transfers between devices with their start and end apart: 81, of which 49 were waited for; matrix products, arithmetic and copies ran while one was open for 39% of the time, Pallas kernels for 0%

profile of v1, /device:TPU:0, one launch (start us, length us, event | category | flops | bytes accessed | tf_op | source)
XLA Modules:
  0.0 735.9 jit_solution(3818951437038204964)
XLA Ops:
  8.8 32.7 %all-gather.11.cloned.1.call-done = bf16[4096,256]{1,0:T(8,128)(2,1)} async-done(((bf16[512,256]{1,0:T(8,128)(2,1)}), bf16[4096,256]{1,0:T(8,128)(2,1)}) %all-gather.11.cloned.1.call-update) | async-done | bytes 2097168 | tf_op jit(solution)/shard_map/all_gather | solution.py:179
  81.3 5.6 collective-permute-done.1
  87.0 9.2 %collective-permute-done.17 = bf16[128,2048]{1,0:T(8,128)(2,1)S(1)} collective-permute-done((bf16[128,2048]{1,0:T(8,128)(2,1)S(1)}, bf16[128,2048]{1,0:T(8,128)(2,1)S(1)}, u32[]{:S(2)}, u32[]{:S(2)}) %collective-permute-start.17) | collective-permute-done | bytes 524320 | tf_op jit(solution)/shard_map/ppermute | solution.py:35
  100.9 6.5 all-gather.9.cloned.1.call-done
  107.4 8.9 %copy.189 = bf16[1536,2048]{1,0:T(8,128)(2,1)} copy(bf16[1536,2048]{0,1:T(8,128)(2,1)} %bitcast.497) | data formatting | bytes 12582912 | tf_op jit(solution)/shard_map/dot_general | solution.py:271
  116.4 6.5 fusion.18
  122.9 3.5 fusion.20
  144.6 2.8 fusion.97
  150.4 2.7 fusion.69
  160.1 2.1 bitcast_convert_fusion.9
  178.8 2.1 collective-permute-done.21
  180.9 2.2 collective-permute-done.7
  194.8 2.2 collective-permute-start.9
  197.1 2.4 collective-permute-start.11
  199.5 3.8 collective-permute-done.24
  205.1 7.9 %collective-permute-done.9 = bf16[128,2048]{1,0:T(8,128)(2,1)S(1)} collective-permute-done((bf16[128,2048]{1,0:T(8,128)(2,1)S(1)}, bf16[128,2048]{1,0:T(8,128)(2,1)S(1)}, u32[]{:S(2)}, u32[]{:S(2)}) %collective-permute-start.9) | collective-permute-done | bytes 524320 | tf_op jit(solution)/shard_map/ppermute | solution.py:35
  213.0 9.3 %collective-permute-done.25 = bf16[128,2048]{1,0:T(8,128)(2,1)S(1)} collective-permute-done((bf16[128,2048]{1,0:T(8,128)(2,1)S(1)}, bf16[128,2048]{1,0:T(8,128)(2,1)S(1)}, u32[]{:S(2)}, u32[]{:S(2)}) %collective-permute-start.25) | collective-permute-done | bytes 524320 | tf_op jit(solution)/shard_map/ppermute | solution.py:35
  224.0 10.4 %fusion.222 = f32[512,2048]{1,0:T(8,128)} fusion(bf16[512,2048]{1,0:T(8,128)(2,1)S(1)} %constant_dynamic-update-slice_fusion.18, bf16[2048,2048]{1,0:T(8,128)(2,1)} %all-gather.13.cloned.1.call-done), kind=kOutput, calls=%fused_computation.568 | convolution fusion | flops 4294967296 | bytes 14680064 | tf_op jit(solution)/shard_map/dot_general | solution.py:304
  234.4 37.5 %all-gather.15.cloned.1.call-done = bf16[16384,256]{1,0:T(8,128)(2,1)} async-done(((bf16[2048,256]{1,0:T(8,128)(2,1)}), bf16[16384,256]{1,0:T(8,128)(2,1)}) %all-gather.15.cloned.1.call-update) | async-done | bytes 8388624 | tf_op jit(solution)/shard_map/all_gather | solution.py:179
  271.8 9.5 %fusion.33 = bf16[512,8,256]{0,2,1:T(8,128)(2,1)S(1)} fusion(bf16[8,2048,256]{2,1,0:T(8,128)(2,1)} %bitcast.538, f32[512,2048]{1,0:T(8,128)} %fusion.222, s32[2048]{0:T(1024)S(1)} %copy-done.103, s32[512]{0:T(512)S(1)} %copy-done.141), kind=kOutput, calls=%fused_computation.65 | convolution fusion | flops 4301258752 | bytes 14690304 | tf_op jit(solution)/shard_map/dot_general | solution.py:321
  287.1 9.5 %fusion.221 = f32[512,2048]{1,0:T(8,128)} fusion(bf16[512,2048]{1,0:T(8,128)(2,1)S(1)} %copy-done.85, bf16[2048,2048]{1,0:T(8,128)(2,1)} %all-gather.13.cloned.1.call-done), kind=kOutput, calls=%fused_computation.567 | convolution fusion | flops 4294967296 | bytes 14680064 | tf_op jit(solution)/shard_map/dot_general | solution.py:304
  296.7 7.5 %fusion.30 = bf16[512,8,256]{0,2,1:T(8,128)(2,1)S(1)} fusion(bf16[8,2048,256]{2,1,0:T(8,128)(2,1)S(1)} %bitcast.542, f32[512,2048]{1,0:T(8,128)} %fusion.221, s32[2048]{0:T(1024)S(1)} %copy-done.103, s32[512]{0:T(512)S(1)} %copy-done.140), kind=kOutput, calls=%fused_computation.64 | convolution fusion | flops 4301258752 | bytes 14690304 | tf_op jit(solution)/shard_map/dot_general | solution.py:321
  328.3 2.7 collective-permute-done.31
  331.2 3.8 collective-permute-done.15
  341.0 6.5 collective-permute-done.32
  349.8 3.3 collective-permute-done.50
  356.1 15.8 %collective-permute-done.51 = bf16[128,2048]{1,0:T(8,128)(2,1)S(1)} collective-permute-done((bf16[128,2048]{1,0:T(8,128)(2,1)S(1)}, bf16[128,2048]{1,0:T(8,128)(2,1)S(1)}, u32[]{:S(2)}, u32[]{:S(2)}) %collective-permute-start.51) | collective-permute-done | bytes 524320 | tf_op jit(solution)/shard_map/ppermute | solution.py:35
  373.5 8.9 %fusion.184 = f32[2048,2048]{0,1:T(8,128)} fusion(bf16[512,2048]{1,0:T(8,128)(2,1)S(1)} %constant_dynamic-update-slice_fusion.36, f32[512,2048]{1,0:T(8,128)S(1)} %copy-done.166, s32[2048]{0:T(1024)S(1)} %copy-done.103, s32[512]{0:T(512)S(1)} %copy-done.141), kind=kOutput, calls=%fused_computation.536 | convolution fusion | flops 4300210176 | bytes 23078912 | tf_op jit(solution)/shard_map/dot_general | solution.py:21
  385.6 15.7 %add_convert_fusion = bf16[2048,2048]{0,1:T(8,128)(2,1)} fusion(f32[2048,2048]{0,1:T(8,128)} %fusion.184, bf16[512,2048]{1,0:T(8,128)(2,1)} %constant_dynamic-update-slice_fusion.24, f32[512,2048]{1,0:T(8,128)} %fusion.221, s32[2048]{0:T(1024)S(1)} %copy-done.103, s32[512]{0:T(512)S(1)} %copy-done.140), kind=kOutput, calls=%fused_computation | convolution fusion | flops 4308598784 | bytes 31467520 | tf_op jit(solution)/shard_map/dot_general | solution.py:21
  401.3 11.3 %copy.240 = bf16[2048,8,256]{2,0,1:T(8,128)(2,1)} copy(bf16[2048,8,256]{0,2,1:T(8,128)(2,1)} %bitcast.495) | data formatting | bytes 16777216 | tf_op jit(solution)/shard_map/reshape | solution.py:312
  414.3 10.7 %fusion.1 = bf16[512,2048]{1,0:T(8,128)(2,1)S(1)} fusion(f32[512,2048]{1,0:T(8,128)} %fusion.221, bf16[8,2048,256]{2,1,0:T(8,128)(2,1)} %bitcast.539, bf16[64,8,8,256]{3,2,1,0:T(8,128)(2,1)} %bitcast.168, s32[2048]{0:T(1024)S(1)} %copy-done.103, s32[512]{0:T(512)S(1)} %copy-done.140), kind=kOutput, calls=%fused_computation.6 | convolution fusion | flops 4301258752 | bytes 16787456 | tf_op jit(solution)/shard_map/dot_general | solution.py:333
  425.0 10.5 %convolution_convert_fusion.3 = bf16[512,2048]{1,0:T(8,128)(2,1)} fusion(bf16[512,2048]{1,0:T(8,128)(2,1)S(1)} %fusion.1, bf16[2048,2048]{1,0:T(8,128)(2,1)} %all-gather.13.cloned.1.call-done), kind=kOutput, calls=%fused_computation.33 | convolution fusion | flops 4296015872 | bytes 12582912 | tf_op jit(solution)/shard_map/dot_general | solution.py:25
  435.6 7.6 %fusion = bf16[512,2048]{1,0:T(8,128)(2,1)} fusion(f32[512,2048]{1,0:T(8,128)} %fusion.222, bf16[8,2048,256]{2,1,0:T(8,128)(2,1)S(1)} %bitcast.545, bf16[64,8,8,256]{3,2,1,0:T(8,128)(2,1)S(1)} %bitcast.525, s32[2048]{0:T(1024)S(1)} %copy-done.103, s32[512]{0:T(512)S(1)} %copy-done.141), kind=kOutput, calls=%fused_computation.4 | convolution fusion | flops 4301258752 | bytes 16787456 | tf_op jit(solution)/shard_map/dot_general | solution.py:333
  443.2 10.1 %fusion.226 = f32[2048,2048]{1,0:T(8,128)} fusion(bf16[512,2048]{1,0:T(8,128)(2,1)S(1)} %copy-done.88, bf16[512,2048]{1,0:T(8,128)(2,1)} %fusion), kind=kOutput, calls=%fused_computation.572 | convolution fusion | flops 4294967296 | bytes 20971520 | tf_op jit(solution)/shard_map/dot_general | solution.py:21
  453.2 10.4 %add_convert_fusion.1 = bf16[2048,2048]{1,0:T(8,128)(2,1)} fusion(f32[2048,2048]{1,0:T(8,128)} %fusion.226, bf16[512,2048]{1,0:T(8,128)(2,1)S(1)} %copy-done.86, bf16[512,2048]{1,0:T(8,128)(2,1)S(1)} %copy-done.169), kind=kOutput, calls=%fused_computation.1 | convolution fusion | flops 4303355904 | bytes 29360128 | tf_op jit(solution)/shard_map/dot_general | solution.py:21
  463.7 35.7 %reduce-scatter.5.cloned.1.call-done = bf16[1,2048,256]{2,1,0:T(8,128)(2,1)} async-done(((bf16[8,2048,256]{2,1,0:T(8,128)(2,1)}), bf16[1,2048,256]{2,1,0:T(8,128)(2,1)}) %reduce-scatter.5.cloned.1.call-update) | async-done | bytes 1048592 | tf_op jit(solution)/shard_map/reduce_scatter | solution.py:315
  499.4 2.7 bitcast_convert_fusion.1
  506.6 8.6 %convolution_convert_fusion.1 = bf16[512,2048]{1,0:T(8,128)(2,1)S(1)} fusion(bf16[512,2048]{1,0:T(8,128)(2,1)S(1)} %copy-done.167, bf16[2048,2048]{1,0:T(8,128)(2,1)} %all-gather.13.cloned.1.call-done), kind=kOutput, calls=%fused_computation.31 | convolution fusion | flops 4296015872 | bytes 12582912 | tf_op jit(solution)/shard_map/dot_general | solution.py:25
  520.8 9.5 %collective-permute-done.54 = bf16[128,2048]{1,0:T(8,128)(2,1)S(1)} collective-permute-done((bf16[128,2048]{1,0:T(8,128)(2,1)S(1)}, bf16[128,2048]{1,0:T(8,128)(2,1)S(1)}, u32[]{:S(2)}, u32[]{:S(2)}) %collective-permute-start.54) | collective-permute-done | bytes 524320 | tf_op jit(solution)/shard_map/ppermute | solution.py:41
  534.9 3.3 collective-permute-done.57
  547.8 6.2 collective-permute-done.40
  556.3 3.3 collective-permute-done.58
  562.0 7.6 %collective-permute-done.41 = bf16[128,2048]{1,0:T(8,128)(2,1)S(1)} collective-permute-done((bf16[128,2048]{1,0:T(8,128)(2,1)S(1)}, bf16[128,2048]{1,0:T(8,128)(2,1)S(1)}, u32[]{:S(2)}, u32[]{:S(2)}) %collective-permute-start.41) | collective-permute-done | bytes 524320 | tf_op jit(solution)/shard_map/ppermute | solution.py:35
  573.1 2.2 multiply_reduce_fusion.1
  589.1 4.1 multiply_reduce_fusion
  593.2 2.8 bitcast_convert_fusion
  596.1 4.7 multiply_convert_fusion
  608.9 6.6 fusion.224
  615.5 8.5 %add_convert_fusion.2 = bf16[2048,1536]{1,0:T(8,128)(2,1)} fusion(f32[2048,1536]{1,0:T(8,128)} %fusion.224, bf16[512,2048]{1,0:T(8,128)(2,1)S(1)} %copy-done.51, bf16[512,1536]{0,1:T(8,128)(2,1)S(1)} %bitcast.517), kind=kOutput, calls=%fused_computation.2 | convolution fusion | flops 3227516928 | bytes 22544384 | tf_op jit(solution)/shard_map/dot_general | solution.py:21
  624.0 7.6 %reduce-scatter.9.cloned.1.call-done = bf16[1,512,256]{2,1,0:T(8,128)(2,1)} async-done(((bf16[8,512,256]{2,1,0:T(8,128)(2,1)}), bf16[1,512,256]{2,1,0:T(8,128)(2,1)}) %reduce-scatter.9.cloned.1.call-update) | async-done | bytes 262160 | tf_op jit(solution)/shard_map/reduce_scatter | solution.py:315
  637.5 3.3 fusion.90
  653.3 6.7 convolution_convert_fusion.2
  662.4 3.9 convolution_convert_fusion
  668.5 6.6 collective-permute-done.44
  678.6 7.3 collective-permute-done.62
  689.8 4.0 collective-permute-done.65
  693.8 2.1 collective-permute-done.63
  696.0 2.7 fusion.77
  700.1 3.8 collective-permute-done.68
  705.2 3.7 collective-permute-done.69
  710.4 2.3 fusion.76
  712.8 3.2 collective-permute-done.71
  717.6 6.9 collective-permute-done.72
  726.4 2.5 bitcast_convert_fusion.2
  (815 shorter events, 243.3 us)
Async XLA Ops:
  7.2 34.3 %all-gather.11.cloned.1.call-start = ((), (), s32[]{:S(2)}) async-start(), calls=%async_computation.9 | async-start | bytes 2359296 | tf_op jit(solution)/shard_map/all_gather | solution.py:179
  8.0 99.5 %all-gather.9.cloned.1.call-start = ((), (), s32[]{:S(2)}) async-start(), calls=%async_computation.8 | async-start | bytes 7077888 | tf_op jit(solution)/shard_map/all_gather | solution.py:179
  8.7 215.3 %all-gather.13.cloned.1.call-start = ((), (), s32[]{:S(2)}) async-start(), calls=%async_computation.10 | async-start | bytes 9437184 | tf_op jit(solution)/shard_map/all_gather | solution.py:179
  41.5 230.3 %all-gather.15.cloned.1.call-start = ((), (), s32[]{:S(2)}) async-start(), calls=%async_computation.11 | async-start | bytes 9437184 | tf_op jit(solution)/shard_map/all_gather | solution.py:179
  43.7 29.9 %collective-permute-start.2 = (bf16[64,2048]{1,0:T(8,128)(2,1)S(1)}, bf16[64,2048]{1,0:T(8,128)(2,1)}, u32[]{:S(2)}, u32[]{:S(2)}) collective-permute-start(bf16[64,2048]{1,0:T(8,128)(2,1)S(1)} %get-tuple-element.177), channel_id=1, source_target_pairs={{2,0},{3,1},{0,2},{1,3},{6,4},{7,5},{4,6},{5,7},{10,8},{11,9},{8,1... | collective-permute-start | bytes 786440 | tf_op jit(solution)/shard_map/ppermute | solution.py:35
  45.2 25.7 %collective-permute-start = (bf16[64,2048]{1,0:T(8,128)(2,1)S(1)}, bf16[64,2048]{1,0:T(8,128)(2,1)}, u32[]{:S(2)}, u32[]{:S(2)}) collective-permute-start(bf16[64,2048]{1,0:T(8,128)(2,1)S(1)} %get-tuple-element.179), channel_id=1, source_target_pairs={{0,1},{1,0},{2,3},{3,2},{4,5},{5,4},{6,7},{7,6},{8,9},{9,8},{10,11... | collective-permute-start | bytes 786440 | tf_op jit(solution)/shard_map/ppermute | solution.py:29
  47.4 30.3 %collective-permute-start.18 = (bf16[64,2048]{1,0:T(8,128)(2,1)S(1)}, bf16[64,2048]{1,0:T(8,128)(2,1)}, u32[]{:S(2)}, u32[]{:S(2)}) collective-permute-start(bf16[64,2048]{1,0:T(8,128)(2,1)S(1)} %get-tuple-element.183), channel_id=1, source_target_pairs={{2,0},{3,1},{0,2},{1,3},{6,4},{7,5},{4,6},{5,7},{10,8},{11,9},{8,1... | collective-permute-start | bytes 786440 | tf_op jit(solution)/shard_map/ppermute | solution.py:35
  48.0 28.1 %collective-permute-start.16 = (bf16[64,2048]{1,0:T(8,128)(2,1)S(1)}, bf16[64,2048]{1,0:T(8,128)(2,1)}, u32[]{:S(2)}, u32[]{:S(2)}) collective-permute-start(bf16[64,2048]{1,0:T(8,128)(2,1)S(1)} %get-tuple-element.185), channel_id=1, source_target_pairs={{0,1},{1,0},{2,3},{3,2},{4,5},{5,4},{6,7},{7,6},{8,9},{9,8},{10,11... | collective-permute-start | bytes 786440 | tf_op jit(solution)/shard_map/ppermute | solution.py:29
  48.6 450.9 %reduce-scatter.5.cloned.1.call-start = ((), (), s32[]{:S(2)}) async-start(), calls=%async_computation.4 | async-start | bytes 9437184 | tf_op jit(solution)/shard_map/reduce_scatter | solution.py:315
  72.0 14.9 %collective-permute-start.1 = (bf16[128,2048]{1,0:T(8,128)(2,1)S(1)}, bf16[128,2048]{1,0:T(8,128)(2,1)S(1)}, u32[]{:S(2)}, u32[]{:S(2)}) collective-permute-start(bf16[128,2048]{1,0:T(8,128)(2,1)S(1)} %pad_maximum_fusion.4), channel_id=1, source_target_pairs={{2,0},{3,1},{0,2},{1,3},{6,4},{7,5},{4,6},{5,7},{10,8},{11,9},{8,1... | collective-permute-start | bytes 1572872 | tf_op jit(solution)/shard_map/ppermute | solution.py:35
  74.6 22.8 %collective-permute-start.3 = (bf16[128,2048]{1,0:T(8,128)(2,1)S(1)}, bf16[128,2048]{1,0:T(8,128)(2,1)S(1)}, u32[]{:S(2)}, u32[]{:S(2)}) collective-permute-start(bf16[128,2048]{1,0:T(8,128)(2,1)S(1)} %pad_maximum_fusion.5), channel_id=1, source_target_pairs={{0,1},{1,0},{2,3},{3,2},{4,5},{5,4},{6,7},{7,6},{8,9},{9,8},{10,11... | collective-permute-start | bytes 1572872 | tf_op jit(solution)/shard_map/ppermute | solution.py:29
  77.1 19.1 %collective-permute-start.17 = (bf16[128,2048]{1,0:T(8,128)(2,1)S(1)}, bf16[128,2048]{1,0:T(8,128)(2,1)S(1)}, u32[]{:S(2)}, u32[]{:S(2)}) collective-permute-start(bf16[128,2048]{1,0:T(8,128)(2,1)S(1)} %pad_maximum_fusion.8), channel_id=1, source_target_pairs={{2,0},{3,1},{0,2},{1,3},{6,4},{7,5},{4,6},{5,7},{10,8},{11,9},{8,1... | collective-permute-start | bytes 1572872 | tf_op jit(solution)/shard_map/ppermute | solution.py:35
  78.8 20.4 %collective-permute-start.19 = (bf16[128,2048]{1,0:T(8,128)(2,1)S(1)}, bf16[128,2048]{1,0:T(8,128)(2,1)S(1)}, u32[]{:S(2)}, u32[]{:S(2)}) collective-permute-start(bf16[128,2048]{1,0:T(8,128)(2,1)S(1)} %pad_maximum_fusion.9), channel_id=1, source_target_pairs={{0,1},{1,0},{2,3},{3,2},{4,5},{5,4},{6,7},{7,6},{8,9},{9,8},{10,11... | collective-permute-start | bytes 1572872 | tf_op jit(solution)/shard_map/ppermute | solution.py:29
  141.5 26.3 %collective-permute-start.22 = (bf16[128,2048]{1,0:T(8,128)(2,1)}, bf16[128,2048]{1,0:T(8,128)(2,1)}, u32[]{:S(2)}, u32[]{:S(2)}) collective-permute-start(bf16[128,2048]{1,0:T(8,128)(2,1)} %copy.282), channel_id=1, source_target_pairs={{0,1},{1,0},{2,3},{3,2},{4,5},{5,4},{6,7},{7,6},{8,9},{9,8},{10,11... | collective-permute-start | bytes 1572872 | tf_op jit(solution)/shard_map/ppermute | solution.py:29
  143.0 28.1 %collective-permute-start.20 = (bf16[128,2048]{1,0:T(8,128)(2,1)}, bf16[128,2048]{1,0:T(8,128)(2,1)}, u32[]{:S(2)}, u32[]{:S(2)}) collective-permute-start(bf16[128,2048]{1,0:T(8,128)(2,1)} %copy.280), channel_id=1, source_target_pairs={{0,2},{1,3},{2,0},{3,1},{4,6},{5,7},{6,4},{7,5},{8,10},{9,11},{10,... | collective-permute-start | bytes 1572872 | tf_op jit(solution)/shard_map/ppermute | solution.py:41
  158.0 15.8 %collective-permute-start.6 = (bf16[128,2048]{1,0:T(8,128)(2,1)}, bf16[128,2048]{1,0:T(8,128)(2,1)}, u32[]{:S(2)}, u32[]{:S(2)}) collective-permute-start(bf16[128,2048]{1,0:T(8,128)(2,1)} %copy.273), channel_id=1, source_target_pairs={{0,1},{1,0},{2,3},{3,2},{4,5},{5,4},{6,7},{7,6},{8,9},{9,8},{10,11... | collective-permute-start | bytes 1572872 | tf_op jit(solution)/shard_map/ppermute | solution.py:29
  158.5 17.1 %collective-permute-start.4 = (bf16[128,2048]{1,0:T(8,128)(2,1)}, bf16[128,2048]{1,0:T(8,128)(2,1)}, u32[]{:S(2)}, u32[]{:S(2)}) collective-permute-start(bf16[128,2048]{1,0:T(8,128)(2,1)} %copy.271), channel_id=1, source_target_pairs={{0,2},{1,3},{2,0},{3,1},{4,6},{5,7},{6,4},{7,5},{8,10},{9,11},{10,... | collective-permute-start | bytes 1572872 | tf_op jit(solution)/shard_map/ppermute | solution.py:41
  169.4 9.3 %collective-permute-start.23 = (bf16[64,2048]{1,0:T(8,128)(2,1)S(1)}, bf16[64,2048]{1,0:T(8,128)(2,1)S(1)}, u32[]{:S(2)}, u32[]{:S(2)}) collective-permute-start(bf16[64,2048]{1,0:T(8,128)(2,1)S(1)} %slice.947), channel_id=1, source_target_pairs={{0,2},{1,3},{2,0},{3,1},{4,6},{5,7},{6,4},{7,5},{8,10},{9,11},{10,... | collective-permute-start | bytes 786440 | tf_op jit(solution)/shard_map/ppermute | solution.py:41
  172.3 8.6 %collective-permute-start.21 = (bf16[64,2048]{1,0:T(8,128)(2,1)S(1)}, bf16[64,2048]{1,0:T(8,128)(2,1)S(1)}, u32[]{:S(2)}, u32[]{:S(2)}) collective-permute-start(bf16[64,2048]{1,0:T(8,128)(2,1)S(1)} %slice.948), channel_id=1, source_target_pairs={{0,1},{1,0},{2,3},{3,2},{4,5},{5,4},{6,7},{7,6},{8,9},{9,8},{10,11... | collective-permute-start | bytes 786440 | tf_op jit(solution)/shard_map/ppermute | solution.py:29
  187.3 9.7 %collective-permute-start.10 = (bf16[64,2048]{1,0:T(8,128)(2,1)S(1)}, bf16[64,2048]{1,0:T(8,128)(2,1)S(1)}, u32[]{:S(2)}, u32[]{:S(2)}) collective-permute-start(bf16[64,2048]{1,0:T(8,128)(2,1)S(1)} %get-tuple-element.174), channel_id=1, source_target_pairs={{2,0},{3,1},{0,2},{1,3},{6,4},{7,5},{4,6},{5,7},{10,8},{11,9},{8,1... | collective-permute-start | bytes 786440 | tf_op jit(solution)/shard_map/ppermute | solution.py:35
  192.5 11.4 %collective-permute-start.26 = (bf16[64,2048]{1,0:T(8,128)(2,1)S(1)}, bf16[64,2048]{1,0:T(8,128)(2,1)S(1)}, u32[]{:S(2)}, u32[]{:S(2)}) collective-permute-start(bf16[64,2048]{1,0:T(8,128)(2,1)S(1)} %get-tuple-element.180), channel_id=1, source_target_pairs={{2,0},{3,1},{0,2},{1,3},{6,4},{7,5},{4,6},{5,7},{10,8},{11,9},{8,1... | collective-permute-start | bytes 786440 | tf_op jit(solution)/shard_map/ppermute | solution.py:35
  194.1 9.2 %collective-permute-start.24 = (bf16[64,2048]{1,0:T(8,128)(2,1)S(1)}, bf16[64,2048]{1,0:T(8,128)(2,1)S(1)}, u32[]{:S(2)}, u32[]{:S(2)}) collective-permute-start(bf16[64,2048]{1,0:T(8,128)(2,1)S(1)} %get-tuple-element.182), channel_id=1, source_target_pairs={{0,1},{1,0},{2,3},{3,2},{4,5},{5,4},{6,7},{7,6},{8,9},{9,8},{10,11... | collective-permute-start | bytes 786440 | tf_op jit(solution)/shard_map/ppermute | solution.py:29
  194.8 18.2 %collective-permute-start.9 = (bf16[128,2048]{1,0:T(8,128)(2,1)S(1)}, bf16[128,2048]{1,0:T(8,128)(2,1)S(1)}, u32[]{:S(2)}, u32[]{:S(2)}) collective-permute-start(bf16[128,2048]{1,0:T(8,128)(2,1)S(1)} %pad_maximum_fusion.6), channel_id=1, source_target_pairs={{2,0},{3,1},{0,2},{1,3},{6,4},{7,5},{4,6},{5,7},{10,8},{11,9},{8,1... | collective-permute-start | bytes 1572872 | tf_op jit(solution)/shard_map/ppermute | solution.py:35
  197.1 25.4 %collective-permute-start.11 = (bf16[128,2048]{1,0:T(8,128)(2,1)S(1)}, bf16[128,2048]{1,0:T(8,128)(2,1)S(1)}, u32[]{:S(2)}, u32[]{:S(2)}) collective-permute-start(bf16[128,2048]{1,0:T(8,128)(2,1)S(1)} %pad_maximum_fusion.7), channel_id=1, source_target_pairs={{0,1},{1,0},{2,3},{3,2},{4,5},{5,4},{6,7},{7,6},{8,9},{9,8},{10,11... | collective-permute-start | bytes 1572872 | tf_op jit(solution)/shard_map/ppermute | solution.py:29
  203.4 19.0 %collective-permute-start.25 = (bf16[128,2048]{1,0:T(8,128)(2,1)S(1)}, bf16[128,2048]{1,0:T(8,128)(2,1)S(1)}, u32[]{:S(2)}, u32[]{:S(2)}) collective-permute-start(bf16[128,2048]{1,0:T(8,128)(2,1)S(1)} %pad_maximum_fusion.10), channel_id=1, source_target_pairs={{2,0},{3,1},{0,2},{1,3},{6,4},{7,5},{4,6},{5,7},{10,8},{11,9},{8,1... | collective-permute-start | bytes 1572872 | tf_op jit(solution)/shard_map/ppermute | solution.py:35
  203.9 18.6 %collective-permute-start.27 = (bf16[128,2048]{1,0:T(8,128)(2,1)S(1)}, bf16[128,2048]{1,0:T(8,128)(2,1)S(1)}, u32[]{:S(2)}, u32[]{:S(2)}) collective-permute-start(bf16[128,2048]{1,0:T(8,128)(2,1)S(1)} %pad_maximum_fusion.11), channel_id=1, source_target_pairs={{0,1},{1,0},{2,3},{3,2},{4,5},{5,4},{6,7},{7,6},{8,9},{9,8},{10,11... | collective-permute-start | bytes 1572872 | tf_op jit(solution)/shard_map/ppermute | solution.py:29
  283.9 33.8 %collective-permute-start.30 = (bf16[128,2048]{1,0:T(8,128)(2,1)}, bf16[128,2048]{1,0:T(8,128)(2,1)}, u32[]{:S(2)}, u32[]{:S(2)}) collective-permute-start(bf16[128,2048]{1,0:T(8,128)(2,1)} %copy.286), channel_id=1, source_target_pairs={{0,1},{1,0},{2,3},{3,2},{4,5},{5,4},{6,7},{7,6},{8,9},{9,8},{10,11... | collective-permute-start | bytes 1572872 | tf_op jit(solution)/shard_map/ppermute | solution.py:29
  285.4 35.1 %collective-permute-start.28 = (bf16[128,2048]{1,0:T(8,128)(2,1)}, bf16[128,2048]{1,0:T(8,128)(2,1)}, u32[]{:S(2)}, u32[]{:S(2)}) collective-permute-start(bf16[128,2048]{1,0:T(8,128)(2,1)} %copy.284), channel_id=1, source_target_pairs={{0,2},{1,3},{2,0},{3,1},{4,6},{5,7},{6,4},{7,5},{8,10},{9,11},{10,... | collective-permute-start | bytes 1572872 | tf_op jit(solution)/shard_map/ppermute | solution.py:41
  309.8 14.0 %collective-permute-start.14 = (bf16[128,2048]{1,0:T(8,128)(2,1)}, bf16[128,2048]{1,0:T(8,128)(2,1)}, u32[]{:S(2)}, u32[]{:S(2)}) collective-permute-start(bf16[128,2048]{1,0:T(8,128)(2,1)} %copy.277), channel_id=1, source_target_pairs={{0,1},{1,0},{2,3},{3,2},{4,5},{5,4},{6,7},{7,6},{8,9},{9,8},{10,11... | collective-permute-start | bytes 1572872 | tf_op jit(solution)/shard_map/ppermute | solution.py:29
  310.3 15.2 %collective-permute-start.12 = (bf16[128,2048]{1,0:T(8,128)(2,1)}, bf16[128,2048]{1,0:T(8,128)(2,1)}, u32[]{:S(2)}, u32[]{:S(2)}) collective-permute-start(bf16[128,2048]{1,0:T(8,128)(2,1)} %copy.275), channel_id=1, source_target_pairs={{0,2},{1,3},{2,0},{3,1},{4,6},{5,7},{6,4},{7,5},{8,10},{9,11},{10,... | collective-permute-start | bytes 1572872 | tf_op jit(solution)/shard_map/ppermute | solution.py:41
  319.2 11.8 %collective-permute-start.31 = (bf16[64,2048]{1,0:T(8,128)(2,1)S(1)}, bf16[64,2048]{1,0:T(8,128)(2,1)S(1)}, u32[]{:S(2)}, u32[]{:S(2)}) collective-permute-start(bf16[64,2048]{1,0:T(8,128)(2,1)S(1)} %slice.945), channel_id=1, source_target_pairs={{0,2},{1,3},{2,0},{3,1},{4,6},{5,7},{6,4},{7,5},{8,10},{9,11},{10,... | collective-permute-start | bytes 786440 | tf_op jit(solution)/shard_map/ppermute | solution.py:41
  321.7 9.4 %collective-permute-start.29 = (bf16[64,2048]{1,0:T(8,128)(2,1)S(1)}, bf16[64,2048]{1,0:T(8,128)(2,1)S(1)}, u32[]{:S(2)}, u32[]{:S(2)}) collective-permute-start(bf16[64,2048]{1,0:T(8,128)(2,1)S(1)} %slice.946), channel_id=1, source_target_pairs={{0,1},{1,0},{2,3},{3,2},{4,5},{5,4},{6,7},{7,6},{8,9},{9,8},{10,11... | collective-permute-start | bytes 786440 | tf_op jit(solution)/shard_map/ppermute | solution.py:29
  325.0 10.0 %collective-permute-start.15 = (bf16[64,2048]{1,0:T(8,128)(2,1)S(1)}, bf16[64,2048]{1,0:T(8,128)(2,1)S(1)}, u32[]{:S(2)}, u32[]{:S(2)}) collective-permute-start(bf16[64,2048]{1,0:T(8,128)(2,1)S(1)} %slice.949), channel_id=1, source_target_pairs={{0,2},{1,3},{2,0},{3,1},{4,6},{5,7},{6,4},{7,5},{8,10},{9,11},{10,... | collective-permute-start | bytes 786440 | tf_op jit(solution)/shard_map/ppermute | solution.py:41
  336.8 11.4 %collective-permute-start.34 = (bf16[64,2048]{1,0:T(8,128)(2,1)S(1)}, bf16[64,2048]{1,0:T(8,128)(2,1)S(1)}, u32[]{:S(2)}, u32[]{:S(2)}) collective-permute-start(bf16[64,2048]{1,0:T(8,128)(2,1)S(1)} %get-tuple-element.168), channel_id=1, source_target_pairs={{2,0},{3,1},{0,2},{1,3},{6,4},{7,5},{4,6},{5,7},{10,8},{11,9},{8,1... | collective-permute-start | bytes 786440 | tf_op jit(solution)/shard_map/ppermute | solution.py:35
  338.2 9.2 %collective-permute-start.32 = (bf16[64,2048]{1,0:T(8,128)(2,1)S(1)}, bf16[64,2048]{1,0:T(8,128)(2,1)S(1)}, u32[]{:S(2)}, u32[]{:S(2)}) collective-permute-start(bf16[64,2048]{1,0:T(8,128)(2,1)S(1)} %get-tuple-element.170), channel_id=1, source_target_pairs={{0,1},{1,0},{2,3},{3,2},{4,5},{5,4},{6,7},{7,6},{8,9},{9,8},{10,11... | collective-permute-start | bytes 786440 | tf_op jit(solution)/shard_map/ppermute | solution.py:29
  338.9 14.9 %collective-permute-start.52 = (bf16[64,2048]{1,0:T(8,128)(2,1)S(1)}, bf16[64,2048]{1,0:T(8,128)(2,1)S(1)}, u32[]{:S(2)}, u32[]{:S(2)}) collective-permute-start(bf16[64,2048]{1,0:T(8,128)(2,1)S(1)} %get-tuple-element.171), channel_id=1, source_target_pairs={{2,0},{3,1},{0,2},{1,3},{6,4},{7,5},{4,6},{5,7},{10,8},{11,9},{8,1... | collective-permute-start | bytes 786440 | tf_op jit(solution)/shard_map/ppermute | solution.py:35
  340.5 12.6 %collective-permute-start.50 = (bf16[64,2048]{1,0:T(8,128)(2,1)S(1)}, bf16[64,2048]{1,0:T(8,128)(2,1)S(1)}, u32[]{:S(2)}, u32[]{:S(2)}) collective-permute-start(bf16[64,2048]{1,0:T(8,128)(2,1)S(1)} %get-tuple-element.173), channel_id=1, source_target_pairs={{0,1},{1,0},{2,3},{3,2},{4,5},{5,4},{6,7},{7,6},{8,9},{9,8},{10,11... | collective-permute-start | bytes 786440 | tf_op jit(solution)/shard_map/ppermute | solution.py:29
  347.5 34.9 %collective-permute-start.33 = (bf16[128,2048]{1,0:T(8,128)(2,1)S(1)}, bf16[128,2048]{1,0:T(8,128)(2,1)S(1)}, u32[]{:S(2)}, u32[]{:S(2)}) collective-permute-start(bf16[128,2048]{1,0:T(8,128)(2,1)S(1)} %pad_maximum_fusion.12), channel_id=1, source_target_pairs={{2,0},{3,1},{0,2},{1,3},{6,4},{7,5},{4,6},{5,7},{10,8},{11,9},{8,1... | collective-permute-start | bytes 1572872 | tf_op jit(solution)/shard_map/ppermute | solution.py:35
  348.3 36.5 %collective-permute-start.35 = (bf16[128,2048]{1,0:T(8,128)(2,1)S(1)}, bf16[128,2048]{1,0:T(8,128)(2,1)S(1)}, u32[]{:S(2)}, u32[]{:S(2)}) collective-permute-start(bf16[128,2048]{1,0:T(8,128)(2,1)S(1)} %pad_maximum_fusion.13), channel_id=1, source_target_pairs={{0,1},{1,0},{2,3},{3,2},{4,5},{5,4},{6,7},{7,6},{8,9},{9,8},{10,11... | collective-permute-start | bytes 1572872 | tf_op jit(solution)/shard_map/ppermute | solution.py:29
  353.1 18.8 %collective-permute-start.51 = (bf16[128,2048]{1,0:T(8,128)(2,1)S(1)}, bf16[128,2048]{1,0:T(8,128)(2,1)S(1)}, u32[]{:S(2)}, u32[]{:S(2)}) collective-permute-start(bf16[128,2048]{1,0:T(8,128)(2,1)S(1)} %pad_maximum_fusion.16), channel_id=1, source_target_pairs={{2,0},{3,1},{0,2},{1,3},{6,4},{7,5},{4,6},{5,7},{10,8},{11,9},{8,1... | collective-permute-start | bytes 1572872 | tf_op jit(solution)/shard_map/ppermute | solution.py:35
  353.9 19.6 %collective-permute-start.53 = (bf16[128,2048]{1,0:T(8,128)(2,1)S(1)}, bf16[128,2048]{1,0:T(8,128)(2,1)S(1)}, u32[]{:S(2)}, u32[]{:S(2)}) collective-permute-start(bf16[128,2048]{1,0:T(8,128)(2,1)S(1)} %pad_maximum_fusion.17), channel_id=1, source_target_pairs={{0,1},{1,0},{2,3},{3,2},{4,5},{5,4},{6,7},{7,6},{8,9},{9,8},{10,11... | collective-permute-start | bytes 1572872 | tf_op jit(solution)/shard_map/ppermute | solution.py:29
  412.7 180.5 %reduce-scatter.7.cloned.1.call-start = ((), (), s32[]{:S(2)}) async-start(), calls=%async_computation.5 | async-start | bytes 9437184 | tf_op jit(solution)/shard_map/reduce_scatter | solution.py:315
  502.1 129.5 %reduce-scatter.9.cloned.1.call-start = ((), (), s32[]{:S(2)}) async-start(), calls=%async_computation.6 | async-start | bytes 2359296 | tf_op jit(solution)/shard_map/reduce_scatter | solution.py:315
  503.6 13.4 %collective-permute-start.36 = (bf16[128,2048]{1,0:T(8,128)(2,1)S(1)}, bf16[128,2048]{1,0:T(8,128)(2,1)S(1)}, u32[]{:S(2)}, u32[]{:S(2)}) collective-permute-start(bf16[128,2048]{1,0:T(8,128)(2,1)S(1)} %get-tuple-element.112), channel_id=1, source_target_pairs={{0,2},{1,3},{2,0},{3,1},{4,6},{5,7},{6,4},{7,5},{8,10},{9,11},{10,... | collective-permute-start | bytes 1572872 | tf_op jit(solution)/shard_map/ppermute | solution.py:41
  505.1 12.4 %collective-permute-start.38 = (bf16[128,2048]{1,0:T(8,128)(2,1)S(1)}, bf16[128,2048]{1,0:T(8,128)(2,1)S(1)}, u32[]{:S(2)}, u32[]{:S(2)}) collective-permute-start(bf16[128,2048]{1,0:T(8,128)(2,1)S(1)} %get-tuple-element.113), channel_id=1, source_target_pairs={{0,1},{1,0},{2,3},{3,2},{4,5},{5,4},{6,7},{7,6},{8,9},{9,8},{10,11... | collective-permute-start | bytes 1572872 | tf_op jit(solution)/shard_map/ppermute | solution.py:29
  515.3 14.9 %collective-permute-start.54 = (bf16[128,2048]{1,0:T(8,128)(2,1)S(1)}, bf16[128,2048]{1,0:T(8,128)(2,1)S(1)}, u32[]{:S(2)}, u32[]{:S(2)}) collective-permute-start(bf16[128,2048]{1,0:T(8,128)(2,1)S(1)} %get-tuple-element.116), channel_id=1, source_target_pairs={{0,2},{1,3},{2,0},{3,1},{4,6},{5,7},{6,4},{7,5},{8,10},{9,11},{10,... | collective-permute-start | bytes 1572872 | tf_op jit(solution)/shard_map/ppermute | solution.py:41
  516.5 14.9 %collective-permute-start.56 = (bf16[128,2048]{1,0:T(8,128)(2,1)S(1)}, bf16[128,2048]{1,0:T(8,128)(2,1)S(1)}, u32[]{:S(2)}, u32[]{:S(2)}) collective-permute-start(bf16[128,2048]{1,0:T(8,128)(2,1)S(1)} %get-tuple-element.117), channel_id=1, source_target_pairs={{0,1},{1,0},{2,3},{3,2},{4,5},{5,4},{6,7},{7,6},{8,9},{9,8},{10,11... | collective-permute-start | bytes 1572872 | tf_op jit(solution)/shard_map/ppermute | solution.py:29
  518.0 16.9 %collective-permute-start.39 = (bf16[64,2048]{1,0:T(8,128)(2,1)S(1)}, bf16[64,2048]{1,0:T(8,128)(2,1)S(1)}, u32[]{:S(2)}, u32[]{:S(2)}) collective-permute-start(bf16[64,2048]{1,0:T(8,128)(2,1)S(1)} %slice.943), channel_id=1, source_target_pairs={{0,2},{1,3},{2,0},{3,1},{4,6},{5,7},{6,4},{7,5},{8,10},{9,11},{10,... | collective-permute-start | bytes 786440 | tf_op jit(solution)/shard_map/ppermute | solution.py:41
  519.0 20.9 %collective-permute-start.37 = (bf16[64,2048]{1,0:T(8,128)(2,1)S(1)}, bf16[64,2048]{1,0:T(8,128)(2,1)S(1)}, u32[]{:S(2)}, u32[]{:S(2)}) collective-permute-start(bf16[64,2048]{1,0:T(8,128)(2,1)S(1)} %slice.944), channel_id=1, source_target_pairs={{0,1},{1,0},{2,3},{3,2},{4,5},{5,4},{6,7},{7,6},{8,9},{9,8},{10,11... | collective-permute-start | bytes 786440 | tf_op jit(solution)/shard_map/ppermute | solution.py:29
  543.5 11.3 %collective-permute-start.42 = (bf16[64,2048]{1,0:T(8,128)(2,1)S(1)}, bf16[64,2048]{1,0:T(8,128)(2,1)S(1)}, u32[]{:S(2)}, u32[]{:S(2)}) collective-permute-start(bf16[64,2048]{1,0:T(8,128)(2,1)S(1)} %get-tuple-element.165), channel_id=1, source_target_pairs={{2,0},{3,1},{0,2},{1,3},{6,4},{7,5},{4,6},{5,7},{10,8},{11,9},{8,1... | collective-permute-start | bytes 786440 | tf_op jit(solution)/shard_map/ppermute | solution.py:35
  544.7 9.2 %collective-permute-start.40 = (bf16[64,2048]{1,0:T(8,128)(2,1)S(1)}, bf16[64,2048]{1,0:T(8,128)(2,1)S(1)}, u32[]{:S(2)}, u32[]{:S(2)}) collective-permute-start(bf16[64,2048]{1,0:T(8,128)(2,1)S(1)} %get-tuple-element.167), channel_id=1, source_target_pairs={{0,1},{1,0},{2,3},{3,2},{4,5},{5,4},{6,7},{7,6},{8,9},{9,8},{10,11... | collective-permute-start | bytes 786440 | tf_op jit(solution)/shard_map/ppermute | solution.py:29
  545.9 14.6 %collective-permute-start.60 = (bf16[64,2048]{1,0:T(8,128)(2,1)S(1)}, bf16[64,2048]{1,0:T(8,128)(2,1)S(1)}, u32[]{:S(2)}, u32[]{:S(2)}) collective-permute-start(bf16[64,2048]{1,0:T(8,128)(2,1)S(1)} %get-tuple-element.162), channel_id=1, source_target_pairs={{2,0},{3,1},{0,2},{1,3},{6,4},{7,5},{4,6},{5,7},{10,8},{11,9},{8,1... | collective-permute-start | bytes 786440 | tf_op jit(solution)/shard_map/ppermute | solution.py:35
  547.0 12.6 %collective-permute-start.58 = (bf16[64,2048]{1,0:T(8,128)(2,1)S(1)}, bf16[64,2048]{1,0:T(8,128)(2,1)S(1)}, u32[]{:S(2)}, u32[]{:S(2)}) collective-permute-start(bf16[64,2048]{1,0:T(8,128)(2,1)S(1)} %get-tuple-element.164), channel_id=1, source_target_pairs={{0,1},{1,0},{2,3},{3,2},{4,5},{5,4},{6,7},{7,6},{8,9},{9,8},{10,11... | collective-permute-start | bytes 786440 | tf_op jit(solution)/shard_map/ppermute | solution.py:29
  554.0 15.6 %collective-permute-start.41 = (bf16[128,2048]{1,0:T(8,128)(2,1)S(1)}, bf16[128,2048]{1,0:T(8,128)(2,1)S(1)}, u32[]{:S(2)}, u32[]{:S(2)}) collective-permute-start(bf16[128,2048]{1,0:T(8,128)(2,1)S(1)} %pad_maximum_fusion.14), channel_id=1, source_target_pairs={{2,0},{3,1},{0,2},{1,3},{6,4},{7,5},{4,6},{5,7},{10,8},{11,9},{8,1... | collective-permute-start | bytes 1572872 | tf_op jit(solution)/shard_map/ppermute | solution.py:35
  554.9 16.0 %collective-permute-start.43 = (bf16[128,2048]{1,0:T(8,128)(2,1)S(1)}, bf16[128,2048]{1,0:T(8,128)(2,1)S(1)}, u32[]{:S(2)}, u32[]{:S(2)}) collective-permute-start(bf16[128,2048]{1,0:T(8,128)(2,1)S(1)} %pad_maximum_fusion.15), channel_id=1, source_target_pairs={{0,1},{1,0},{2,3},{3,2},{4,5},{5,4},{6,7},{7,6},{8,9},{9,8},{10,11... | collective-permute-start | bytes 1572872 | tf_op jit(solution)/shard_map/ppermute | solution.py:29
  559.7 21.3 %collective-permute-start.59 = (bf16[128,2048]{1,0:T(8,128)(2,1)S(1)}, bf16[128,2048]{1,0:T(8,128)(2,1)S(1)}, u32[]{:S(2)}, u32[]{:S(2)}) collective-permute-start(bf16[128,2048]{1,0:T(8,128)(2,1)S(1)} %pad_maximum_fusion.18), channel_id=1, source_target_pairs={{2,0},{3,1},{0,2},{1,3},{6,4},{7,5},{4,6},{5,7},{10,8},{11,9},{8,1... | collective-permute-start | bytes 1572872 | tf_op jit(solution)/shard_map/ppermute | solution.py:35
  560.5 20.6 %collective-permute-start.61 = (bf16[128,2048]{1,0:T(8,128)(2,1)S(1)}, bf16[128,2048]{1,0:T(8,128)(2,1)S(1)}, u32[]{:S(2)}, u32[]{:S(2)}) collective-permute-start(bf16[128,2048]{1,0:T(8,128)(2,1)S(1)} %pad_maximum_fusion.19), channel_id=1, source_target_pairs={{0,1},{1,0},{2,3},{3,2},{4,5},{5,4},{6,7},{7,6},{8,9},{9,8},{10,11... | collective-permute-start | bytes 1572872 | tf_op jit(solution)/shard_map/ppermute | solution.py:29
  596.0 130.4 %reduce-scatter.11.cloned.1.call-start = ((), (), s32[]{:S(2)}) async-start(), calls=%async_computation.7 | async-start | bytes 7077888 | tf_op jit(solution)/shard_map/reduce_scatter | solution.py:315
  660.2 14.9 %collective-permute-start.44 = (bf16[128,2048]{1,0:T(8,128)(2,1)S(1)}, bf16[128,2048]{1,0:T(8,128)(2,1)S(1)}, u32[]{:S(2)}, u32[]{:S(2)}) collective-permute-start(bf16[128,2048]{1,0:T(8,128)(2,1)S(1)} %get-tuple-element.108), channel_id=1, source_target_pairs={{0,2},{1,3},{2,0},{3,1},{4,6},{5,7},{6,4},{7,5},{8,10},{9,11},{10,... | collective-permute-start | bytes 1572872 | tf_op jit(solution)/shard_map/ppermute | solution.py:41
  661.8 14.9 %collective-permute-start.46 = (bf16[128,2048]{1,0:T(8,128)(2,1)S(1)}, bf16[128,2048]{1,0:T(8,128)(2,1)S(1)}, u32[]{:S(2)}, u32[]{:S(2)}) collective-permute-start(bf16[128,2048]{1,0:T(8,128)(2,1)S(1)} %get-tuple-element.109), channel_id=1, source_target_pairs={{0,1},{1,0},{2,3},{3,2},{4,5},{5,4},{6,7},{7,6},{8,9},{9,8},{10,11... | collective-permute-start | bytes 1572872 | tf_op jit(solution)/shard_map/ppermute | solution.py:29
  666.4 19.6 %collective-permute-start.62 = (bf16[128,2048]{1,0:T(8,128)(2,1)S(1)}, bf16[128,2048]{1,0:T(8,128)(2,1)S(1)}, u32[]{:S(2)}, u32[]{:S(2)}) collective-permute-start(bf16[128,2048]{1,0:T(8,128)(2,1)S(1)} %get-tuple-element.104), channel_id=1, source_target_pairs={{0,2},{1,3},{2,0},{3,1},{4,6},{5,7},{6,4},{7,5},{8,10},{9,11},{10,... | collective-permute-start | bytes 1572872 | tf_op jit(solution)/shard_map/ppermute | solution.py:41
  667.5 19.4 %collective-permute-start.64 = (bf16[128,2048]{1,0:T(8,128)(2,1)S(1)}, bf16[128,2048]{1,0:T(8,128)(2,1)S(1)}, u32[]{:S(2)}, u32[]{:S(2)}) collective-permute-start(bf16[128,2048]{1,0:T(8,128)(2,1)S(1)} %get-tuple-element.105), channel_id=1, source_target_pairs={{0,1},{1,0},{2,3},{3,2},{4,5},{5,4},{6,7},{7,6},{8,9},{9,8},{10,11... | collective-permute-start | bytes 1572872 | tf_op jit(solution)/shard_map/ppermute | solution.py:29
  677.1 12.4 %collective-permute-start.47 = (bf16[64,2048]{1,0:T(8,128)(2,1)S(1)}, bf16[64,2048]{1,0:T(8,128)(2,1)S(1)}, u32[]{:S(2)}, u32[]{:S(2)}) collective-permute-start(bf16[64,2048]{1,0:T(8,128)(2,1)S(1)} %slice.941), channel_id=1, source_target_pairs={{0,2},{1,3},{2,0},{3,1},{4,6},{5,7},{6,4},{7,5},{8,10},{9,11},{10,... | collective-permute-start | bytes 786440 | tf_op jit(solution)/shard_map/ppermute | solution.py:41
  677.6 12.1 %collective-permute-start.45 = (bf16[64,2048]{1,0:T(8,128)(2,1)S(1)}, bf16[64,2048]{1,0:T(8,128)(2,1)S(1)}, u32[]{:S(2)}, u32[]{:S(2)}) collective-permute-start(bf16[64,2048]{1,0:T(8,128)(2,1)S(1)} %slice.942), channel_id=1, source_target_pairs={{0,1},{1,0},{2,3},{3,2},{4,5},{5,4},{6,7},{7,6},{8,9},{9,8},{10,11... | collective-permute-start | bytes 786440 | tf_op jit(solution)/shard_map/ppermute | solution.py:29
  (193 other events, 1875.5 us)
Sparse Core Ops, SparseCore 0:
  9.7 31.7 all-gather.10
  43.1 64.2 all-gather.8
  109.0 80.6 all-gather.12
  191.2 80.5 all-gather.14
  412.8 86.5 reduce-scatter.4
  502.3 87.9 reduce-scatter.6
  596.1 35.4 reduce-scatter.8
  633.9 68.4 reduce-scatter.10

commit v2 on v1

v2 whole, which is shorter than its diff:
```python
import functools
import types

import jax
import jax.numpy as jnp
from jax import lax
from jax.experimental import pallas as pl
from jax.experimental.pallas import tpu as pltpu
from jax.sharding import PartitionSpec as P

H = 16
HD = 128
FF = 8192
NB = 4
NHC = 4

EPSILON = 1e-05
HIGHEST = lax.Precision.HIGHEST
MASKED = -1e30
BF16 = jnp.bfloat16
F32 = jnp.float32
MESH = pl.DeviceIdType.MESH
MIB = 1024 * 1024
LANES = 128
STEP = 16

GATE = 4
LIVE = 5
SEQ = 8


def dot(left, right):
    return jnp.dot(left, right, preferred_element_type=F32)


def dot_nt(left, right):
    return lax.dot_general(left, right, (((1,), (1,)), ((), ())), preferred_element_type=F32)


def dot_tn(left, right):
    return lax.dot_general(left, right, (((0,), (0,)), ((), ())), preferred_element_type=F32)


def at(start, size=STEP):
    return pl.ds(pl.multiple_of(start, STEP), size)


class Links:
    def __init__(self, size, rows, send_sems, recv_sems):
        me = lax.axis_index("tensor")
        hi, lo = me // 2, me % 2
        self.me, self.size, self.high, self.half = me, size, size // 2, rows // 2
        self.near = hi * 2 + (1 - lo)
        self.ahead = [lax.rem(hi + s, self.high) * 2 + lo for s in range(self.high)]
        self.behind = [
            lax.rem(hi + self.high - s, self.high) * 2 + lo for s in range(self.high)
        ]
        self.send_sems, self.recv_sems, self.used = send_sems, recv_sems, 0
        self.second = self.half * size

    def greet(self, others=()):
        barrier = pltpu.get_barrier_semaphore()
        peers = [self.near] + self.ahead[1:] + list(others)
        for peer in peers:
            pl.semaphore_signal(
                barrier, inc=1, device_id={"tensor": peer}, device_id_type=MESH
            )
        pl.semaphore_wait(barrier, len(peers))

    def copy(self, src, dst, to):
        made = pltpu.make_async_remote_copy(
            src_ref=src,
            dst_ref=dst,
            send_sem=self.send_sems.at[self.used],
            recv_sem=self.recv_sems.at[self.used],
            device_id={"tensor": to},
            device_id_type=MESH,
        )
        self.used += 1
        made.start()
        return made


def transfers(size):
    return 2 * (size // 2)


class Gather:
    def __init__(self, links, buf, base):
        self.links, self.buf, self.base = links, buf, base

    def rows(self, start, count):
        return self.buf.at[pl.ds(self.base + start, count)]

    def start(self):
        k, half, second = self.links, self.links.half, self.links.second
        self.first_near = k.copy(self.rows(0, half), self.rows(half, half), k.near)
        self.second_far = [
            k.copy(self.rows(second, half), self.rows(second + s * half, half), k.behind[s])
            for s in range(1, k.high)
        ]

    def middle(self):
        k, half, second = self.links, self.links.half, self.links.second
        self.first_near.wait_recv()
        self.first_far = [
            k.copy(self.rows(0, 2 * half), self.rows(2 * half * s, 2 * half), k.behind[s])
            for s in range(1, k.high)
        ]
        for made in self.second_far:
            made.wait_recv()
        block = k.high * half
        self.second_near = k.copy(self.rows(second, block), self.rows(second + block, block), k.near)

    def finish(self):
        for made in self.first_far + [self.second_near]:
            made.wait_recv()
        for made in [self.first_near, self.second_near] + self.first_far + self.second_far:
            made.wait_send()


class Scatter:
    def __init__(self, links, part, base, landing, staged, last, total):
        self.links, self.part, self.base = links, part, base
        self.landing, self.staged, self.last, self.total = landing, staged, last, total

    def start(self):
        k, half = self.links, self.links.half
        block = k.high * half
        self.first_far = [
            k.copy(
                self.part.at[pl.ds(self.base + 2 * half * s, 2 * half)],
                self.landing.at[pl.ds(2 * half * (s - 1), 2 * half)],
                k.ahead[s],
            )
            for s in range(1, k.high)
        ]
        self.second_near = k.copy(
            self.part.at[pl.ds(self.base + k.second + block, block)],
            self.landing.at[pl.ds(2 * half * (k.high - 1), block)],
            k.near,
        )

    def middle(self):
        k, half, base = self.links, self.links.half, self.base
        steps = half // STEP
        for made in self.first_far:
            made.wait_recv()

        def first(i, _):
            for where in range(2):
                row = where * half + i * STEP
                value = self.part[at(base + row), :].astype(F32)
                for s in range(1, k.high):
                    value = value + self.landing[at(2 * half * (s - 1) + row), :].astype(F32)
                if where == 0:
                    self.total[at(i * STEP), :] = value
                else:
                    self.staged[at(i * STEP), :] = value.astype(BF16)
            return 0

        lax.fori_loop(0, steps, first, 0)
        self.first_near = k.copy(
            self.staged.at[pl.ds(0, half)], self.last.at[pl.ds(0, half)], k.near
        )
        self.second_near.wait_recv()
        landed = 2 * half * (k.high - 1)

        def second(i, _):
            for s in range(k.high):
                row = s * half + i * STEP
                value = self.part[at(base + k.second + row), :].astype(F32)
                value = value + self.landing[at(landed + row), :].astype(F32)
                if s == 0:
                    self.total[at(half + i * STEP), :] = value
                else:
                    self.staged[at(row), :] = value.astype(BF16)
            return 0

        lax.fori_loop(0, steps, second, 0)
        self.second_far = [
            k.copy(
                self.staged.at[pl.ds(half * s, half)], self.last.at[pl.ds(half * s, half)], k.ahead[s]
            )
            for s in range(1, k.high)
        ]
        for made in self.first_far + [self.second_near]:
            made.wait_send()

    def finish(self):
        for made in [self.first_near] + self.second_far:
            made.wait_recv()
            made.wait_send()

    def chunk(self, where, i):
        k, half = self.links, self.links.half
        value = self.total[at(where * half + i * STEP), :]
        if where == 0:
            return value + self.last[at(i * STEP), :].astype(F32)
        for s in range(1, k.high):
            value = value + self.last[at(half * s + i * STEP), :].astype(F32)
        return value


def over_rows(half, body):
    for where in range(2):

        def inner(i, _, where=where):
            body(where, i, where * half + i * STEP)
            return 0

        lax.fori_loop(0, half // STEP, inner, 0)


class Loads:
    def __init__(self, sems):
        self.sems, self.used = sems, 0

    def copy(self, src, dst):
        made = pltpu.make_async_copy(src, dst, self.sems.at[self.used])
        self.used += 1
        made.start()
        return made


def wait_all(*groups):
    for group in groups:
        for made in group if isinstance(group, list) else [group]:
            made.wait()


def columns_in(loads, blocks, flat):
    count, _, width = blocks.shape
    return [loads.copy(blocks.at[j], flat.at[:, pl.ds(j * width, width)]) for j in range(count)]


def tiles_out(count, make, tile, sems, target):
    def one(c, slot, wait):
        copy = pltpu.make_async_copy(tile.at[slot], target(c), sems.at[slot])
        if wait is not None:

            @pl.when(wait)
            def _():
                copy.wait()

        make(c, tile.at[slot])
        copy.start()

    if count == 1:
        one(0, 0, None)
    else:

        def pair(i, _):
            one(2 * i, 0, i > 0)
            one(2 * i + 1, 1, i > 0)
            return 0

        lax.fori_loop(0, count // 2, pair, 0)
    for slot in range(min(count, 2)):
        pltpu.make_async_copy(tile.at[slot], target(slot), sems.at[slot]).wait()


def normalized(value):
    centred = value - jnp.mean(value, axis=-1, keepdims=True)
    inverse = lax.rsqrt(jnp.mean(centred * centred, axis=-1, keepdims=True) + EPSILON)
    return centred * inverse, inverse


def norm_back(back, normed, inverse, gain):
    scaled = back * gain
    inner = jnp.mean(scaled, axis=-1, keepdims=True)
    along = jnp.mean(scaled * normed, axis=-1, keepdims=True)
    return inverse * (scaled - inner - normed * along)


def turned(value, cosine, sine):
    return value * cosine + pltpu.roll(value, HD // 2, 1) * sine


def first_norm_kernel(size, tokens, gain, bias, rows_out, buf, send, recv, out_sems):
    micro, rows, _ = tokens.shape
    links = Links(size, rows, send, recv)
    total = rows * size
    links.greet()
    gathers, loads = [], Loads(out_sems)
    for m in range(micro):

        def body(where, i, row, m=m):
            value = tokens[m, at(row), :].astype(F32)
            low = (normalized(value)[0] * gain[...] + bias[...]).astype(BF16)
            buf[at(m * total + where * links.second + i * STEP), :] = low

        over_rows(links.half, body)
        gathers.append(Gather(links, buf, m * total))
        gathers[m].start()
    for g in gathers:
        g.middle()
    outs = []
    for m, g in enumerate(gathers):
        g.finish()
        here = pl.ds(m * total, total)
        outs.append(loads.copy(buf.at[here], rows_out.at[here]))
    wait_all(outs)


def attend_kernel(
    size,
    heads,
    rows_hbm,
    mix_hbm,
    out_hbm,
    mask_hbm,
    cosine,
    sine,
    row_info,
    own,
    tokens,
    cotangent,
    gain,
    bias,
    router,
    qkv_out,
    heads_out,
    attention_out,
    second_out,
    share_out,
    branch_out,
    rows_buf,
    mix,
    out,
    mask,
    qkv,
    head_rows,
    part,
    landing,
    staged,
    last,
    second_buf,
    send,
    recv,
    load_sems,
):
    micro, rows, width = tokens.shape
    total = rows * size
    links = Links(size, rows, send, recv)
    half = links.half
    loads = Loads(load_sems)
    mix_copy = loads.copy(mix_hbm, mix)
    row_copies = [
        loads.copy(rows_hbm.at[pl.ds(m * total, total)], rows_buf.at[pl.ds(m * total, total)])
        for m in range(micro)
    ]
    mask_copy = loads.copy(mask_hbm, mask)
    out_copies = columns_in(loads, out_hbm, out)
    links.greet()
    mix_copy.wait()
    scale = HD ** (-0.5)
    span = 3 * HD
    chunk = min(128, total)
    tile = min(512, width)
    saves = []

    def project(m):
        base = m * total
        cos, sin = cosine[m], sine[m]

        def head(h, _):
            mixed = dot(
                rows_buf[pl.ds(base, total), :], mix[:, pl.ds(pl.multiple_of(h * span, HD), span)]
            )
            here = pl.ds(pl.multiple_of(h * HD, HD), HD)
            qkv[m, 0, :, here] = turned(mixed[:, :HD], cos, sin).astype(BF16)
            qkv[m, 1, :, here] = turned(mixed[:, HD : 2 * HD], cos, sin).astype(BF16)
            qkv[m, 2, :, here] = mixed[:, 2 * HD :].astype(BF16)
            return 0

        lax.fori_loop(0, heads, head, 0)

    def attend(m):
        base = m * total

        def some(c, _):
            rows_here = pl.ds(pl.multiple_of(c * chunk, chunk), chunk)
            bias_here = mask[m, rows_here, :]
            info = row_info[m, rows_here, :]
            for h in range(heads):
                here = pl.ds(h * HD, HD)
                scores = dot_nt(qkv[m, 0, rows_here, here], qkv[m, 1, :, here]) * scale + bias_here
                peak = jnp.max(scores, axis=-1, keepdims=True)
                powers = jnp.exp(scores - peak)
                share = powers / jnp.sum(powers, axis=-1, keepdims=True)
                value = dot(share.astype(BF16), qkv[m, 2, :, here]).astype(BF16)
                value = value.astype(F32) * info[:, h : h + 1]
                head_rows[pl.ds(pl.multiple_of(base + c * chunk, chunk), chunk), here] = value.astype(
                    BF16
                )
            return 0

        lax.fori_loop(0, total // chunk, some, 0)

    def merge(m):
        base = m * total

        def body(j, _):
            here = pl.ds(pl.multiple_of(j * tile, tile), tile)
            part[pl.ds(base, total), here] = dot(
                head_rows[pl.ds(base, total), :], out[:, here]
            ).astype(BF16)
            return 0

        lax.fori_loop(0, width // tile, body, 0)

    scatters = [
        Scatter(
            links,
            part,
            m * total,
            landing.at[m],
            staged.at[m],
            last.at[m],
            attention_out.at[m],
        )
        for m in range(micro)
    ]
    gathers = [Gather(links, second_buf, m * total) for m in range(micro)]

    def second_norm(m):
        scatter = scatters[m]

        def body(where, i, row):
            attended = scatter.chunk(where, i)
            info = own[m, at(row), :]
            hidden = tokens[m, at(row), :].astype(F32) + info[:, GATE : GATE + 1] * attended
            attention_out[m, at(row), :] = attended
            low = (normalized(hidden)[0] * gain[...] + bias[...]).astype(BF16)
            second_buf[at(m * total + where * links.second + i * STEP), :] = low
            logits = dot(low, router[...])
            lane = lax.broadcasted_iota(jnp.int32, logits.shape, 1)
            logits = jnp.where(lane < NB, logits, MASKED)
            powers = jnp.exp(logits - jnp.max(logits, axis=-1, keepdims=True))
            share = powers / jnp.sum(powers, axis=-1, keepdims=True)
            share = jnp.where(lane < NB, share, 0.0)
            share_out[m, at(row), :] = share
            gate = NB * jnp.sum(share * info, axis=-1, keepdims=True)
            outer = cotangent[m, at(row), :].astype(F32) * info[:, LIVE : LIVE + 1]
            branch_out[m, at(row), :] = (gate * outer).astype(BF16)

        over_rows(half, body)

    for m in range(micro):
        row_copies[m].wait()
        project(m)
        if m > 0:
            scatters[m - 1].middle()
        if m == 0:
            mask_copy.wait()
        attend(m)
        if m == 0:
            wait_all(out_copies)
        merge(m)
        scatters[m].start()
    for m in range(micro):
        if m == micro - 1:
            scatters[m].middle()
        scatters[m].finish()
        second_norm(m)
        gathers[m].start()
        if m > 0:
            gathers[m - 1].middle()
    saves.append(loads.copy(qkv, qkv_out))
    saves.append(loads.copy(head_rows, heads_out))
    gathers[micro - 1].middle()
    for m in range(micro):
        gathers[m].finish()
        here = pl.ds(m * total, total)
        saves.append(loads.copy(second_buf.at[here], second_out.at[here]))
    wait_all(saves)


def widen_kernel(
    size,
    unit_lane,
    second_hbm,
    up_hbm,
    branch,
    row_info,
    rect_out,
    active_out,
    branch_out,
    down_out,
    second_rows,
    up,
    branch_buf,
    rect,
    active,
    tile,
    send,
    recv,
    load_sems,
    tile_sems,
):
    micro, rows, width = branch.shape
    total = rows * size
    units = up.shape[1]
    links = Links(size, rows, send, recv)
    loads = Loads(load_sems)
    up_copy = loads.copy(up_hbm, up)
    second_copies = [
        loads.copy(second_hbm.at[pl.ds(m * total, total)], second_rows.at[pl.ds(m * total, total)])
        for m in range(micro)
    ]
    half = links.half
    own_copies = []
    for m in range(micro):
        for where in range(2):
            own_copies.append(
                loads.copy(
                    branch.at[m, pl.ds(where * half, half)],
                    branch_buf.at[pl.ds(m * total + where * links.second, half)],
                )
            )
    links.greet()
    wait_all(own_copies)
    gathers = [Gather(links, branch_buf, m * total) for m in range(micro)]
    for g in gathers:
        g.start()
    up_copy.wait()
    step = min(512, units)
    saves = []
    for m in range(micro):
        second_copies[m].wait()

        def body(j, _, m=m):
            here = pl.ds(pl.multiple_of(j * step, step), step)
            before = dot(second_rows[pl.ds(m * total, total), :], up[:, here])
            kept = jnp.maximum(before, 0.0) * row_info[m, :, unit_lane : unit_lane + 1]
            rect[pl.ds(m * total, total), here] = kept.astype(BF16)
            active[pl.ds(m * total, total), here] = (kept * kept).astype(BF16)
            return 0

        lax.fori_loop(0, units // step, body, 0)
        gathers[m].middle()
        here = pl.ds(m * total, total)
        saves.append(loads.copy(rect.at[here], rect_out.at[here]))
        saves.append(loads.copy(active.at[here], active_out.at[here]))
    for m, g in enumerate(gathers):
        g.finish()
        here = pl.ds(m * total, total)
        saves.append(loads.copy(branch_buf.at[here], branch_out.at[here]))
    count, _, block = down_out.shape
    wide = tile.shape[2]

    def make(c, slot):
        value = dot_tn(active[:, pl.ds(pl.multiple_of(c * wide, wide), wide)], branch_buf[...])
        for j in range(count):
            slot[j] = value[:, j * block : (j + 1) * block].astype(BF16)

    tiles_out(
        units // wide,
        make,
        tile,
        tile_sems,
        lambda c: down_out.at[:, pl.ds(pl.multiple_of(c * wide, wide), wide), :],
    )
    wait_all(saves)


def narrow_kernel(
    size,
    down_hbm,
    up_hbm,
    active_hbm,
    rect_hbm,
    branch_hbm,
    second_hbm,
    tokens,
    cotangent,
    attention,
    share,
    own,
    gain,
    router,
    block_out,
    up_out,
    hidden_out,
    back_out,
    stats_out,
    gate_out,
    down,
    up,
    active,
    rect,
    shared_rows,
    part,
    landing,
    staged,
    last,
    total_rows,
    gate_back,
    tile,
    send,
    recv,
    load_sems,
    tile_sems,
):
    micro, rows, width = tokens.shape
    total = rows * size
    units = up.shape[1]
    links = Links(size, rows, send, recv)
    half = links.half
    loads = Loads(load_sems)
    here = [pl.ds(m * total, total) for m in range(micro)]
    down_copies = columns_in(loads, down_hbm, down)
    active_copies = [loads.copy(active_hbm.at[h], active.at[h]) for h in here]
    branch_copies = [loads.copy(branch_hbm.at[h], shared_rows.at[h]) for h in here]
    rect_copies = [loads.copy(rect_hbm.at[h], rect.at[h]) for h in here]
    up_copy = loads.copy(up_hbm, up)
    stats_out[...] = jnp.zeros_like(stats_out)
    gate_out[...] = jnp.zeros_like(gate_out)
    links.greet()
    step = min(512, units)
    tile_cols = min(512, width)
    outs = [
        Scatter(
            links, part, m * total, landing.at[m], staged.at[m], last.at[m], total_rows.at[m]
        )
        for m in range(micro)
    ]
    backs = [
        Scatter(
            links,
            part,
            m * total,
            landing.at[micro + m],
            staged.at[micro + m],
            last.at[micro + m],
            hidden_out.at[m],
        )
        for m in range(micro)
    ]
    wait_all(down_copies)
    for m in range(micro):
        active_copies[m].wait()

        def body(j, _, m=m):
            cols = pl.ds(pl.multiple_of(j * tile_cols, tile_cols), tile_cols)
            part[here[m], cols] = dot(active[here[m], :], down[:, cols]).astype(BF16)
            return 0

        lax.fori_loop(0, width // tile_cols, body, 0)
        outs[m].start()
    for m in range(micro):
        branch_copies[m].wait()
        rect_copies[m].wait()

        def body(j, _, m=m):
            cols = pl.ds(pl.multiple_of(j * step, step), step)
            back = dot_nt(shared_rows[here[m], :], down[cols, :])
            active[here[m], cols] = (2.0 * rect[here[m], cols].astype(F32) * back).astype(BF16)
            return 0

        lax.fori_loop(0, units // step, body, 0)
        if m == 0:
            up_copy.wait()
    second_copies = [loads.copy(second_hbm.at[h], shared_rows.at[h]) for h in here]
    for m in range(micro):
        outs[m].middle()

        def body(j, _, m=m):
            cols = pl.ds(pl.multiple_of(j * tile_cols, tile_cols), tile_cols)
            part[here[m], cols] = dot_nt(active[here[m], :], up[cols, :]).astype(BF16)
            return 0

        lax.fori_loop(0, width // tile_cols, body, 0)
        backs[m].start()

    def finish_out(m):
        outs[m].finish()

        def body(where, i, row):
            branch = outs[m].chunk(where, i)
            info = own[m, at(row), :]
            live = info[:, LIVE : LIVE + 1]
            outer = cotangent[m, at(row), :].astype(F32) * live
            hidden = tokens[m, at(row), :].astype(F32)
            hidden = hidden + info[:, GATE : GATE + 1] * attention[m, at(row), :]
            gate = NB * jnp.sum(share[m, at(row), :] * info, axis=-1, keepdims=True)
            block_out[m, at(row), :] = (live * (hidden + gate * branch)).astype(BF16)
            value = jnp.sum(outer * branch, axis=-1, keepdims=True)
            gate_back[m, at(row), :] = jnp.broadcast_to(value, (STEP, LANES))

        over_rows(half, body)

    def finish_back(m):
        backs[m].finish()

        def body(where, i, row):
            back = backs[m].chunk(where, i)
            info = own[m, at(row), :]
            portions = share[m, at(row), :]
            live = info[:, LIVE : LIVE + 1]
            outer = cotangent[m, at(row), :].astype(F32) * live
            hidden = tokens[m, at(row), :].astype(F32)
            attended = attention[m, at(row), :]
            hidden = hidden + info[:, GATE : GATE + 1] * attended
            normed, inverse = normalized(hidden)
            low = (normed * gain[0:1, :] + gain[1:2, :]).astype(BF16).astype(F32)
            picked = jnp.sum(portions * info, axis=-1, keepdims=True)
            logit_back = NB * picked * (info - portions) * gate_back[m, at(row), :]
            for b in range(NB):
                column = logit_back[:, b : b + 1]
                back = back + column * router[b : b + 1, :]
                stats_out[2 + b : 3 + b, :] += jnp.sum(column * low, axis=0, keepdims=True)
            stats_out[0:1, :] += jnp.sum(back * normed, axis=0, keepdims=True)
            stats_out[1:2, :] += jnp.sum(back, axis=0, keepdims=True)
            hidden_back = outer + norm_back(back, normed, inverse, gain[0:1, :])
            hidden_out[m, at(row), :] = hidden_back
            back_out[m, at(row), :] = (info[:, GATE : GATE + 1] * hidden_back).astype(BF16)
            gate_part = jnp.sum(hidden_back * attended, axis=-1, keepdims=True)
            gate_out[m : m + 1, :] += jnp.sum(info * gate_part, axis=0, keepdims=True)

        over_rows(half, body)

    for m in range(micro):
        finish_out(m)
    wait_all(second_copies)
    block = up_out.shape[1]

    def make(c, slot):
        slot[...] = dot_tn(
            shared_rows[:, pl.ds(pl.multiple_of(c * block, block), block)], active[...]
        ).astype(BF16)

    tiles_out(up_out.shape[0], make, tile, tile_sems, lambda c: up_out.at[c])
    for m in range(micro):
        backs[m].middle()
    for m in range(micro):
        finish_back(m)


def attend_back_kernel(
    size,
    heads,
    _before,
    back,
    gate,
    out_hbm,
    qkv_hbm,
    heads_hbm,
    rows_hbm,
    mask_hbm,
    cosine,
    sine,
    row_info,
    mixed_out,
    out_term,
    mix_term,
    gate_out,
    buf,
    out,
    qkv,
    head_rows,
    rows_buf,
    mask,
    heads_back,
    mixed_back,
    score_back,
    shares,
    out_tile,
    mix_tile,
    gates,
    send,
    recv,
    load_sems,
    out_sems,
    mix_sems,
):
    micro, rows, width = back.shape
    total = rows * size
    links = Links(size, rows, send, recv)
    half = links.half
    loads = Loads(load_sems)
    own_copies = []
    for m in range(micro):
        for where in range(2):
            own_copies.append(
                loads.copy(
                    back.at[m, pl.ds(where * half, half)],
                    buf.at[pl.ds(m * total + where * links.second, half)],
                )
            )
    out_copies = columns_in(loads, out_hbm, out)
    qkv_copy = loads.copy(qkv_hbm, qkv)
    mask_copy = loads.copy(mask_hbm, mask)
    heads_copy = loads.copy(heads_hbm, head_rows)
    rows_copy = loads.copy(rows_hbm, rows_buf)
    gates[links.me] = gate[...]
    others = [lax.rem(links.me + s, size) for s in range(1, size)]
    barrier = pltpu.get_barrier_semaphore()
    for peer in others:
        pl.semaphore_signal(barrier, inc=1, device_id={"tensor": peer}, device_id_type=MESH)
    pl.semaphore_wait(barrier, size - 1)
    wait_all(own_copies)
    gathers = [Gather(links, buf, m * total) for m in range(micro)]
    for g in gathers:
        g.start()
    gate_copies = [links.copy(gate, gates.at[links.me], peer) for peer in others]
    wait_all(out_copies)
    qkv_copy.wait()
    mask_copy.wait()
    scale = HD ** (-0.5)
    chunk = min(128, total)
    for g in gathers:
        g.middle()
    for m in range(micro):
        gathers[m].finish()
        base = m * total
        every = pl.ds(base, total)
        value = dot_nt(buf[every, :], out[...])
        for h in range(heads):
            here = pl.ds(h * HD, HD)
            heads_back[:, here] = (
                value[:, h * HD : (h + 1) * HD] * row_info[m, :, h : h + 1]
            ).astype(BF16)
        for h in range(heads):
            here = pl.ds(h * HD, HD)

            def some(c, _, m=m, here=here):
                rows_here = pl.ds(pl.multiple_of(c * chunk, chunk), chunk)
                scores = dot_nt(qkv[m, 0, rows_here, here], qkv[m, 1, :, here]) * scale
                scores = scores + mask[m, rows_here, :]
                powers = jnp.exp(scores - jnp.max(scores, axis=-1, keepdims=True))
                share = powers / jnp.sum(powers, axis=-1, keepdims=True)
                share_back = dot_nt(heads_back[rows_here, here], qkv[m, 2, :, here])
                inner = jnp.sum(share * share_back, axis=-1, keepdims=True)
                score_back[rows_here, :] = (share * (share_back - inner)).astype(BF16)
                shares[rows_here, :] = share.astype(BF16)
                return 0

            lax.fori_loop(0, total // chunk, some, 0)
            cos, sin = cosine[m], -sine[m]
            query_back = dot(score_back[...], qkv[m, 1, :, here]) * scale
            keys_back = dot_tn(score_back[...], qkv[m, 0, :, here]) * scale
            values_back = dot_tn(shares[...], heads_back[:, here])
            col = 3 * h * HD
            mixed_back[every, pl.ds(col, HD)] = turned(query_back, cos, sin).astype(BF16)
            mixed_back[every, pl.ds(col + HD, HD)] = turned(keys_back, cos, sin).astype(BF16)
            mixed_back[every, pl.ds(col + 2 * HD, HD)] = values_back.astype(BF16)
    mixed_save = loads.copy(mixed_back, mixed_out)
    heads_copy.wait()
    count, depth, block = out_term.shape
    wide = out_tile.shape[2]

    def make_out(c, slot):
        value = dot_tn(head_rows[:, pl.ds(pl.multiple_of(c * wide, wide), wide)], buf[...])
        for j in range(count):
            slot[j] = value[:, j * block : (j + 1) * block].astype(BF16)

    tiles_out(
        depth // wide,
        make_out,
        out_tile,
        out_sems,
        lambda c: out_term.at[:, pl.ds(pl.multiple_of(c * wide, wide), wide), :],
    )
    rows_copy.wait()

    def make_mix(c, slot):
        slot[...] = dot_tn(
            rows_buf[:, pl.ds(pl.multiple_of(c * block, block), block)], mixed_back[...]
        ).astype(BF16)

    tiles_out(count, make_mix, mix_tile, mix_sems, lambda c: mix_term.at[c])
    for made in gate_copies:
        made.wait()
    gate_sum = gates[0]
    for r in range(1, size):
        gate_sum = gate_sum + gates[r]
    gate_out[...] = gate_sum
    mixed_save.wait()


def first_back_kernel(
    size,
    micro,
    _before,
    mixed_hbm,
    mix_hbm,
    back_out,
    mixed_back,
    mix,
    part,
    landing,
    staged,
    last,
    send,
    recv,
    load_sems,
):
    total = mixed_back.shape[0] // micro
    rows = total // size
    width = mix.shape[0]
    links = Links(size, rows, send, recv)
    loads = Loads(load_sems)
    here = [pl.ds(m * total, total) for m in range(micro)]
    mix_copy = loads.copy(mix_hbm, mix)
    mixed_copies = [loads.copy(mixed_hbm.at[h], mixed_back.at[h]) for h in here]
    links.greet()
    scatters = [
        Scatter(links, part, m * total, landing.at[m], staged.at[m], last.at[m], back_out.at[m])
        for m in range(micro)
    ]
    mix_copy.wait()
    tile = min(512, width)
    for m in range(micro):
        mixed_copies[m].wait()

        def body(j, _, m=m):
            cols = pl.ds(pl.multiple_of(j * tile, tile), tile)
            part[here[m], cols] = dot_nt(mixed_back[here[m], :], mix[cols, :]).astype(BF16)
            return 0

        lax.fori_loop(0, width // tile, body, 0)
        scatters[m].start()
    for s in scatters:
        s.middle()
    for m, s in enumerate(scatters):
        s.finish()

        def body(where, i, row, m=m, s=s):
            back_out[m, at(row), :] = s.chunk(where, i)

        over_rows(links.half, body)


def butterfly(value, axis, size):
    step = 1
    while step < size:
        value = value + lax.ppermute(value, axis, [(i, i ^ step) for i in range(size)])
        step *= 2
    return value


def norm_rows(value):
    centred = value - jnp.mean(value, axis=-1, keepdims=True)
    inverse = lax.rsqrt(jnp.mean(centred * centred, axis=-1, keepdims=True) + EPSILON)
    return centred * inverse, inverse


def rotary_tables(place):
    half = HD // 2
    rates = jnp.power(10000.0, -2.0 * jnp.arange(half, dtype=F32) / HD)
    angles = place.astype(F32)[:, None] * rates[None, :]
    cosine, sine = jnp.cos(angles), jnp.sin(angles)
    return jnp.concatenate([cosine, cosine], axis=1), jnp.concatenate([-sine, sine], axis=1)


def softmax_rows(logits):
    powers = jnp.exp(logits - jnp.max(logits, axis=-1, keepdims=True))
    return powers / jnp.sum(powers, axis=-1, keepdims=True)


def place_rows(lengths, slots):
    slot_count = lengths.shape[0]
    ends = jnp.cumsum(lengths, dtype=jnp.int32)
    starts = ends - lengths
    filled = ends[-1]
    member = jnp.sum((ends[None, :] <= slots[:, None]).astype(jnp.int32), axis=1, dtype=jnp.int32)
    begins = jnp.concatenate([starts, filled[None]])
    onehot = member[:, None] == jnp.arange(slot_count + 1, dtype=jnp.int32)[None, :]
    place = slots - jnp.sum(jnp.where(onehot, begins[None, :], 0), axis=1, dtype=jnp.int32)
    return member, place, slots < filled, onehot[:, :slot_count]


def gather_weights(piece):
    return lax.all_gather(piece, "dp", axis=0, tiled=False)


def share_out(term):
    return lax.psum_scatter(term, "dp", scatter_dimension=0, tiled=False)


ANY = pl.BlockSpec(memory_space=pl.ANY)
VMEM = pl.BlockSpec(memory_space=pltpu.VMEM)


def call(kernel, ident, ins, outs, scratch, copies, loads, extra=(), flops=0, limit=56):
    dma = pltpu.SemaphoreType.DMA
    sems = [dma((copies,)), dma((copies,)), dma((loads,))] + [dma((n,)) for n in extra]
    moved = sum(a.size * a.dtype.itemsize for a, _ in ins)
    return pl.pallas_call(
        kernel,
        out_shape=[jax.ShapeDtypeStruct(shape, kind) for shape, kind, _ in outs],
        in_specs=[VMEM if near else ANY for _, near in ins],
        out_specs=[VMEM if near else ANY for _, _, near in outs],
        scratch_shapes=[pltpu.VMEM(shape, kind) for shape, kind in scratch] + sems,
        compiler_params=pltpu.CompilerParams(
            collective_id=ident, has_side_effects=True, vmem_limit_bytes=limit * MIB
        ),
        cost_estimate=pl.CostEstimate(flops=flops, bytes_accessed=moved, transcendentals=0),
    )(*[a for a, _ in ins])


def local(
    dp_size,
    size,
    tokens,
    cotangent,
    mixer,
    merger,
    expand,
    shrink,
    attend_gain,
    attend_bias,
    feed_gain,
    feed_bias,
    width_router,
    head_router,
    lengths,
    head_choice,
    width_bucket,
):
    rank = lax.axis_index("tensor")
    micro, rows, width = tokens.shape
    total = width_bucket.shape[1]
    every = micro * total
    half = rows // 2
    high = size // 2
    heads = merger.shape[0] // HD
    units = expand.shape[1]
    block = width // dp_size
    gain_one = attend_gain.astype(F32)[None]
    bias_one = attend_bias.astype(F32)[None]
    gain_two = feed_gain.astype(F32)[None]
    bias_two = feed_bias.astype(F32)[None]
    router_width = width_router.astype(F32)
    router_head = head_router.astype(F32)

    mix_weight = gather_weights(mixer).reshape(width, -1)
    out_weight = gather_weights(merger)
    up_weight = gather_weights(expand).reshape(width, -1)
    down_weight = gather_weights(shrink)

    few = transfers(size)
    first_rows = call(
        functools.partial(first_norm_kernel, size),
        1,
        [(tokens, True), (gain_one, True), (bias_one, True)],
        [((every, width), BF16, False)],
        [((every, width), BF16)],
        micro * few,
        micro,
    )[0]

    hi, lo = rank // 2, rank % 2
    first_ranks = [((hi + s) % high) * 2 + (lo + l) % 2 for s in range(high) for l in range(2)]
    second_ranks = [((hi + s) % high) * 2 + (lo + l) % 2 for l in range(2) for s in range(high)]
    starts = [r * rows for r in first_ranks] + [r * rows + half for r in second_ranks]
    slots = jnp.concatenate([start + jnp.arange(half, dtype=jnp.int32) for start in starts])
    own_slots = rank * rows + jnp.arange(rows, dtype=jnp.int32)

    def columns(parts, count):
        joined = jnp.concatenate(parts, axis=1)
        return jnp.pad(joined, ((0, 0), (0, count - joined.shape[1])))

    infos, owns, masks, cosines, sines, micros = [], [], [], [], [], []
    for m in range(micro):
        member, place, _, seqmask = place_rows(lengths[m], slots)
        _, _, own_live, own_seq = place_rows(lengths[m], own_slots)
        choices = head_choice[m]
        buckets = jnp.concatenate(
            [lax.dynamic_slice_in_dim(width_bucket[m], start, half, 0) for start in starts]
        )
        own_buckets = lax.dynamic_slice_in_dim(width_bucket[m], rank * rows, rows, 0)
        bucket_hot = (own_buckets[:, None] == jnp.arange(NB, dtype=jnp.int32)[None, :]).astype(F32)
        choice_hot = (choices[:, None] == jnp.arange(NHC, dtype=jnp.int32)[None, :]).astype(F32)
        heads_used = jnp.sum(
            jnp.where(seqmask, H // NHC * (choices[None, :] + 1), 0), axis=1, dtype=jnp.int32
        )
        head_ids = rank * heads + jnp.arange(heads, dtype=jnp.int32)
        head_on = (head_ids[None, :] < heads_used[:, None]).astype(F32)
        unit_on = (rank * units < FF // NB * (buckets[:, None] + 1)).astype(F32)
        infos.append(columns([head_on, unit_on], LANES))
        seen = (member[:, None] == member[None, :]) & (slots[:, None] >= slots[None, :])
        masks.append(jnp.where(seen, 0.0, MASKED).astype(F32))
        cosine, sine = rotary_tables(place)
        cosines.append(cosine)
        sines.append(sine)
        seq_float = seqmask.astype(F32)
        own_seq = own_seq.astype(F32)
        own_live = own_live.astype(F32)
        divisor = jnp.maximum(jnp.sum(seq_float, axis=0), 1.0)
        sums = dot(seq_float.T.astype(BF16), first_rows[m * total : (m + 1) * total])
        means = sums / divisor[:, None]
        head_share = softmax_rows(jnp.dot(means, router_head, precision=HIGHEST))
        picked_head = jnp.sum(head_share * choice_hot, axis=1)
        own_gate = jnp.sum(own_seq * (NHC * picked_head)[None, :], axis=1, keepdims=True)
        pad = jnp.zeros((rows, SEQ - LIVE - 1), F32)
        owns.append(columns([bucket_hot, own_gate, own_live[:, None], pad, own_seq], LANES))
        micros.append(
            types.SimpleNamespace(
                divisor=divisor,
                head_share=head_share,
                picked_head=picked_head,
                choice_hot=choice_hot,
                own_seq=own_seq,
                width_use=jnp.sum(bucket_hot * own_live[:, None], axis=0),
                head_use=jnp.sum(own_seq[:, :, None] * choice_hot[None, :, :], axis=(0, 1)),
            )
        )
    row_info, own, mask = jnp.stack(infos), jnp.stack(owns), jnp.stack(masks)
    cosine, sine = jnp.stack(cosines), jnp.stack(sines)
    router_lanes = jnp.pad(width_router, ((0, 0), (0, LANES - NB)))
    router_rows = jnp.pad(router_width.T, ((0, 8 - NB), (0, 0)))
    gains_two = jnp.concatenate([gain_two, bias_two, jnp.zeros((6, width), F32)], axis=0)

    lands = half * (2 * (high - 1) + high)
    stages = half * high
    wide_heads = heads * HD
    span = 3 * wide_heads
    buffers = [((micro, lands, width), BF16), ((micro, stages, width), BF16), ((micro, stages, width), BF16)]
    qkv, head_rows, attention, second_rows, width_share, branch_own = call(
        functools.partial(attend_kernel, size, heads),
        2,
        [
            (first_rows, False),
            (mix_weight, False),
            (out_weight, False),
            (mask, False),
            (cosine, True),
            (sine, True),
            (row_info, True),
            (own, True),
            (tokens, True),
            (cotangent, True),
            (gain_two, True),
            (bias_two, True),
            (router_lanes, True),
        ],
        [
            ((micro, 3, total, wide_heads), BF16, False),
            ((every, wide_heads), BF16, False),
            ((micro, rows, width), F32, True),
            ((every, width), BF16, False),
            ((micro, rows, LANES), F32, True),
            ((micro, rows, width), BF16, True),
        ],
        [
            ((every, width), BF16),
            ((width, span), BF16),
            ((wide_heads, width), BF16),
            ((micro, total, total), F32),
            ((micro, 3, total, wide_heads), BF16),
            ((every, wide_heads), BF16),
            ((every, width), BF16),
        ]
        + buffers
        + [((every, width), BF16)],
        2 * micro * few,
        2 + micro + dp_size + 2 + micro,
        flops=2 * every * width * (span + wide_heads) + 8 * heads * micro * total * total * HD,
    )

    unit_tile = 256
    rect, active, branch_rows, down_term = call(
        functools.partial(widen_kernel, size, heads),
        3,
        [(second_rows, False), (up_weight, False), (branch_own, False), (row_info, True)],
        [
            ((every, units), BF16, False),
            ((every, units), BF16, False),
            ((every, width), BF16, False),
            ((dp_size, units, block), BF16, False),
        ],
        [
            ((every, width), BF16),
            ((width, units), BF16),
            ((every, width), BF16),
            ((every, units), BF16),
            ((every, units), BF16),
            ((2, dp_size, unit_tile, block), BF16),
        ],
        micro * few,
        1 + 6 * micro,
        (2,),
        flops=4 * every * width * units,
    )
    down_sum = share_out(down_term)

    block_output, up_term, hidden_back, back_own, stats_two, gate_part = call(
        functools.partial(narrow_kernel, size),
        4,
        [
            (down_weight, False),
            (up_weight, False),
            (active, False),
            (rect, False),
            (branch_rows, False),
            (second_rows, False),
            (tokens, True),
            (cotangent, True),
            (attention, True),
            (width_share, True),
            (own, True),
            (gains_two, True),
            (router_rows, True),
        ],
        [
            ((micro, rows, width), BF16, True),
            ((dp_size, block, units), BF16, False),
            ((micro, rows, width), F32, True),
            ((micro, rows, width), BF16, True),
            ((8, width), F32, True),
            ((8, LANES), F32, True),
        ],
        [
            ((units, width), BF16),
            ((width, units), BF16),
            ((every, units), BF16),
            ((every, units), BF16),
            ((every, width), BF16),
            ((every, width), BF16),
            ((2 * micro, lands, width), BF16),
            ((2 * micro, stages, width), BF16),
            ((2 * micro, stages, width), BF16),
            ((micro, rows, width), F32),
            ((micro, rows, LANES), F32),
            ((2, block, units), BF16),
        ],
        2 * micro * few,
        dp_size + 4 * micro + 1,
        (2,),
        flops=8 * every * width * units,
        limit=62,
    )
    up_sum = share_out(up_term)

    out_tile = min(256, wide_heads)
    mixed_back, out_term, mix_term, gate_total = call(
        functools.partial(attend_back_kernel, size, heads),
        5,
        [
            (down_sum, False),
            (back_own, False),
            (gate_part, True),
            (out_weight, False),
            (qkv, False),
            (head_rows, False),
            (first_rows, False),
            (mask, False),
            (cosine, True),
            (sine, True),
            (row_info, True),
        ],
        [
            ((every, span), BF16, False),
            ((dp_size, wide_heads, block), BF16, False),
            ((dp_size, block, span), BF16, False),
            ((8, LANES), F32, True),
        ],
        [
            ((every, width), BF16),
            ((wide_heads, width), BF16),
            ((micro, 3, total, wide_heads), BF16),
            ((every, wide_heads), BF16),
            ((every, width), BF16),
            ((micro, total, total), F32),
            ((total, wide_heads), BF16),
            ((every, span), BF16),
            ((total, total), BF16),
            ((total, total), BF16),
            ((2, dp_size, out_tile, block), BF16),
            ((2, block, span), BF16),
            ((size, 8, LANES), F32),
        ],
        micro * few + size - 1,
        2 * micro + dp_size + 5,
        (2, 2),
        flops=2 * every * width * (2 * wide_heads + span) + 20 * heads * micro * total * total * HD,
    )
    out_sum = share_out(out_term)
    mix_sum = share_out(mix_term)

    first_back = call(
        functools.partial(first_back_kernel, size, micro),
        6,
        [(up_sum, False), (mixed_back, False), (mix_weight, False)],
        [((micro, rows, width), F32, True)],
        [((every, span), BF16), ((width, span), BF16), ((every, width), BF16)] + buffers,
        micro * few,
        1 + micro,
        flops=2 * every * width * span,
    )[0]

    input_backs = []
    gain_one_sum = 0.0
    bias_one_sum = 0.0
    head_router_sum = 0.0
    for m, s in enumerate(micros):
        normed, inverse = norm_rows(tokens[m].astype(F32))
        low = (normed * gain_one + bias_one).astype(BF16)
        seq_gate_back = gate_total[m, SEQ : SEQ + s.own_seq.shape[1]]
        head_logit_back = (
            NHC * s.picked_head[:, None] * (s.choice_hot - s.head_share) * seq_gate_back[:, None]
        )
        spread = jnp.dot(s.own_seq, head_logit_back / s.divisor[:, None], precision=HIGHEST)
        back = first_back[m] + jnp.dot(spread, router_head.T, precision=HIGHEST)
        head_router_sum = head_router_sum + jnp.dot(spread.T, low.astype(F32), precision=HIGHEST)
        gain_one_sum = gain_one_sum + jnp.sum(back * normed, axis=0)
        bias_one_sum = bias_one_sum + jnp.sum(back, axis=0)
        input_backs.append(hidden_back[m] + norm_back(back, normed, inverse, gain_one))

    use = jnp.concatenate([sum(s.width_use for s in micros), sum(s.head_use for s in micros)])
    use_row = jnp.pad(use[None], ((0, 0), (0, width - NB - NHC)))
    stats = jnp.concatenate(
        [stats_two[: 2 + NB], gain_one_sum[None], bias_one_sum[None], head_router_sum, use_row],
        axis=0,
    )
    stats = butterfly(butterfly(stats, "tensor", size), "dp", dp_size)
    after = 4 + NB
    return (
        block_output,
        jnp.stack(input_backs, axis=0),
        mix_sum.astype(F32),
        out_sum.astype(F32),
        up_sum.astype(F32),
        down_sum.astype(F32),
        stats[2 + NB],
        stats[3 + NB],
        stats[0],
        stats[1],
        stats[2 : 2 + NB].T,
        stats[after : after + NHC].T,
        stats[after + NHC, :NB],
        stats[after + NHC, NB : NB + NHC],
    )


def solution(mesh):
    def run(*args):
        return local(mesh.shape["dp"], mesh.shape["tensor"], *args)

    rows = P(None, ("dp", "tensor"), None)
    tall, wide = P("dp", "tensor"), P("tensor", "dp")
    weights = (tall, wide, tall, wide)
    return jax.shard_map(
        run,
        mesh=mesh,
        in_specs=(rows, rows) + weights + (P(),) * 6 + (P(None, "dp"),) * 3,
        out_specs=(rows, rows) + weights + (P(),) * 8,
        check_vma=False,
    )
```

time: 744 us -> 586 us (0.79)
  Pallas kernels: 0 us -> 400 us
  matrix products: 188 us -> 9.24 us
  waiting for transfers between devices: 279 us -> 107 us
  local copies, waits for them, and re-layouts: 85.8 us -> 7.65 us
  starting transfers between devices: 79.1 us -> 8.32 us
  other arithmetic: 86.2 us -> 29.5 us
    pallas_call x0 -> x6, Pallas kernels: none -> 400 us  [call(): pl.pallas_call(kernel, out_shape=[jax.ShapeDtypeStruct(shape, kind) for s...]
    dot_general x52 -> x10, matrix products: 188 us -> 9.24 us  [the longest x2 3.99 us: dot(): return jnp.dot(left, right, preferred_element_type=F32)]
    ppermute x64 -> x0, waiting for transfers between devices: 135 us -> none  [the longest x16 55.5 us: from_high(): return lax.ppermute(value, 'tensor', pairs)]
    ppermute x64 -> x0, starting transfers between devices: 70.9 us -> none  [the longest x32 36.7 us: swap_low(): return lax.ppermute(value, 'tensor', [(i, i ^ 1) for i in range(size)])]
    all_gather x4, waiting for transfers between devices: 76.8 us -> 38.5 us  [gather_weights(): return lax.all_gather(piece, 'dp', axis=0, tiled=False)]
    unnamed x384 -> x40, local copies, waits for them, and re-layouts: 27.4 us -> 1.38 us
    convert_element_type x31 -> x13, other arithmetic: 36.8 us -> 11.1 us  [the longest x2 2.6 us: local(): own_live = own_live.astype(F32)]
    slice x41 -> x1, local copies, waits for them, and re-layouts: 20.6 us -> 0.62 us  [local(): stats[1]]
  transfers between devices with their start and end apart: 81 -> 13, of which waited for: 49 -> 8; matrix products, arithmetic and copies ran while one was open for 39% -> 7% of each run, Pallas kernels for 0% -> 69%
where the time goes in v2:
time: 586 us; the launch traced here: 577 us
  Pallas kernels  400 us (68%)
  waiting for transfers between devices  107 us (18%)
  other arithmetic  29.5 us (5%)
  between operations  15.2 us (3%)
  matrix products  9.24 us (2%)
  starting transfers between devices  8.32 us (1%)
  local copies, waits for them, and re-layouts  7.65 us (1%)
    pallas_call x6, Pallas kernels, call(): pl.pallas_call(kernel, out_shape=[jax.ShapeDtypeStruct(shape, kind) for s...  400 us
    reduce_scatter x4, waiting for transfers between devices, share_out(): return lax.psum_scatter(term, 'dp', scatter_dimension=0, tiled=False)  42.9 us
    all_gather x4, waiting for transfers between devices, gather_weights(): return lax.all_gather(piece, 'dp', axis=0, tiled=False)  38.5 us
    ppermute x5, waiting for transfers between devices, butterfly(): lax.ppermute(value, axis, [(i, i ^ step) for i in range(size)])  22.3 us
  transfers between devices with their start and end apart: 13, of which 8 were waited for; matrix products, arithmetic and copies ran while one was open for 7% of the time, Pallas kernels for 69%

profile of v2, /device:TPU:0, one launch (start us, length us, event | category | flops | bytes accessed | tf_op | source)
XLA Modules:
  0.0 577.1 jit_solution(526527834598945985)
XLA Ops:
  7.3 0.7 all-gather.15.cloned.1.call-update
  8.0 0.7 all-gather.13.cloned.1.call-update
  8.8 0.7 all-gather.11.cloned.1.call-update
  9.5 0.5 all-gather.9.cloned.1.call-update
  10.6 0.6 convert_element_type.172
  11.2 0.6 convert_element_type.173
  11.8 0.6 slice.121
  12.3 0.6 slice.123
  12.9 43.0 %shard_map.254.rows_hbm = bf16[1024,2048]{1,0:T(8,128)(2,1)} custom-call(bf16[2,128,2048]{2,1,0:T(8,128)(2,1)} %tokens.5, f32[1,2048]{1,0:T(1,128)} %bitcast.210, f32[1,2048]{1,0:T(1,128)} %bitcast.213), custom_call_target="tpu_custom_call" | custom-call | bytes 1064960 | tf_op jit(solution)/shard_map/pallas_call | solution.py:991
  56.1 1.3 compare_convert_fusion.2
  57.8 2.0 convolution_divide_fusion.1
  60.1 2.0 convolution_divide_fusion
  63.5 0.2 copy.59
  63.8 0.2 copy.60
  64.0 0.6 broadcast_in_dim.90
  64.6 0.6 broadcast_in_dim.91
  65.2 0.3 copy.63
  65.5 0.9 pad.34.router
  66.4 1.4 pad_add_fusion.2
  68.1 0.7 pad_maximum_fusion.4.own
  68.8 1.9 fusion.45
  71.2 0.8 add_convert_fusion.row_info
  72.1 0.8 pad_maximum_fusion.3.sine
  72.9 0.8 pad_maximum_fusion.2.cosine
  73.7 0.5 fusion.34
  74.2 1.5 pad_maximum_fusion.mask_hbm
  75.7 31.8 %all-gather.13.cloned.1.call-done.mix_hbm = bf16[2048,1536]{1,0:T(8,128)(2,1)} async-done(((bf16[256,1536]{1,0:T(8,128)(2,1)}), bf16[2048,1536]{1,0:T(8,128)(2,1)}) %all-gather.13.cloned.1.call-update) | async-done | bytes 6291472 | tf_op jit(solution)/shard_map/all_gather | solution.py:976
  107.5 103.6 %shard_map.255 = (bf16[2,3,512,512]{3,2,1,0:T(8,128)(2,1)}, bf16[1024,512]{1,0:T(8,128)(2,1)}, f32[2,128,2048]{2,1,0:T(8,128)}, bf16[1024,2048]{1,0:T(8,128)(2,1...) custom-call(bf16[1024,2048]{1,0:T(8,128)(2,1)} %shard_map.254.rows_hbm, ...), custom_call_target="tpu_custom_call" | custom-call | flops 10737418240 | bytes 19021824 | tf_op jit(solution)/shard_map/pallas_call | solution.py:991
  211.1 52.6 %shard_map.256 = (bf16[1024,2048]{1,0:T(8,128)(2,1)}, bf16[1024,2048]{1,0:T(8,128)(2,1)}, bf16[1024,2048]{1,0:T(8,128)(2,1)}, bf16[8,2048,256]{2,1,0:T(8,128)(2,1)}) custom-call(bf16[1024,2048]{1,0:T(8,128)(2,1)} %get-tuple-element.34.second_hbm, bf16[2048,2048]{1,0:T(8,128)(2,1)} %all-gather.11.cloned.1.call-done.up_hbm, ...), custom_call_target="tpu_custom_call" | custom-call | flops 17179869184 | bytes 14155776 | tf_op jit(solution)/shard_map/pallas_call | solution.py:991
  263.9 0.6 pad_convert_fusion.router
  264.5 0.7 maximum_maximum_fusion.gain
  265.2 6.7 %all-gather.9.cloned.1.call-done = bf16[16384,256]{1,0:T(8,128)(2,1)} async-done(((bf16[2048,256]{1,0:T(8,128)(2,1)}), bf16[16384,256]{1,0:T(8,128)(2,1)}) %all-gather.9.cloned.1.call-update) | async-done | bytes 8388624 | tf_op jit(solution)/shard_map/all_gather | solution.py:976
  272.0 94.7 %shard_map.257 = (bf16[2,128,2048]{2,1,0:T(8,128)(2,1)}, bf16[8,256,2048]{2,1,0:T(8,128)(2,1)}, f32[2,128,2048]{2,1,0:T(8,128)}, bf16[2,128,2048]{2,1,0:T(8,128)...) custom-call(bf16[8,2048,256]{2,1,0:T(8,128)(2,1)} %bitcast.230, bf16[2048,2048]{1,0:T(8,128)(2,1)} %all-gather.11.cloned.1.call-done.up_hbm, ...), custom_call_target="tpu_custom_call" | custom-call | flops 34359738368 | bytes 38141952 | tf_op jit(solution)/shard_map/pallas_call | solution.py:991
  366.7 63.6 %shard_map.258 = (bf16[1024,1536]{1,0:T(8,128)(2,1)}, bf16[8,512,256]{2,1,0:T(8,128)(2,1)}, bf16[8,256,1536]{2,1,0:T(8,128)(2,1)}, f32[8,128]{1,0:T(8,128)}) custom-call(bf16[2048,256]{1,0:T(8,128)(2,1)} %bitcast.208, bf16[2,128,2048]{2,1,0:T(8,128)(2,1)} %get-tuple-element.45.back, f32[8,128]{1,0:T(8,128)} %get-tuple-element.46.gate, ...), custom_call_target="tpu_custom_call" | custom-call | flops 16106127360 | bytes 16257024 | tf_op jit(solution)/shard_map/pallas_call | solution.py:991
  430.4 0.7 reduce-scatter.9.cloned.1.call-update
  431.3 1.3 compare_convert_fusion
  433.3 0.2 convert_reduce_fusion.1
  433.5 0.4 fusion.17
  434.0 0.8 slice_bitcast_fusion.5
  435.1 18.9 %reduce-scatter.5.cloned.1.call-done = bf16[1,256,2048]{2,1,0:T(8,128)(2,1)} async-done(((bf16[8,256,2048]{2,1,0:T(8,128)(2,1)}), bf16[1,256,2048]{2,1,0:T(8,128)(2,1)}) %reduce-scatter.5.cloned.1.call-update) | async-done | bytes 1048592 | tf_op jit(solution)/shard_map/reduce_scatter | solution.py:980
  454.0 42.7 %shard_map.259 = f32[2,128,2048]{2,1,0:T(8,128)} custom-call(bf16[256,2048]{1,0:T(8,128)(2,1)} %bitcast.209, bf16[1024,1536]{1,0:T(8,128)(2,1)} %get-tuple-element.49.mixed_hbm, bf16[2048,1536]{1,0:T(8,128)(2,1)} %all-gather.13.cloned.1.call-done.mix_hbm), custom_call_target="tpu_custom_call" | custom-call | flops 6442450944 | bytes 10485760 | tf_op jit(solution)/shard_map/pallas_call | solution.py:991
  496.7 2.1 convolution_add_fusion
  498.9 1.4 fusion.14
  500.4 0.5 fusion.41
  500.9 0.5 convolution_add_fusion.2
  501.5 1.7 collective-permute-start
  503.2 3.3 collective-permute-done
  506.6 1.7 collective-permute-start.1
  508.3 2.4 fusion.13
  510.7 0.9 collective-permute-done.1
  511.7 1.6 bitcast_convert_fusion.3
  513.3 2.3 collective-permute-start.3
  515.6 1.5 bitcast_convert_fusion.2
  517.0 6.5 %collective-permute-done.3 = f32[13,2048]{1,0:T(8,128)S(1)} collective-permute-done((f32[13,2048]{1,0:T(8,128)S(1)}, f32[13,2048]{1,0:T(8,128)S(1)}, u32[]{:S(2)}, u32[]{:S(2)}) %collective-permute-start.3) | collective-permute-done | bytes 106528 | tf_op jit(solution)/shard_map/ppermute | solution.py:939
  523.5 2.3 collective-permute-start.4
  525.8 1.5 pad_maximum_fusion.1
  527.4 11.6 %collective-permute-done.4 = f32[13,2048]{1,0:T(8,128)S(1)} collective-permute-done((f32[13,2048]{1,0:T(8,128)S(1)}, f32[13,2048]{1,0:T(8,128)S(1)}, u32[]{:S(2)}, u32[]{:S(2)}) %collective-permute-start.4) | collective-permute-done | bytes 106528 | tf_op jit(solution)/shard_map/ppermute | solution.py:939
  538.9 0.6 slice_bitcast_fusion.2
  539.5 0.6 fusion.89
  540.2 0.6 slice_bitcast_fusion
  540.8 1.8 bitcast_convert_fusion.1
  542.6 24.0 %reduce-scatter.9.cloned.1.call-done = bf16[1,256,1536]{2,1,0:T(8,128)(2,1)} async-done(((bf16[8,256,1536]{2,1,0:T(8,128)(2,1)}), bf16[1,256,1536]{2,1,0:T(8,128)(2,1)}) %reduce-scatter.9.cloned.1.call-update) | async-done | bytes 786448 | tf_op jit(solution)/shard_map/reduce_scatter | solution.py:980
  566.6 2.5 bitcast_convert_fusion
  569.1 1.0 copy.67
  (151 shorter events, 5.3 us)
Async XLA Ops:
  7.2 52.6 %copy-start = (bf16[2048,4]{0,1:T(4,128)(2,1)S(1)}, bf16[2048,4]{0,1:T(4,128)(2,1)}, u32[]{:S(2)}) copy-start(bf16[2048,4]{0,1:T(4,128)(2,1)} %param.26) | copy-start | bytes 49156
  7.2 3.0 copy-start.16
  7.2 3.3 copy-start.12
  7.2 3.9 copy-start.13
  7.2 68.5 %all-gather.15.cloned.1.call-start = ((), (), s32[]{:S(2)}) async-start(), calls=%async_computation.11 | async-start | bytes 2359296 | tf_op jit(solution)/shard_map/all_gather | solution.py:976
  8.0 99.5 %all-gather.13.cloned.1.call-start = ((), (), s32[]{:S(2)}) async-start(), calls=%async_computation.10 | async-start | bytes 7077888 | tf_op jit(solution)/shard_map/all_gather | solution.py:976
  8.7 202.4 %all-gather.11.cloned.1.call-start = ((), (), s32[]{:S(2)}) async-start(), calls=%async_computation.9 | async-start | bytes 9437184 | tf_op jit(solution)/shard_map/all_gather | solution.py:976
  9.4 262.5 %all-gather.9.cloned.1.call-start = ((), (), s32[]{:S(2)}) async-start(), calls=%async_computation.8 | async-start | bytes 9437184 | tf_op jit(solution)/shard_map/all_gather | solution.py:976
  10.0 356.7 %reduce-scatter.7.cloned.1.call-start = ((), (), s32[]{:S(2)}) async-start(), calls=%async_computation.5 | async-start | bytes 9437184 | tf_op jit(solution)/shard_map/reduce_scatter | solution.py:980
  12.9 44.5 %copy-start.17 = (s32[2,512]{1,0:T(2,128)S(1)}, s32[2,512]{1,0:T(2,128)}, u32[]{:S(2)}) copy-start(s32[2,512]{1,0:T(2,128)} %param.29) | copy-start | bytes 12292
  57.7 4.6 copy-start.18
  57.7 6.3 %copy-start.14 = (bf16[2048]{0:T(1024)(128)(2,1)S(1)}, bf16[2048]{0:T(1024)(128)(2,1)}, u32[]{:S(2)}) copy-start(bf16[2048]{0:T(1024)(128)(2,1)} %param.23) | copy-start | bytes 12292
  57.7 6.9 %copy-start.15 = (bf16[2048]{0:T(1024)(128)(2,1)S(1)}, bf16[2048]{0:T(1024)(128)(2,1)}, u32[]{:S(2)}) copy-start(bf16[2048]{0:T(1024)(128)(2,1)} %param.24) | copy-start | bytes 12292
  57.8 7.5 %copy-start.7 = (bf16[2048,4]{0,1:T(4,128)(2,1)S(1)}, bf16[2048,4]{0,1:T(4,128)(2,1)}, u32[]{:S(2)}) copy-start(bf16[2048,4]{0,1:T(4,128)(2,1)} %param.25) | copy-start | bytes 49156
  263.7 0.8 copy-start.10
  263.7 0.8 copy-start.11
  263.8 190.2 %reduce-scatter.5.cloned.1.call-start = ((), (), s32[]{:S(2)}) async-start(), calls=%async_computation.4 | async-start | bytes 9437184 | tf_op jit(solution)/shard_map/reduce_scatter | solution.py:980
  366.6 174.1 %reduce-scatter.11.cloned.1.call-start = ((), (), s32[]{:S(2)}) async-start(), calls=%async_computation.7 | async-start | bytes 2359296 | tf_op jit(solution)/shard_map/reduce_scatter | solution.py:980
  430.3 136.3 %reduce-scatter.9.cloned.1.call-start = ((), (), s32[]{:S(2)}) async-start(), calls=%async_computation.6 | async-start | bytes 7077888 | tf_op jit(solution)/shard_map/reduce_scatter | solution.py:980
  430.4 2.9 copy-start.1
  496.7 2.2 copy-start.5
  496.7 2.2 copy-start.6
  498.9 1.5 copy-start.9
  500.4 1.1 copy-start.8
  501.5 5.0 collective-permute-start
  506.6 5.0 collective-permute-start.1
  508.3 3.4 copy-start.3
  510.7 4.9 copy-start.2
  511.6 1.7 collective-permute-start.2
  513.3 10.2 %collective-permute-start.3 = (f32[13,2048]{1,0:T(8,128)S(1)}, f32[13,2048]{1,0:T(8,128)S(1)}, u32[]{:S(2)}, u32[]{:S(2)}) collective-permute-start(f32[13,2048]{1,0:T(8,128)S(1)} %add.429), channel_id=1, source_target_pairs={{0,8},{4,12},{8,0},{12,4},{16,24},{20,28},{24,16},{28,20},{1,9},{5... | collective-permute-start | bytes 319496 | tf_op jit(solution)/shard_map/ppermute | solution.py:939
  523.5 15.4 %collective-permute-start.4 = (f32[13,2048]{1,0:T(8,128)S(1)}, f32[13,2048]{1,0:T(8,128)S(1)}, u32[]{:S(2)}, u32[]{:S(2)}) collective-permute-start(f32[13,2048]{1,0:T(8,128)S(1)} %add.430), channel_id=1, source_target_pairs={{0,16},{4,20},{8,24},{12,28},{16,0},{20,4},{24,8},{28,12},{1,17},{... | collective-permute-start | bytes 319496 | tf_op jit(solution)/shard_map/ppermute | solution.py:939
  527.4 41.7 %copy-start.4 = (bf16[2,128,2048]{2,1,0:T(8,128)(2,1)S(1)}, bf16[2,128,2048]{2,1,0:T(8,128)(2,1)}, u32[]{:S(2)}) copy-start(bf16[2,128,2048]{2,1,0:T(8,128)(2,1)} %get-tuple-element.170) | copy-start | bytes 3145732
Sparse Core Ops, SparseCore 0:
  9.7 31.8 all-gather.14
  43.2 64.2 all-gather.12
  109.1 80.6 all-gather.10
  191.3 80.6 all-gather.8
  274.1 88.1 reduce-scatter.6
  366.8 87.1 reduce-scatter.4
  456.3 34.1 reduce-scatter.10
  492.7 73.7 reduce-scatter.8

commit v3 on v2

--- a/solution.py
+++ b/solution.py
@@ -1,5 +1,4 @@
 import functools
-import types
 
 import jax
 import jax.numpy as jnp
@@ -27,6 +26,16 @@
 GATE = 4
 LIVE = 5
 SEQ = 8
+CHOICE = 16
+
+PICKED = 4
+DIVISOR = 5
+CHOSEN = 6
+
+ATTEND = 0
+FEED = 2
+WIDTH_ROUTER = 4
+HEAD_ROUTER = 8
 
 
 def dot(left, right):
@@ -45,8 +54,33 @@
     return pl.ds(pl.multiple_of(start, STEP), size)
 
 
+class Copies:
+    def __init__(self, send_sems, recv_sems):
+        self.send_sems, self.recv_sems, self.used = send_sems, recv_sems, 0
+
+    def start(self, src, dst, axis, to):
+        made = pltpu.make_async_remote_copy(
+            src_ref=src,
+            dst_ref=dst,
+            send_sem=self.send_sems.at[self.used],
+            recv_sem=self.recv_sems.at[self.used],
+            device_id={axis: to},
+            device_id_type=MESH,
+        )
+        self.used += 1
+        made.start()
+        return made
+
+
+def greet(*peers):
+    barrier = pltpu.get_barrier_semaphore()
+    for axis, to in peers:
+        pl.semaphore_signal(barrier, inc=1, device_id={axis: to}, device_id_type=MESH)
+    pl.semaphore_wait(barrier, len(peers))
+
+
 class Links:
-    def __init__(self, size, rows, send_sems, recv_sems):
+    def __init__(self, size, rows, copies):
         me = lax.axis_index("tensor")
         hi, lo = me // 2, me % 2
         self.me, self.size, self.high, self.half = me, size, size // 2, rows // 2
@@ -55,30 +89,158 @@
         self.behind = [
             lax.rem(hi + self.high - s, self.high) * 2 + lo for s in range(self.high)
         ]
-        self.send_sems, self.recv_sems, self.used = send_sems, recv_sems, 0
         self.second = self.half * size
-
-    def greet(self, others=()):
-        barrier = pltpu.get_barrier_semaphore()
-        peers = [self.near] + self.ahead[1:] + list(others)
-        for peer in peers:
-            pl.semaphore_signal(
-                barrier, inc=1, device_id={"tensor": peer}, device_id_type=MESH
+        self.copies = copies
+        steps = range(self.high)
+        grid = [[lax.rem(hi + s, self.high) * 2 + (lo + l) % 2 for l in range(2)] for s in steps]
+        self.first_ranks = [grid[s][l] for s in steps for l in range(2)]
+        self.second_ranks = [grid[s][l] for l in range(2) for s in steps]
+        self.peers = [("tensor", to) for to in [self.near] + self.ahead[1:]]
+
+    def copy(self, src, dst, to):
+        return self.copies.start(src, dst, "tensor", to)
+
+
+class Column:
+    def __init__(self, size, copies):
+        self.me, self.chips, self.copies = lax.axis_index("dp"), size // 2, copies
+        self.chip, self.core = self.me // 2, self.me % 2
+        self.twin = self.chip * 2 + 1 - self.core
+        self.right = self.block(1)
+        self.left = self.block(-1)
+        self.ring = [("dp", self.left)]
+        self.pair = [("dp", self.twin)]
+
+    def chip_at(self, step):
+        return lax.rem(self.chip + self.chips + step, self.chips)
+
+    def block(self, step):
+        return self.chip_at(step) * 2 + self.core
+
+    def copy(self, src, dst, to):
+        return self.copies.start(src, dst, "dp", to)
+
+
+class WeightRing:
+    def __init__(self, column, loads, own, slot):
+        self.column, self.loads, self.own, self.slot = column, loads, own, slot
+
+    def start(self):
+        k = self.column
+        here = self.slot(k.me)
+        self.hops = [k.copy(self.own, here, k.right)]
+        self.twins = [k.copy(self.own, here, k.twin)]
+        self.local = self.loads.copy(self.own, here)
+
+    def advance(self):
+        k = self.column
+        step = len(self.twins)
+        self.hops[step - 1].wait_recv()
+        here = self.slot(k.block(-step))
+        if step < k.chips - 1:
+            self.hops.append(k.copy(here, here, k.right))
+        self.twins.append(k.copy(here, here, k.twin))
+
+    def finish(self):
+        while len(self.twins) < self.column.chips:
+            self.advance()
+        for made in self.twins:
+            made.wait()
+        for made in self.hops:
+            made.wait_send()
+        self.local.wait()
+
+
+def ring_copies(size):
+    return size // 2 * 2 - 1
+
+
+class SumRing:
+    def __init__(self, column, loads, mine, twin, target, own, other, landing, staged, tile, tile_sems):
+        self.column, self.loads = column, loads
+        self.mine, self.twin, self.target = mine, twin, target
+        self.own, self.other, self.landing, self.staged = own, other, landing, staged
+        self.tile, self.tile_sems = tile, tile_sems
+        self.hops = []
+        self.rows = tile.shape[1]
+
+    def load(self):
+        block = self.column.chip_at(-1 - len(self.hops))
+        self.loading = [
+            self.loads.copy(self.mine.at[block], self.own),
+            self.loads.copy(self.twin.at[block], self.other),
+        ]
+
+    def send(self, landed):
+        k, rows = self.column, self.rows
+
+        def body(i, _):
+            here = pl.ds(pl.multiple_of(i * rows, rows), rows)
+            value = self.own[here, :].astype(F32) + self.other[here, :].astype(F32)
+            if landed is not None:
+                value = value + self.landing[landed, here, :].astype(F32)
+            self.staged[here, :] = value.astype(BF16)
+            return 0
+
+        lax.fori_loop(0, self.own.shape[0] // rows, body, 0)
+        self.hops.append(k.copy(self.staged, self.landing.at[len(self.hops)], k.right))
+        self.load()
+
+    def start(self):
+        self.load()
+        wait_all(self.loading)
+        self.send(None)
+
+    def advance(self):
+        self.hops[-1].wait()
+        wait_all(self.loading)
+        self.send(len(self.hops) - 1)
+
+    def finish(self):
+        k, rows = self.column, self.rows
+        while len(self.hops) < k.chips - 1:
+            self.advance()
+        self.hops[-1].wait()
+        wait_all(self.loading)
+        landed = k.chips - 2
+
+        def body(i, _):
+            here = pl.ds(pl.multiple_of(i * rows, rows), rows)
+            slot = lax.rem(i, 2)
+            copy = pltpu.make_async_copy(
+                self.tile.at[slot], self.target.at[here], self.tile_sems.at[slot]
             )
-        pl.semaphore_wait(barrier, len(peers))
-
-    def copy(self, src, dst, to):
-        made = pltpu.make_async_remote_copy(
-            src_ref=src,
-            dst_ref=dst,
-            send_sem=self.send_sems.at[self.used],
-            recv_sem=self.recv_sems.at[self.used],
-            device_id={"tensor": to},
-            device_id_type=MESH,
-        )
-        self.used += 1
-        made.start()
-        return made
+
+            @pl.when(i >= 2)
+            def _():
+                copy.wait()
+
+            value = self.own[here, :].astype(F32) + self.other[here, :].astype(F32)
+            self.tile[slot] = value + self.landing[landed, here, :].astype(F32)
+            copy.start()
+            return 0
+
+        count = self.own.shape[0] // rows
+        lax.fori_loop(0, count, body, 0)
+        for i in range(max(count - 2, 0), count):
+            here = pl.ds(i * rows, rows)
+            pltpu.make_async_copy(
+                self.tile.at[i % 2], self.target.at[here], self.tile_sems.at[i % 2]
+            ).wait()
+
+
+def sum_rows(width):
+    return 128 if width <= 256 else 16
+
+
+def sum_scratch(chips, rows, width):
+    return [
+        ((rows, width), BF16),
+        ((rows, width), BF16),
+        ((chips - 1, rows, width), BF16),
+        ((rows, width), BF16),
+        ((2, sum_rows(width), width), F32),
+    ]
 
 
 def transfers(size):
@@ -234,30 +396,94 @@
     return [loads.copy(blocks.at[j], flat.at[:, pl.ds(j * width, width)]) for j in range(count)]
 
 
-def tiles_out(count, make, tile, sems, target):
-    def one(c, slot, wait):
-        copy = pltpu.make_async_copy(tile.at[slot], target(c), sems.at[slot])
-        if wait is not None:
-
-            @pl.when(wait)
-            def _():
-                copy.wait()
-
-        make(c, tile.at[slot])
-        copy.start()
-
-    if count == 1:
-        one(0, 0, None)
-    else:
-
-        def pair(i, _):
-            one(2 * i, 0, i > 0)
-            one(2 * i + 1, 1, i > 0)
-            return 0
-
-        lax.fori_loop(0, count // 2, pair, 0)
-    for slot in range(min(count, 2)):
-        pltpu.make_async_copy(tile.at[slot], target(slot), sems.at[slot]).wait()
+def halves_out(column, count, make, tile, mine, twin, sems, twin_sem):
+    wide = tile.shape[3]
+
+    def outs(c, slot):
+        here = pl.ds(pl.multiple_of(c * wide, wide), wide)
+        local = pltpu.make_async_copy(tile.at[slot, 0], mine.at[:, here, :], sems.at[slot])
+        away = pltpu.make_async_remote_copy(
+            src_ref=tile.at[slot, 1],
+            dst_ref=twin.at[:, here, :],
+            send_sem=sems.at[2 + slot],
+            recv_sem=twin_sem.at[0],
+            device_id={"dp": column.twin},
+            device_id_type=MESH,
+        )
+        return local, away
+
+    def body(c, _):
+        slot = lax.rem(c, 2)
+        local, away = outs(c, slot)
+
+        @pl.when(c >= 2)
+        def _():
+            local.wait()
+            away.wait_send()
+
+        def put(block, value):
+            tile[slot, lax.rem(block + column.core, 2), block // 2] = value
+
+        make(c, put)
+        local.start()
+        away.start()
+        return 0
+
+    lax.fori_loop(0, count, body, 0)
+    for c in range(max(count - 2, 0), count):
+        local, away = outs(c, c % 2)
+        local.wait()
+        away.wait_send()
+    all_landed(column, twin, sems, twin_sem)
+
+
+def blocks_out(column, make, tile, mine, twin, sems, twin_sem):
+    def outs(i):
+        local = pltpu.make_async_copy(tile.at[0], mine.at[i], sems.at[0])
+        away = pltpu.make_async_remote_copy(
+            src_ref=tile.at[1],
+            dst_ref=twin.at[i],
+            send_sem=sems.at[1],
+            recv_sem=twin_sem.at[0],
+            device_id={"dp": column.twin},
+            device_id_type=MESH,
+        )
+        return local, away
+
+    def body(i, _):
+        local, away = outs(i)
+
+        @pl.when(i > 0)
+        def _():
+            away.wait_send()
+
+        make(2 * i + 1 - column.core, tile.at[1])
+        away.start()
+
+        @pl.when(i > 0)
+        def _():
+            local.wait()
+
+        make(2 * i + column.core, tile.at[0])
+        local.start()
+        return 0
+
+    lax.fori_loop(0, column.chips, body, 0)
+    local, away = outs(column.chips - 1)
+    local.wait()
+    away.wait_send()
+    all_landed(column, twin, sems, twin_sem)
+
+
+def all_landed(column, twin, sems, twin_sem):
+    pltpu.make_async_remote_copy(
+        src_ref=twin,
+        dst_ref=twin,
+        send_sem=sems.at[0],
+        recv_sem=twin_sem.at[0],
+        device_id={"dp": column.twin},
+        device_id_type=MESH,
+    ).wait_recv()
 
 
 def normalized(value):
@@ -273,37 +499,188 @@
     return inverse * (scaled - inner - normed * along)
 
 
+def softmax_lanes(logits, lanes):
+    logits = jnp.where(lanes, logits, MASKED)
+    powers = jnp.exp(logits - jnp.max(logits, axis=-1, keepdims=True))
+    return jnp.where(lanes, powers / jnp.sum(powers, axis=-1, keepdims=True), 0.0)
+
+
 def turned(value, cosine, sine):
     return value * cosine + pltpu.roll(value, HD // 2, 1) * sine
 
 
-def first_norm_kernel(size, tokens, gain, bias, rows_out, buf, send, recv, out_sems):
+def first_norm_kernel(
+    dp_size,
+    size,
+    heads,
+    units,
+    tokens,
+    params,
+    rates,
+    bucket,
+    lengths,
+    choices,
+    mixer,
+    merger,
+    rows_out,
+    mix_out,
+    out_out,
+    mask,
+    cosine,
+    sine,
+    row_info,
+    own,
+    seq_info,
+    usage,
+    buf,
+    slot_col,
+    member_col,
+    bucket_col,
+    send,
+    recv,
+    load_sems,
+):
     micro, rows, _ = tokens.shape
-    links = Links(size, rows, send, recv)
+    count = lengths.shape[1]
+    copies, loads = Copies(send, recv), Loads(load_sems)
+    links, column = Links(size, rows, copies), Column(dp_size, copies)
     total = rows * size
-    links.greet()
-    gathers, loads = [], Loads(out_sems)
+    greet(*links.peers, *column.ring, *column.pair)
+    rings = [
+        WeightRing(column, loads, mixer, lambda i: mix_out.at[i]),
+        WeightRing(column, loads, merger, lambda i: out_out.at[i]),
+    ]
+    for ring in rings:
+        ring.start()
+    gathers = []
     for m in range(micro):
 
         def body(where, i, row, m=m):
             value = tokens[m, at(row), :].astype(F32)
-            low = (normalized(value)[0] * gain[...] + bias[...]).astype(BF16)
+            low = normalized(value)[0] * params[ATTEND : ATTEND + 1, :]
+            low = (low + params[ATTEND + 1 : ATTEND + 2, :]).astype(BF16)
             buf[at(m * total + where * links.second + i * STEP), :] = low
 
         over_rows(links.half, body)
         gathers.append(Gather(links, buf, m * total))
         gathers[m].start()
+
+    half = links.half
+    starts = [r * rows for r in links.first_ranks] + [r * rows + half for r in links.second_ranks]
+
+    def slots(shape, dimension):
+        index = lax.broadcasted_iota(jnp.int32, shape, dimension)
+        offset = jnp.full(shape, starts[0], jnp.int32)
+        for k in range(1, len(starts)):
+            offset = jnp.where(index >= k * half, starts[k] - k * half, offset)
+        return index + offset
+
+    def ends(m):
+        found, end = [], 0
+        for s in range(count):
+            end = end + lengths[m, s]
+            found.append(end)
+        return found
+
+    def members(m, slot):
+        member = jnp.zeros(slot.shape, jnp.int32)
+        begin = jnp.zeros(slot.shape, jnp.int32)
+        for end in ends(m):
+            member = member + jnp.where(slot >= end, 1, 0)
+            begin = jnp.where(slot >= end, end, begin)
+        return member, slot - begin
+
+    def by_member(member, values, other):
+        value = jnp.full(member.shape, other)
+        for s in range(count):
+            value = jnp.where(member == s, values[s], value)
+        return value
+
+    chunk = min(128, total)
+    lane = lax.broadcasted_iota(jnp.int32, (chunk, LANES), 1)
+    slot_row = slots((8, total), 1)
+    slot_col[...] = slots((total, LANES), 0)
+    member_rows = [members(m, slot_row)[0] for m in range(micro)]
+    for m in range(micro):
+
+        def table(c, _, m=m):
+            here = pl.ds(pl.multiple_of(c * chunk, chunk), chunk)
+            slot = slot_col[here, :]
+            member, place = members(m, slot)
+            member_col[m, here, :] = member
+            seen = (member[:, :1] == member_rows[m][:1, :]) & (slot[:, :1] >= slot_row[:1, :])
+            mask[m, here, :] = jnp.where(seen, 0.0, MASKED)
+            angle = place.astype(F32) * rates[...]
+            turn = jnp.sin(angle)
+            cosine[m, here, :] = jnp.cos(angle)
+            sine[m, here, :] = jnp.where(lane < HD // 2, -turn, turn)
+            natural = lax.broadcasted_iota(jnp.int32, (chunk, total), 1)
+            picked = jnp.where(slot[:, :1] == natural, bucket[m : m + 1, :].astype(F32), 0.0)
+            bucket_here = jnp.sum(picked, axis=-1, keepdims=True)
+            bucket_col[m, here, :] = jnp.broadcast_to(bucket_here, (chunk, LANES))
+            used = by_member(member, [H // NHC * (choices[m, s] + 1) for s in range(count)], 0)
+            head_on = jnp.where(links.me * heads + lane < used, 1.0, 0.0)
+            first_unit = jnp.full(lane.shape, links.me * units, jnp.int32).astype(F32)
+            unit_on = jnp.where(first_unit < FF // NB * (bucket_here + 1.0), 1.0, 0.0)
+            row_info[m, here, :] = jnp.where(
+                lane < heads, head_on, jnp.where(lane == heads, unit_on, 0.0)
+            )
+            return 0
+
+        lax.fori_loop(0, total // chunk, table, 0)
     for g in gathers:
         g.middle()
+    for ring in rings:
+        ring.advance()
     outs = []
+    usage[...] = jnp.zeros_like(usage)
+    few = lax.broadcasted_iota(jnp.int32, (8, LANES), 1)
+    which = lax.broadcasted_iota(jnp.int32, (8, LANES), 0)
+    lane_own = lax.broadcasted_iota(jnp.int32, (half, LANES), 1)
     for m, g in enumerate(gathers):
         g.finish()
         here = pl.ds(m * total, total)
         outs.append(loads.copy(buf.at[here], rows_out.at[here]))
+        sequence = lax.broadcasted_iota(jnp.int32, (8, total), 0)
+        hot = jnp.where(member_rows[m] == sequence, 1.0, 0.0).astype(BF16)
+        divisor = jnp.maximum(by_member(which, [lengths[m, s] for s in range(count)], 0), 1)
+        divisor = divisor.astype(F32)
+        chosen = by_member(which, [choices[m, s] for s in range(count)], 0)
+        means = dot(hot, buf[here, :]) / divisor[:, :1]
+        logits = jnp.full((8, LANES), MASKED)
+        for c in range(NHC):
+            router = params[HEAD_ROUTER + c : HEAD_ROUTER + c + 1, :]
+            logit = jnp.sum(means * router, axis=-1, keepdims=True)
+            logits = jnp.where(few == c, logit, logits)
+        share = softmax_lanes(logits, few < NHC)
+        picked = jnp.sum(jnp.where(few == chosen, share, 0.0), axis=-1, keepdims=True)
+        table = jnp.where(few == PICKED, picked, share)
+        table = jnp.where(few == DIVISOR, divisor, table)
+        seq_info[m] = jnp.where(few == CHOSEN, chosen.astype(F32), table)
+        for where in range(2):
+            source = pl.ds(where * links.second, half)
+            member = member_col[m, source, :]
+            gate = by_member(member, [NHC * picked[s : s + 1, :] for s in range(count)], 0.0)
+            choice = by_member(member, [choices[m, s] for s in range(count)], -NHC)
+            live = jnp.where(member < count, 1.0, 0.0)
+            kind = bucket_col[m, source, :].astype(jnp.int32)
+            hot = (lane_own == kind) | (lane_own == CHOICE + choice)
+            hot = hot | ((lane_own == SEQ + member) & (member < count))
+            value = jnp.where(hot & (choice >= -NHC), 1.0, 0.0)
+            value = jnp.where(lane_own == GATE, gate, value)
+            value = jnp.where(lane_own == LIVE, live, value)
+            own[m, pl.ds(where * half, half), :] = value
+            usage[0:1, :] += jnp.sum(value * live, axis=0, keepdims=True)
+    for step in range(column.chips - 2):
+        for ring in rings:
+            ring.advance()
+    for ring in rings:
+        ring.finish()
     wait_all(outs)
 
 
 def attend_kernel(
+    dp_size,
     size,
     heads,
     rows_hbm,
@@ -316,15 +693,17 @@
     own,
     tokens,
     cotangent,
-    gain,
-    bias,
-    router,
+    params,
+    expand,
+    shrink,
     qkv_out,
     heads_out,
     attention_out,
     second_out,
     share_out,
     branch_out,
+    up_out,
+    down_out,
     rows_buf,
     mix,
     out,
@@ -342,9 +721,9 @@
 ):
     micro, rows, width = tokens.shape
     total = rows * size
-    links = Links(size, rows, send, recv)
+    copies, loads = Copies(send, recv), Loads(load_sems)
+    links, column = Links(size, rows, copies), Column(dp_size, copies)
     half = links.half
-    loads = Loads(load_sems)
     mix_copy = loads.copy(mix_hbm, mix)
     row_copies = [
         loads.copy(rows_hbm.at[pl.ds(m * total, total)], rows_buf.at[pl.ds(m * total, total)])
@@ -352,7 +731,14 @@
     ]
     mask_copy = loads.copy(mask_hbm, mask)
     out_copies = columns_in(loads, out_hbm, out)
-    links.greet()
+    greet(*links.peers, *column.ring, *column.pair)
+    early = shrink.shape[0] // 2
+    rings = [
+        WeightRing(column, loads, expand, lambda i: up_out.at[i]),
+        WeightRing(column, loads, shrink.at[pl.ds(0, early)], lambda i: down_out.at[i]),
+    ]
+    for ring in rings:
+        ring.start()
     mix_copy.wait()
     scale = HD ** (-0.5)
     span = 3 * HD
@@ -432,14 +818,16 @@
             info = own[m, at(row), :]
             hidden = tokens[m, at(row), :].astype(F32) + info[:, GATE : GATE + 1] * attended
             attention_out[m, at(row), :] = attended
-            low = (normalized(hidden)[0] * gain[...] + bias[...]).astype(BF16)
+            low = normalized(hidden)[0] * params[FEED : FEED + 1, :]
+            low = (low + params[FEED + 1 : FEED + 2, :]).astype(BF16)
             second_buf[at(m * total + where * links.second + i * STEP), :] = low
-            logits = dot(low, router[...])
-            lane = lax.broadcasted_iota(jnp.int32, logits.shape, 1)
-            logits = jnp.where(lane < NB, logits, MASKED)
-            powers = jnp.exp(logits - jnp.max(logits, axis=-1, keepdims=True))
-            share = powers / jnp.sum(powers, axis=-1, keepdims=True)
-            share = jnp.where(lane < NB, share, 0.0)
+            low = low.astype(F32)
+            lane = lax.broadcasted_iota(jnp.int32, (STEP, LANES), 1)
+            logits = jnp.full((STEP, LANES), MASKED)
+            for b in range(NB):
+                router = params[WIDTH_ROUTER + b : WIDTH_ROUTER + b + 1, :]
+                logits = jnp.where(lane == b, jnp.sum(low * router, axis=-1, keepdims=True), logits)
+            share = softmax_lanes(logits, lane < NB)
             share_out[m, at(row), :] = share
             gate = NB * jnp.sum(share * info, axis=-1, keepdims=True)
             outer = cotangent[m, at(row), :].astype(F32) * info[:, LIVE : LIVE + 1]
@@ -452,6 +840,8 @@
         project(m)
         if m > 0:
             scatters[m - 1].middle()
+            for ring in rings:
+                ring.advance()
         if m == 0:
             mask_copy.wait()
         attend(m)
@@ -467,6 +857,9 @@
         gathers[m].start()
         if m > 0:
             gathers[m - 1].middle()
+        if m == 0:
+            for ring in rings:
+                ring.advance()
     saves.append(loads.copy(qkv, qkv_out))
     saves.append(loads.copy(head_rows, heads_out))
     gathers[micro - 1].middle()
@@ -474,20 +867,26 @@
         gathers[m].finish()
         here = pl.ds(m * total, total)
         saves.append(loads.copy(second_buf.at[here], second_out.at[here]))
+    for ring in rings:
+        ring.finish()
     wait_all(saves)
 
 
 def widen_kernel(
+    dp_size,
     size,
     unit_lane,
     second_hbm,
     up_hbm,
     branch,
     row_info,
+    shrink,
     rect_out,
     active_out,
     branch_out,
     down_out,
+    mine_out,
+    twin_out,
     second_rows,
     up,
     branch_buf,
@@ -498,12 +897,13 @@
     recv,
     load_sems,
     tile_sems,
+    twin_sem,
 ):
     micro, rows, width = branch.shape
     total = rows * size
     units = up.shape[1]
-    links = Links(size, rows, send, recv)
-    loads = Loads(load_sems)
+    copies, loads = Copies(send, recv), Loads(load_sems)
+    links, column = Links(size, rows, copies), Column(dp_size, copies)
     up_copy = loads.copy(up_hbm, up)
     second_copies = [
         loads.copy(second_hbm.at[pl.ds(m * total, total)], second_rows.at[pl.ds(m * total, total)])
@@ -519,7 +919,10 @@
                     branch_buf.at[pl.ds(m * total + where * links.second, half)],
                 )
             )
-    links.greet()
+    greet(*links.peers, *column.ring, *column.pair)
+    late = shrink.shape[0] // 2
+    ring = WeightRing(column, loads, shrink.at[pl.ds(late, late)], lambda i: down_out.at[i])
+    ring.start()
     wait_all(own_copies)
     gathers = [Gather(links, branch_buf, m * total) for m in range(micro)]
     for g in gathers:
@@ -540,6 +943,8 @@
 
         lax.fori_loop(0, units // step, body, 0)
         gathers[m].middle()
+        if m < column.chips - 1:
+            ring.advance()
         here = pl.ds(m * total, total)
         saves.append(loads.copy(rect.at[here], rect_out.at[here]))
         saves.append(loads.copy(active.at[here], active_out.at[here]))
@@ -547,27 +952,23 @@
         g.finish()
         here = pl.ds(m * total, total)
         saves.append(loads.copy(branch_buf.at[here], branch_out.at[here]))
-    count, _, block = down_out.shape
-    wide = tile.shape[2]
-
-    def make(c, slot):
+    block, wide = mine_out.shape[2], tile.shape[3]
+
+    def make(c, put):
         value = dot_tn(active[:, pl.ds(pl.multiple_of(c * wide, wide), wide)], branch_buf[...])
-        for j in range(count):
-            slot[j] = value[:, j * block : (j + 1) * block].astype(BF16)
-
-    tiles_out(
-        units // wide,
-        make,
-        tile,
-        tile_sems,
-        lambda c: down_out.at[:, pl.ds(pl.multiple_of(c * wide, wide), wide), :],
-    )
+        for j in range(dp_size):
+            put(j, value[:, j * block : (j + 1) * block].astype(BF16))
+
+    halves_out(column, units // wide, make, tile, mine_out, twin_out, tile_sems, twin_sem)
+    ring.finish()
     wait_all(saves)
 
 
 def narrow_kernel(
+    dp_size,
     size,
-    down_hbm,
+    down_early,
+    down_late,
     up_hbm,
     active_hbm,
     rect_hbm,
@@ -578,14 +979,17 @@
     attention,
     share,
     own,
-    gain,
-    router,
+    params,
+    mine_hbm,
+    twin_hbm,
     block_out,
-    up_out,
+    mine_out,
+    twin_out,
     hidden_out,
     back_out,
     stats_out,
     gate_out,
+    sum_out,
     down,
     up,
     active,
@@ -598,26 +1002,49 @@
     total_rows,
     gate_back,
     tile,
+    sum_own,
+    sum_other,
+    sum_landing,
+    sum_staged,
+    sum_tile,
     send,
     recv,
     load_sems,
     tile_sems,
+    twin_sem,
+    sum_sems,
 ):
     micro, rows, width = tokens.shape
     total = rows * size
     units = up.shape[1]
-    links = Links(size, rows, send, recv)
+    copies, loads = Copies(send, recv), Loads(load_sems)
+    links, column = Links(size, rows, copies), Column(dp_size, copies)
     half = links.half
-    loads = Loads(load_sems)
     here = [pl.ds(m * total, total) for m in range(micro)]
-    down_copies = columns_in(loads, down_hbm, down)
+    ring = SumRing(
+        column,
+        loads,
+        mine_hbm,
+        twin_hbm,
+        sum_out,
+        sum_own,
+        sum_other,
+        sum_landing,
+        sum_staged,
+        sum_tile,
+        sum_sems,
+    )
+    early = down_early.shape[1]
+    down_copies = columns_in(loads, down_early, down.at[pl.ds(0, early)])
+    down_copies += columns_in(loads, down_late, down.at[pl.ds(early, early)])
     active_copies = [loads.copy(active_hbm.at[h], active.at[h]) for h in here]
     branch_copies = [loads.copy(branch_hbm.at[h], shared_rows.at[h]) for h in here]
-    rect_copies = [loads.copy(rect_hbm.at[h], rect.at[h]) for h in here]
+    rect_copy = loads.copy(rect_hbm.at[here[0]], rect)
     up_copy = loads.copy(up_hbm, up)
     stats_out[...] = jnp.zeros_like(stats_out)
     gate_out[...] = jnp.zeros_like(gate_out)
-    links.greet()
+    greet(*links.peers, *column.ring, *column.pair)
+    ring.start()
     step = min(512, units)
     tile_cols = min(512, width)
     outs = [
@@ -651,18 +1078,22 @@
         outs[m].start()
     for m in range(micro):
         branch_copies[m].wait()
-        rect_copies[m].wait()
+        rect_copy.wait()
 
         def body(j, _, m=m):
             cols = pl.ds(pl.multiple_of(j * step, step), step)
             back = dot_nt(shared_rows[here[m], :], down[cols, :])
-            active[here[m], cols] = (2.0 * rect[here[m], cols].astype(F32) * back).astype(BF16)
+            active[here[m], cols] = (2.0 * rect[:, cols].astype(F32) * back).astype(BF16)
             return 0
 
         lax.fori_loop(0, units // step, body, 0)
+        if m + 1 < micro:
+            rect_copy = loads.copy(rect_hbm.at[here[m + 1]], rect)
         if m == 0:
             up_copy.wait()
     second_copies = [loads.copy(second_hbm.at[h], shared_rows.at[h]) for h in here]
+    if column.chips > 2:
+        ring.advance()
     for m in range(micro):
         outs[m].middle()
 
@@ -704,16 +1135,17 @@
             attended = attention[m, at(row), :]
             hidden = hidden + info[:, GATE : GATE + 1] * attended
             normed, inverse = normalized(hidden)
-            low = (normed * gain[0:1, :] + gain[1:2, :]).astype(BF16).astype(F32)
+            gain = params[FEED : FEED + 1, :]
+            low = (normed * gain + params[FEED + 1 : FEED + 2, :]).astype(BF16).astype(F32)
             picked = jnp.sum(portions * info, axis=-1, keepdims=True)
             logit_back = NB * picked * (info - portions) * gate_back[m, at(row), :]
             for b in range(NB):
                 column = logit_back[:, b : b + 1]
-                back = back + column * router[b : b + 1, :]
+                back = back + column * params[WIDTH_ROUTER + b : WIDTH_ROUTER + b + 1, :]
                 stats_out[2 + b : 3 + b, :] += jnp.sum(column * low, axis=0, keepdims=True)
             stats_out[0:1, :] += jnp.sum(back * normed, axis=0, keepdims=True)
             stats_out[1:2, :] += jnp.sum(back, axis=0, keepdims=True)
-            hidden_back = outer + norm_back(back, normed, inverse, gain[0:1, :])
+            hidden_back = outer + norm_back(back, normed, inverse, gain)
             hidden_out[m, at(row), :] = hidden_back
             back_out[m, at(row), :] = (info[:, GATE : GATE + 1] * hidden_back).astype(BF16)
             gate_part = jnp.sum(hidden_back * attended, axis=-1, keepdims=True)
@@ -721,27 +1153,30 @@
 
         over_rows(half, body)
 
+    if column.chips > 3:
+        ring.advance()
     for m in range(micro):
         finish_out(m)
     wait_all(second_copies)
-    block = up_out.shape[1]
-
-    def make(c, slot):
-        slot[...] = dot_tn(
+    block = mine_out.shape[1]
+
+    def make(c, ref):
+        ref[...] = dot_tn(
             shared_rows[:, pl.ds(pl.multiple_of(c * block, block), block)], active[...]
         ).astype(BF16)
 
-    tiles_out(up_out.shape[0], make, tile, tile_sems, lambda c: up_out.at[c])
+    blocks_out(column, make, tile, mine_out, twin_out, tile_sems, twin_sem)
     for m in range(micro):
         backs[m].middle()
+    ring.finish()
     for m in range(micro):
         finish_back(m)
 
 
 def attend_back_kernel(
+    dp_size,
     size,
     heads,
-    _before,
     back,
     gate,
     out_hbm,
@@ -752,10 +1187,15 @@
     cosine,
     sine,
     row_info,
+    mine_hbm,
+    twin_hbm,
     mixed_out,
-    out_term,
-    mix_term,
+    out_mine,
+    out_twin,
+    mix_mine,
+    mix_twin,
     gate_out,
+    sum_out,
     buf,
     out,
     qkv,
@@ -769,17 +1209,38 @@
     out_tile,
     mix_tile,
     gates,
+    sum_own,
+    sum_other,
+    sum_landing,
+    sum_staged,
+    sum_tile,
     send,
     recv,
     load_sems,
     out_sems,
+    out_twin_sem,
     mix_sems,
+    mix_twin_sem,
+    sum_sems,
 ):
     micro, rows, width = back.shape
     total = rows * size
-    links = Links(size, rows, send, recv)
+    copies, loads = Copies(send, recv), Loads(load_sems)
+    links, column = Links(size, rows, copies), Column(dp_size, copies)
     half = links.half
-    loads = Loads(load_sems)
+    ring = SumRing(
+        column,
+        loads,
+        mine_hbm,
+        twin_hbm,
+        sum_out,
+        sum_own,
+        sum_other,
+        sum_landing,
+        sum_staged,
+        sum_tile,
+        sum_sems,
+    )
     own_copies = []
     for m in range(micro):
         for where in range(2):
@@ -796,14 +1257,12 @@
     rows_copy = loads.copy(rows_hbm, rows_buf)
     gates[links.me] = gate[...]
     others = [lax.rem(links.me + s, size) for s in range(1, size)]
-    barrier = pltpu.get_barrier_semaphore()
-    for peer in others:
-        pl.semaphore_signal(barrier, inc=1, device_id={"tensor": peer}, device_id_type=MESH)
-    pl.semaphore_wait(barrier, size - 1)
+    greet(*[("tensor", to) for to in others], *column.ring, *column.pair)
     wait_all(own_copies)
     gathers = [Gather(links, buf, m * total) for m in range(micro)]
     for g in gathers:
         g.start()
+    ring.start()
     gate_copies = [links.copy(gate, gates.at[links.me], peer) for peer in others]
     wait_all(out_copies)
     qkv_copy.wait()
@@ -814,6 +1273,8 @@
         g.middle()
     for m in range(micro):
         gathers[m].finish()
+        if m + 2 < column.chips:
+            ring.advance()
         base = m * total
         every = pl.ds(base, total)
         value = dot_nt(buf[every, :], out[...])
@@ -848,29 +1309,25 @@
             mixed_back[every, pl.ds(col + 2 * HD, HD)] = values_back.astype(BF16)
     mixed_save = loads.copy(mixed_back, mixed_out)
     heads_copy.wait()
-    count, depth, block = out_term.shape
-    wide = out_tile.shape[2]
-
-    def make_out(c, slot):
+    block, wide = out_mine.shape[2], out_tile.shape[3]
+
+    def make_out(c, put):
         value = dot_tn(head_rows[:, pl.ds(pl.multiple_of(c * wide, wide), wide)], buf[...])
-        for j in range(count):
-            slot[j] = value[:, j * block : (j + 1) * block].astype(BF16)
-
-    tiles_out(
-        depth // wide,
-        make_out,
-        out_tile,
-        out_sems,
-        lambda c: out_term.at[:, pl.ds(pl.multiple_of(c * wide, wide), wide), :],
+        for j in range(dp_size):
+            put(j, value[:, j * block : (j + 1) * block].astype(BF16))
+
+    halves_out(
+        column, heads * HD // wide, make_out, out_tile, out_mine, out_twin, out_sems, out_twin_sem
     )
     rows_copy.wait()
 
-    def make_mix(c, slot):
-        slot[...] = dot_tn(
+    def make_mix(c, ref):
+        ref[...] = dot_tn(
             rows_buf[:, pl.ds(pl.multiple_of(c * block, block), block)], mixed_back[...]
         ).astype(BF16)
 
-    tiles_out(count, make_mix, mix_tile, mix_sems, lambda c: mix_term.at[c])
+    blocks_out(column, make_mix, mix_tile, mix_mine, mix_twin, mix_sems, mix_twin_sem)
+    ring.finish()
     for made in gate_copies:
         made.wait()
     gate_sum = gates[0]
@@ -880,32 +1337,65 @@
     mixed_save.wait()
 
 
+STATS_ONE = 6
+STATS_USE = 12
+STATS_ROWS = 16
+SEQ_COUNT = 4
+
+
 def first_back_kernel(
+    dp_size,
     size,
     micro,
-    _before,
     mixed_hbm,
     mix_hbm,
+    mix_mine,
+    mix_twin,
+    out_mine,
+    out_twin,
+    tokens,
+    hidden_back,
+    own,
+    seq_info,
+    gates,
+    params,
+    stats_two,
+    usage,
     back_out,
+    mix_sum,
+    out_sum,
+    stats_out,
     mixed_back,
     mix,
     part,
     landing,
     staged,
     last,
-    send,
-    recv,
-    load_sems,
+    *rest,
 ):
+    mix_bufs, out_bufs = rest[:5], rest[5:10]
+    stats, share, pieces, sums, whole = rest[10:15]
+    send, recv, load_sems, mix_sems, out_sems = rest[15:]
     total = mixed_back.shape[0] // micro
     rows = total // size
     width = mix.shape[0]
-    links = Links(size, rows, send, recv)
-    loads = Loads(load_sems)
+    copies, loads = Copies(send, recv), Loads(load_sems)
+    links, column = Links(size, rows, copies), Column(dp_size, copies)
     here = [pl.ds(m * total, total) for m in range(micro)]
+    rings = [
+        SumRing(column, loads, mix_mine, mix_twin, mix_sum, *mix_bufs, mix_sems),
+        SumRing(column, loads, out_mine, out_twin, out_sum, *out_bufs, out_sems),
+    ]
     mix_copy = loads.copy(mix_hbm, mix)
     mixed_copies = [loads.copy(mixed_hbm.at[h], mixed_back.at[h]) for h in here]
-    links.greet()
+    near = [lax.rem(links.me + s, size) for s in range(1, size)]
+    far = [lax.rem(column.me + s, dp_size) for s in range(1, dp_size)]
+    greet(*[("tensor", to) for to in near], *[("dp", to) for to in far])
+    for ring in rings:
+        ring.start()
+    stats[...] = jnp.zeros_like(stats)
+    stats[0:8, :] = stats_two[...]
+    stats[STATS_USE : STATS_USE + 1, 0:LANES] = usage[0:1, :]
     scatters = [
         Scatter(links, part, m * total, landing.at[m], staged.at[m], last.at[m], back_out.at[m])
         for m in range(micro)
@@ -922,66 +1412,80 @@
 
         lax.fori_loop(0, width // tile, body, 0)
         scatters[m].start()
+    if column.chips > 2:
+        for ring in rings:
+            ring.advance()
     for s in scatters:
         s.middle()
+    if column.chips > 3:
+        for ring in rings:
+            ring.advance()
     for m, s in enumerate(scatters):
         s.finish()
 
-        def body(where, i, row, m=m, s=s):
-            back_out[m, at(row), :] = s.chunk(where, i)
+        count = SEQ_COUNT
+        lane = lax.broadcasted_iota(jnp.int32, (8, LANES), 1)
+        which = lax.broadcasted_iota(jnp.int32, (8, LANES), 0)
+        info = seq_info[m]
+        gate_back = jnp.where(lane == SEQ + which, gates[m : m + 1, :], 0.0)
+        gate_back = jnp.sum(gate_back, axis=-1, keepdims=True)
+        chosen = jnp.where(lane == info[:, CHOSEN : CHOSEN + 1].astype(jnp.int32), 1.0, 0.0)
+        logit_back = NHC * info[:, PICKED : PICKED + 1] * (chosen - info) * gate_back
+        logit_back = logit_back / info[:, DIVISOR : DIVISOR + 1]
+
+        def body(where, i, row, m=m, s=s, logit_back=logit_back):
+            back = s.chunk(where, i)
+            normed, inverse = normalized(tokens[m, at(row), :].astype(F32))
+            gain = params[ATTEND : ATTEND + 1, :]
+            low = (normed * gain + params[ATTEND + 1 : ATTEND + 2, :]).astype(BF16).astype(F32)
+            rows_info = own[m, at(row), :]
+            spread = jnp.zeros((STEP, LANES), F32)
+            for q in range(count):
+                spread = spread + rows_info[:, SEQ + q : SEQ + q + 1] * logit_back[q : q + 1, :]
+            for c in range(NHC):
+                column = spread[:, c : c + 1]
+                back = back + column * params[HEAD_ROUTER + c : HEAD_ROUTER + c + 1, :]
+                at_row = STATS_ONE + 2 + c
+                stats[at_row : at_row + 1, :] += jnp.sum(column * low, axis=0, keepdims=True)
+            at_row = STATS_ONE
+            stats[at_row : at_row + 1, :] += jnp.sum(back * normed, axis=0, keepdims=True)
+            stats[at_row + 1 : at_row + 2, :] += jnp.sum(back, axis=0, keepdims=True)
+            value = norm_back(back, normed, inverse, gain)
+            back_out[m, at(row), :] = hidden_back[m, at(row), :] + value
 
         over_rows(links.half, body)
 
-
-def butterfly(value, axis, size):
-    step = 1
-    while step < size:
-        value = value + lax.ppermute(value, axis, [(i, i ^ step) for i in range(size)])
-        step *= 2
-    return value
-
-
-def norm_rows(value):
-    centred = value - jnp.mean(value, axis=-1, keepdims=True)
-    inverse = lax.rsqrt(jnp.mean(centred * centred, axis=-1, keepdims=True) + EPSILON)
-    return centred * inverse, inverse
-
-
-def rotary_tables(place):
-    half = HD // 2
-    rates = jnp.power(10000.0, -2.0 * jnp.arange(half, dtype=F32) / HD)
-    angles = place.astype(F32)[:, None] * rates[None, :]
-    cosine, sine = jnp.cos(angles), jnp.sin(angles)
-    return jnp.concatenate([cosine, cosine], axis=1), jnp.concatenate([-sine, sine], axis=1)
-
-
-def softmax_rows(logits):
-    powers = jnp.exp(logits - jnp.max(logits, axis=-1, keepdims=True))
-    return powers / jnp.sum(powers, axis=-1, keepdims=True)
-
-
-def place_rows(lengths, slots):
-    slot_count = lengths.shape[0]
-    ends = jnp.cumsum(lengths, dtype=jnp.int32)
-    starts = ends - lengths
-    filled = ends[-1]
-    member = jnp.sum((ends[None, :] <= slots[:, None]).astype(jnp.int32), axis=1, dtype=jnp.int32)
-    begins = jnp.concatenate([starts, filled[None]])
-    onehot = member[:, None] == jnp.arange(slot_count + 1, dtype=jnp.int32)[None, :]
-    place = slots - jnp.sum(jnp.where(onehot, begins[None, :], 0), axis=1, dtype=jnp.int32)
-    return member, place, slots < filled, onehot[:, :slot_count]
-
-
-def gather_weights(piece):
-    return lax.all_gather(piece, "dp", axis=0, tiled=False)
-
-
-def share_out(term):
-    return lax.psum_scatter(term, "dp", scatter_dimension=0, tiled=False)
+    piece = width // size
+    mine = pl.ds(pl.multiple_of(links.me * piece, piece), piece)
+    sent = [
+        links.copy(
+            stats.at[:, pl.ds(pl.multiple_of(to * piece, piece), piece)], pieces.at[links.me], to
+        )
+        for to in near
+    ]
+    pieces[links.me] = stats[:, mine]
+    wait_all(sent)
+    value = pieces[0]
+    for r in range(1, size):
+        value = value + pieces[r]
+    share[0] = value
+    sums[column.me] = value
+    wait_all([column.copy(share.at[0], sums.at[column.me], to) for to in far])
+    value = sums[0]
+    for r in range(1, dp_size):
+        value = value + sums[r]
+    share[1] = value
+    whole[links.me] = value
+    wait_all([links.copy(share.at[1], whole.at[links.me], to) for to in near])
+    for r in range(size):
+        stats_out[:, r * piece : (r + 1) * piece] = whole[r]
+    for ring in rings:
+        ring.finish()
 
 
 ANY = pl.BlockSpec(memory_space=pl.ANY)
 VMEM = pl.BlockSpec(memory_space=pltpu.VMEM)
+SMEM = pl.BlockSpec(memory_space=pltpu.SMEM)
 
 
 def call(kernel, ident, ins, outs, scratch, copies, loads, extra=(), flops=0, limit=56):
@@ -991,7 +1495,7 @@
     return pl.pallas_call(
         kernel,
         out_shape=[jax.ShapeDtypeStruct(shape, kind) for shape, kind, _ in outs],
-        in_specs=[VMEM if near else ANY for _, near in ins],
+        in_specs=[SMEM if near == "s" else VMEM if near else ANY for _, near in ins],
         out_specs=[VMEM if near else ANY for _, _, near in outs],
         scratch_shapes=[pltpu.VMEM(shape, kind) for shape, kind in scratch] + sems,
         compiler_params=pltpu.CompilerParams(
@@ -1020,7 +1524,6 @@
     head_choice,
     width_bucket,
 ):
-    rank = lax.axis_index("tensor")
     micro, rows, width = tokens.shape
     total = width_bucket.shape[1]
     every = micro * total
@@ -1029,98 +1532,61 @@
     heads = merger.shape[0] // HD
     units = expand.shape[1]
     block = width // dp_size
-    gain_one = attend_gain.astype(F32)[None]
-    bias_one = attend_bias.astype(F32)[None]
-    gain_two = feed_gain.astype(F32)[None]
-    bias_two = feed_bias.astype(F32)[None]
-    router_width = width_router.astype(F32)
-    router_head = head_router.astype(F32)
-
-    mix_weight = gather_weights(mixer).reshape(width, -1)
-    out_weight = gather_weights(merger)
-    up_weight = gather_weights(expand).reshape(width, -1)
-    down_weight = gather_weights(shrink)
-
+    chips = dp_size // 2
     few = transfers(size)
-    first_rows = call(
-        functools.partial(first_norm_kernel, size),
+    ringed = ring_copies(dp_size)
+
+    vectors = jnp.stack([attend_gain, attend_bias, feed_gain, feed_bias])
+    params = jnp.concatenate(
+        [vectors, width_router.T, head_router.T, jnp.zeros((4, width), BF16)], axis=0
+    ).astype(F32)
+    rates = jnp.power(10000.0, -2.0 * jnp.arange(HD // 2, dtype=F32) / HD)
+    rates = jnp.concatenate([rates, rates])[None]
+
+    tables = (micro, total, LANES)
+    first_rows, mix_weight, out_weight, mask, cosine, sine, row_info, own, seq_info, usage = call(
+        functools.partial(first_norm_kernel, dp_size, size, heads, units),
         1,
-        [(tokens, True), (gain_one, True), (bias_one, True)],
-        [((every, width), BF16, False)],
-        [((every, width), BF16)],
-        micro * few,
-        micro,
-    )[0]
-
-    hi, lo = rank // 2, rank % 2
-    first_ranks = [((hi + s) % high) * 2 + (lo + l) % 2 for s in range(high) for l in range(2)]
-    second_ranks = [((hi + s) % high) * 2 + (lo + l) % 2 for l in range(2) for s in range(high)]
-    starts = [r * rows for r in first_ranks] + [r * rows + half for r in second_ranks]
-    slots = jnp.concatenate([start + jnp.arange(half, dtype=jnp.int32) for start in starts])
-    own_slots = rank * rows + jnp.arange(rows, dtype=jnp.int32)
-
-    def columns(parts, count):
-        joined = jnp.concatenate(parts, axis=1)
-        return jnp.pad(joined, ((0, 0), (0, count - joined.shape[1])))
-
-    infos, owns, masks, cosines, sines, micros = [], [], [], [], [], []
-    for m in range(micro):
-        member, place, _, seqmask = place_rows(lengths[m], slots)
-        _, _, own_live, own_seq = place_rows(lengths[m], own_slots)
-        choices = head_choice[m]
-        buckets = jnp.concatenate(
-            [lax.dynamic_slice_in_dim(width_bucket[m], start, half, 0) for start in starts]
-        )
-        own_buckets = lax.dynamic_slice_in_dim(width_bucket[m], rank * rows, rows, 0)
-        bucket_hot = (own_buckets[:, None] == jnp.arange(NB, dtype=jnp.int32)[None, :]).astype(F32)
-        choice_hot = (choices[:, None] == jnp.arange(NHC, dtype=jnp.int32)[None, :]).astype(F32)
-        heads_used = jnp.sum(
-            jnp.where(seqmask, H // NHC * (choices[None, :] + 1), 0), axis=1, dtype=jnp.int32
-        )
-        head_ids = rank * heads + jnp.arange(heads, dtype=jnp.int32)
-        head_on = (head_ids[None, :] < heads_used[:, None]).astype(F32)
-        unit_on = (rank * units < FF // NB * (buckets[:, None] + 1)).astype(F32)
-        infos.append(columns([head_on, unit_on], LANES))
-        seen = (member[:, None] == member[None, :]) & (slots[:, None] >= slots[None, :])
-        masks.append(jnp.where(seen, 0.0, MASKED).astype(F32))
-        cosine, sine = rotary_tables(place)
-        cosines.append(cosine)
-        sines.append(sine)
-        seq_float = seqmask.astype(F32)
-        own_seq = own_seq.astype(F32)
-        own_live = own_live.astype(F32)
-        divisor = jnp.maximum(jnp.sum(seq_float, axis=0), 1.0)
-        sums = dot(seq_float.T.astype(BF16), first_rows[m * total : (m + 1) * total])
-        means = sums / divisor[:, None]
-        head_share = softmax_rows(jnp.dot(means, router_head, precision=HIGHEST))
-        picked_head = jnp.sum(head_share * choice_hot, axis=1)
-        own_gate = jnp.sum(own_seq * (NHC * picked_head)[None, :], axis=1, keepdims=True)
-        pad = jnp.zeros((rows, SEQ - LIVE - 1), F32)
-        owns.append(columns([bucket_hot, own_gate, own_live[:, None], pad, own_seq], LANES))
-        micros.append(
-            types.SimpleNamespace(
-                divisor=divisor,
-                head_share=head_share,
-                picked_head=picked_head,
-                choice_hot=choice_hot,
-                own_seq=own_seq,
-                width_use=jnp.sum(bucket_hot * own_live[:, None], axis=0),
-                head_use=jnp.sum(own_seq[:, :, None] * choice_hot[None, :, :], axis=(0, 1)),
-            )
-        )
-    row_info, own, mask = jnp.stack(infos), jnp.stack(owns), jnp.stack(masks)
-    cosine, sine = jnp.stack(cosines), jnp.stack(sines)
-    router_lanes = jnp.pad(width_router, ((0, 0), (0, LANES - NB)))
-    router_rows = jnp.pad(router_width.T, ((0, 8 - NB), (0, 0)))
-    gains_two = jnp.concatenate([gain_two, bias_two, jnp.zeros((6, width), F32)], axis=0)
+        [
+            (tokens, True),
+            (params, True),
+            (rates, True),
+            (width_bucket, True),
+            (lengths, "s"),
+            (head_choice, "s"),
+            (mixer, False),
+            (merger, False),
+        ],
+        [
+            ((every, width), BF16, False),
+            ((dp_size,) + mixer.shape, BF16, False),
+            ((dp_size,) + merger.shape, BF16, False),
+            ((micro, total, total), F32, True),
+            (tables, F32, True),
+            (tables, F32, True),
+            (tables, F32, True),
+            ((micro, rows, LANES), F32, True),
+            ((micro, 8, LANES), F32, True),
+            ((8, LANES), F32, True),
+        ],
+        [
+            ((every, width), BF16),
+            ((total, LANES), jnp.int32),
+            (tables, jnp.int32),
+            (tables, F32),
+        ],
+        micro * few + 2 * ringed,
+        micro + 2,
+    )
+    mix_weight = mix_weight.reshape(width, -1)
 
     lands = half * (2 * (high - 1) + high)
     stages = half * high
     wide_heads = heads * HD
     span = 3 * wide_heads
     buffers = [((micro, lands, width), BF16), ((micro, stages, width), BF16), ((micro, stages, width), BF16)]
-    qkv, head_rows, attention, second_rows, width_share, branch_own = call(
-        functools.partial(attend_kernel, size, heads),
+    qkv, head_rows, attention, second_rows, width_share, branch_own, up_weight, down_early = call(
+        functools.partial(attend_kernel, dp_size, size, heads),
         2,
         [
             (first_rows, False),
@@ -1133,9 +1599,9 @@
             (own, True),
             (tokens, True),
             (cotangent, True),
-            (gain_two, True),
-            (bias_two, True),
-            (router_lanes, True),
+            (params, True),
+            (expand, False),
+            (shrink, False),
         ],
         [
             ((micro, 3, total, wide_heads), BF16, False),
@@ -1144,6 +1610,8 @@
             ((every, width), BF16, False),
             ((micro, rows, LANES), F32, True),
             ((micro, rows, width), BF16, True),
+            ((dp_size,) + expand.shape, BF16, False),
+            ((dp_size, units // 2, block), BF16, False),
         ],
         [
             ((every, width), BF16),
@@ -1156,21 +1624,30 @@
         ]
         + buffers
         + [((every, width), BF16)],
-        2 * micro * few,
-        2 + micro + dp_size + 2 + micro,
+        2 * micro * few + 2 * ringed,
+        2 + micro + dp_size + 2 + micro + 2,
         flops=2 * every * width * (span + wide_heads) + 8 * heads * micro * total * total * HD,
     )
 
+    up_weight = up_weight.reshape(width, -1)
     unit_tile = 256
-    rect, active, branch_rows, down_term = call(
-        functools.partial(widen_kernel, size, heads),
+    rect, active, branch_rows, down_late, down_mine, down_twin = call(
+        functools.partial(widen_kernel, dp_size, size, heads),
         3,
-        [(second_rows, False), (up_weight, False), (branch_own, False), (row_info, True)],
+        [
+            (second_rows, False),
+            (up_weight, False),
+            (branch_own, False),
+            (row_info, True),
+            (shrink, False),
+        ],
         [
             ((every, units), BF16, False),
             ((every, units), BF16, False),
             ((every, width), BF16, False),
-            ((dp_size, units, block), BF16, False),
+            ((dp_size, units // 2, block), BF16, False),
+            ((chips, units, block), BF16, False),
+            ((chips, units, block), BF16, False),
         ],
         [
             ((every, width), BF16),
@@ -1178,20 +1655,20 @@
             ((every, width), BF16),
             ((every, units), BF16),
             ((every, units), BF16),
-            ((2, dp_size, unit_tile, block), BF16),
+            ((2, 2, chips, unit_tile, block), BF16),
         ],
-        micro * few,
-        1 + 6 * micro,
-        (2,),
+        micro * few + ringed,
+        2 + 6 * micro,
+        (4, 1),
         flops=4 * every * width * units,
     )
-    down_sum = share_out(down_term)
-
-    block_output, up_term, hidden_back, back_own, stats_two, gate_part = call(
-        functools.partial(narrow_kernel, size),
+
+    block_output, up_mine, up_twin, hidden_back, back_own, stats_two, gate_part, down_sum = call(
+        functools.partial(narrow_kernel, dp_size, size),
         4,
         [
-            (down_weight, False),
+            (down_early, False),
+            (down_late, False),
             (up_weight, False),
             (active, False),
             (rect, False),
@@ -1202,22 +1679,25 @@
             (attention, True),
             (width_share, True),
             (own, True),
-            (gains_two, True),
-            (router_rows, True),
+            (params, True),
+            (down_mine, False),
+            (down_twin, False),
         ],
         [
             ((micro, rows, width), BF16, True),
-            ((dp_size, block, units), BF16, False),
+            ((chips, block, units), BF16, False),
+            ((chips, block, units), BF16, False),
             ((micro, rows, width), F32, True),
             ((micro, rows, width), BF16, True),
             ((8, width), F32, True),
             ((8, LANES), F32, True),
+            ((units, block), F32, False),
         ],
         [
             ((units, width), BF16),
             ((width, units), BF16),
             ((every, units), BF16),
-            ((every, units), BF16),
+            ((total, units), BF16),
             ((every, width), BF16),
             ((every, width), BF16),
             ((2 * micro, lands, width), BF16),
@@ -1226,21 +1706,20 @@
             ((micro, rows, width), F32),
             ((micro, rows, LANES), F32),
             ((2, block, units), BF16),
-        ],
-        2 * micro * few,
-        dp_size + 4 * micro + 1,
-        (2,),
+        ]
+        + sum_scratch(chips, units, block),
+        2 * micro * few + chips - 1,
+        2 * dp_size + 4 * micro + 1 + 2 * chips,
+        (2, 1, 2),
         flops=8 * every * width * units,
-        limit=62,
+        limit=63,
     )
-    up_sum = share_out(up_term)
 
     out_tile = min(256, wide_heads)
-    mixed_back, out_term, mix_term, gate_total = call(
-        functools.partial(attend_back_kernel, size, heads),
+    mixed_back, out_mine, out_twin, mix_mine, mix_twin, gate_total, up_sum = call(
+        functools.partial(attend_back_kernel, dp_size, size, heads),
         5,
         [
-            (down_sum, False),
             (back_own, False),
             (gate_part, True),
             (out_weight, False),
@@ -1251,12 +1730,17 @@
             (cosine, True),
             (sine, True),
             (row_info, True),
+            (up_mine, False),
+            (up_twin, False),
         ],
         [
             ((every, span), BF16, False),
-            ((dp_size, wide_heads, block), BF16, False),
-            ((dp_size, block, span), BF16, False),
+            ((chips, wide_heads, block), BF16, False),
+            ((chips, wide_heads, block), BF16, False),
+            ((chips, block, span), BF16, False),
+            ((chips, block, span), BF16, False),
             ((8, LANES), F32, True),
+            ((block, units), F32, False),
         ],
         [
             ((every, width), BF16),
@@ -1269,70 +1753,73 @@
             ((every, span), BF16),
             ((total, total), BF16),
             ((total, total), BF16),
-            ((2, dp_size, out_tile, block), BF16),
+            ((2, 2, chips, out_tile, block), BF16),
             ((2, block, span), BF16),
             ((size, 8, LANES), F32),
-        ],
-        micro * few + size - 1,
-        2 * micro + dp_size + 5,
-        (2, 2),
+        ]
+        + sum_scratch(chips, block, units),
+        micro * few + size - 1 + chips - 1,
+        2 * micro + dp_size + 5 + 2 * chips,
+        (4, 1, 2, 1, 2),
         flops=2 * every * width * (2 * wide_heads + span) + 20 * heads * micro * total * total * HD,
     )
-    out_sum = share_out(out_term)
-    mix_sum = share_out(mix_term)
-
-    first_back = call(
-        functools.partial(first_back_kernel, size, micro),
+
+    tokens_gradient, mix_sum, out_sum, stats = call(
+        functools.partial(first_back_kernel, dp_size, size, micro),
         6,
-        [(up_sum, False), (mixed_back, False), (mix_weight, False)],
-        [((micro, rows, width), F32, True)],
-        [((every, span), BF16), ((width, span), BF16), ((every, width), BF16)] + buffers,
-        micro * few,
-        1 + micro,
+        [
+            (mixed_back, False),
+            (mix_weight, False),
+            (mix_mine, False),
+            (mix_twin, False),
+            (out_mine, False),
+            (out_twin, False),
+            (tokens, True),
+            (hidden_back, True),
+            (own, True),
+            (seq_info, True),
+            (gate_total, True),
+            (params, True),
+            (stats_two, True),
+            (usage, True),
+        ],
+        [
+            ((micro, rows, width), F32, True),
+            ((block, span), F32, False),
+            ((wide_heads, block), F32, False),
+            ((STATS_ROWS, width), F32, True),
+        ],
+        [((every, span), BF16), ((width, span), BF16), ((every, width), BF16)]
+        + buffers
+        + sum_scratch(chips, block, span)
+        + sum_scratch(chips, wide_heads, block)
+        + [
+            ((STATS_ROWS, width), F32),
+            ((2, STATS_ROWS, width // size), F32),
+            ((size, STATS_ROWS, width // size), F32),
+            ((dp_size, STATS_ROWS, width // size), F32),
+            ((size, STATS_ROWS, width // size), F32),
+        ],
+        micro * few + 2 * (chips - 1) + 2 * (size - 1) + dp_size - 1,
+        1 + micro + 4 * chips,
+        (2, 2),
         flops=2 * every * width * span,
-    )[0]
-
-    input_backs = []
-    gain_one_sum = 0.0
-    bias_one_sum = 0.0
-    head_router_sum = 0.0
-    for m, s in enumerate(micros):
-        normed, inverse = norm_rows(tokens[m].astype(F32))
-        low = (normed * gain_one + bias_one).astype(BF16)
-        seq_gate_back = gate_total[m, SEQ : SEQ + s.own_seq.shape[1]]
-        head_logit_back = (
-            NHC * s.picked_head[:, None] * (s.choice_hot - s.head_share) * seq_gate_back[:, None]
-        )
-        spread = jnp.dot(s.own_seq, head_logit_back / s.divisor[:, None], precision=HIGHEST)
-        back = first_back[m] + jnp.dot(spread, router_head.T, precision=HIGHEST)
-        head_router_sum = head_router_sum + jnp.dot(spread.T, low.astype(F32), precision=HIGHEST)
-        gain_one_sum = gain_one_sum + jnp.sum(back * normed, axis=0)
-        bias_one_sum = bias_one_sum + jnp.sum(back, axis=0)
-        input_backs.append(hidden_back[m] + norm_back(back, normed, inverse, gain_one))
-
-    use = jnp.concatenate([sum(s.width_use for s in micros), sum(s.head_use for s in micros)])
-    use_row = jnp.pad(use[None], ((0, 0), (0, width - NB - NHC)))
-    stats = jnp.concatenate(
-        [stats_two[: 2 + NB], gain_one_sum[None], bias_one_sum[None], head_router_sum, use_row],
-        axis=0,
     )
-    stats = butterfly(butterfly(stats, "tensor", size), "dp", dp_size)
-    after = 4 + NB
     return (
         block_output,
-        jnp.stack(input_backs, axis=0),
-        mix_sum.astype(F32),
-        out_sum.astype(F32),
-        up_sum.astype(F32),
-        down_sum.astype(F32),
-        stats[2 + NB],
-        stats[3 + NB],
+        tokens_gradient,
+        mix_sum,
+        out_sum,
+        up_sum,
+        down_sum,
+        stats[STATS_ONE],
+        stats[STATS_ONE + 1],
         stats[0],
         stats[1],
         stats[2 : 2 + NB].T,
-        stats[after : after + NHC].T,
-        stats[after + NHC, :NB],
-        stats[after + NHC, NB : NB + NHC],
+        stats[STATS_ONE + 2 : STATS_ONE + 2 + NHC].T,
+        stats[STATS_USE, :NB],
+        stats[STATS_USE, CHOICE : CHOICE + NHC],
     )
 
 

time: 586 us -> 565 us (0.964); the launches traced: 577 us -> 564 us
  Pallas kernels: 400 us -> 546 us
  waiting for transfers between devices: 107 us -> 0 us
  other arithmetic: 29.5 us -> 1.26 us
  between operations: 15.2 us -> 0.73 us
  matrix products: 9.24 us -> 0 us
  local copies, waits for them, and re-layouts: 7.65 us -> 16.1 us
  starting transfers between devices: 8.32 us -> 0 us
    pallas_call x6, Pallas kernels: 400 us -> 546 us  [call(): pl.pallas_call(kernel, out_shape=[jax.ShapeDtypeStruct(shape, kind) for s...]
    reduce_scatter x4 -> x0, waiting for transfers between devices: 42.9 us -> none  [share_out(): return lax.psum_scatter(term, 'dp', scatter_dimension=0, tiled=False)]
    all_gather x4 -> x0, waiting for transfers between devices: 38.5 us -> none  [gather_weights(): return lax.all_gather(piece, 'dp', axis=0, tiled=False)]
    ppermute x5 -> x0, waiting for transfers between devices: 22.3 us -> none  [butterfly(): lax.ppermute(value, axis, [(i, i ^ step) for i in range(size)])]
    convert_element_type x14 -> x1, other arithmetic: 11.1 us -> 0.67 us  [local(): params = jnp.concatenate([vectors, width_router.T, head_router.T, jnp.zer...]
    another operation x13 -> x0, other arithmetic: 9.47 us -> none  [the longest x2 3.93 us: local(): jnp.stack(input_backs, axis=0)]
    dot_general x10 -> x0, matrix products: 9.24 us -> none  [the longest x2 3.99 us: dot(): return jnp.dot(left, right, preferred_element_type=F32)]
    ppermute x5 -> x0, starting transfers between devices: 8 us -> none  [butterfly(): lax.ppermute(value, axis, [(i, i ^ step) for i in range(size)])]
  transfers between devices with their start and end apart: 13 -> 0, of which waited for: 8 -> 0; matrix products, arithmetic and copies ran while one was open for 7% -> 0% of each run, Pallas kernels for 69% -> 0%
where the time goes in v3:
time: 565 us; the launch traced here: 564 us
  Pallas kernels  546 us (97%)
  local copies, waits for them, and re-layouts  16.1 us (3%)
    pallas_call x6, Pallas kernels, call(): pl.pallas_call(kernel, out_shape=[jax.ShapeDtypeStruct(shape, kind) for s...  546 us

profile of v3, /device:TPU:0, one launch (start us, length us, event | category | flops | bytes accessed | tf_op | source)
XLA Modules:
  0.0 564.1 jit_solution(7960537811108439905)
XLA Ops:
  0.7 0.6 maximum_bitcast_fusion.rates
  1.2 0.7 stack.12
  1.9 0.7 stack.13
  2.6 0.7 stack.14
  3.3 0.7 stack.15
  4.0 1.5 concatenate.6
  5.6 0.7 convert_element_type.3.params
  6.2 80.0 %shard_map.254 = (bf16[1024,2048]{1,0:T(8,128)(2,1)}, bf16[8,256,1536]{2,1,0:T(8,128)(2,1)}, bf16[8,512,256]{2,1,0:T(8,128)(2,1)}, f32[2,512,512]{2,1,0:T(8,128)...) custom-call(bf16[2,128,2048]{2,1,0:T(8,128)(2,1)} %tokens.7, ...), custom_call_target="tpu_custom_call" | custom-call | bytes 2232896 | tf_op jit(solution)/shard_map/pallas_call | solution.py:1495
  86.2 123.5 %shard_map.255 = (bf16[2,3,512,512]{3,2,1,0:T(8,128)(2,1)}, bf16[1024,512]{1,0:T(8,128)(2,1)}, f32[2,128,2048]{2,1,0:T(8,128)}, bf16[1024,2048]{1,0:T(8,128)(2,1...) custom-call(bf16[1024,2048]{1,0:T(8,128)(2,1)} %get-tuple-element.57, ...), custom_call_target="tpu_custom_call" | custom-call | flops 10737418240 | bytes 20709376 | tf_op jit(solution)/shard_map/pallas_call | solution.py:1495
  209.7 57.4 %shard_map.256 = (bf16[1024,2048]{1,0:T(8,128)(2,1)}, bf16[1024,2048]{1,0:T(8,128)(2,1)}, bf16[1024,2048]{1,0:T(8,128)(2,1)}, bf16[8,1024,256]{2,1,0:T(8,128)(2,...) custom-call(bf16[1024,2048]{1,0:T(8,128)(2,1)} %get-tuple-element.66.second_hbm, ...), custom_call_target="tpu_custom_call" | custom-call | flops 17179869184 | bytes 15204352 | tf_op jit(solution)/shard_map/pallas_call | solution.py:1495
  267.1 103.3 %shard_map.257 = (bf16[2,128,2048]{2,1,0:T(8,128)(2,1)}, bf16[4,256,2048]{2,1,0:T(8,128)(2,1)}, bf16[4,256,2048]{2,1,0:T(8,128)(2,1)}, f32[2,128,2048]{2,1,0:T(8...) custom-call(bf16[8,1024,256]{2,1,0:T(8,128)(2,1)} %get-tuple-element.65.down_, ...), custom_call_target="tpu_custom_call" | custom-call | flops 34359738368 | bytes 46530560 | tf_op jit(solution)/shard_map/pallas_call | solution.py:1495
  370.4 88.9 %shard_map.258 = (bf16[1024,1536]{1,0:T(8,128)(2,1)}, bf16[4,512,256]{2,1,0:T(8,128)(2,1)}, bf16[4,512,256]{2,1,0:T(8,128)(2,1)}, bf16[4,256,1536]{2,1,0:T(8,128...) custom-call(bf16[2,128,2048]{2,1,0:T(8,128)(2,1)} %get-tuple-element.78.back, ...), custom_call_target="tpu_custom_call" | custom-call | flops 16106127360 | bytes 23597056 | tf_op jit(solution)/shard_map/pallas_call | solution.py:1495
  459.3 0.0 copy-start.4
  459.3 93.0 %shard_map.259 = (f32[2,128,2048]{2,1,0:T(8,128)}, f32[256,1536]{1,0:T(8,128)}, f32[512,256]{1,0:T(8,128)}, f32[16,2048]{1,0:T(8,128)}) custom-call(bf16[1024,1536]{1,0:T(8,128)(2,1)} %get-tuple-element.84.mixed_hbm, bf16[2048,1536]{1,0:T(8,128)(2,1)} %bitcast.25, bf16[4,256,1536]{2,1,0:T(8,128)(2,1)} %get-tuple-element.85.mix_mine, ...), custom_call_target="tpu_custom_call" | custom-call | flops 6442450944 | bytes 21315584 | tf_op jit(solution)/shard_map/pallas_call | solution.py:1495
  552.3 0.0 copy-start.2
  552.3 1.4 slice_bitcast_fusion.2
  553.7 1.7 fusion
  555.4 1.5 slice_bitcast_fusion
  556.9 0.0 copy-done.4
  556.9 0.0 copy-start.3
  556.9 1.0 copy.35
  557.9 0.0 copy-done.2
  557.9 0.0 copy-start.5
  557.9 1.3 copy.36
  559.2 0.0 copy-done.3
  559.2 0.0 copy-start.1
  559.2 1.1 copy.37
  560.4 0.0 copy-done.5
  560.4 0.0 copy-start
  560.4 0.8 copy.38
  561.2 0.3 copy-done.1
  561.5 1.3 copy.39
  562.8 0.0 copy-done
  562.8 1.3 copy.40
  (2 shorter events, 0.0 us)
Async XLA Ops:
  459.3 97.7 %copy-start.4 = (bf16[2,128,2048]{2,1,0:T(8,128)(2,1)S(1)}, bf16[2,128,2048]{2,1,0:T(8,128)(2,1)}, u32[]{:S(2)}) copy-start(bf16[2,128,2048]{2,1,0:T(8,128)(2,1)} %get-tuple-element.122) | copy-start | bytes 3145732
  552.3 5.6 copy-start.2
  556.9 2.3 copy-start.3
  557.9 2.5 copy-start.5
  559.2 2.3 copy-start.1
  560.4 2.4 copy-start

commit v4 on v3

--- a/solution.py
+++ b/solution.py
@@ -161,17 +161,17 @@
         self.mine, self.twin, self.target = mine, twin, target
         self.own, self.other, self.landing, self.staged = own, other, landing, staged
         self.tile, self.tile_sems = tile, tile_sems
-        self.hops = []
-        self.rows = tile.shape[1]
+        self.sent = 0
+        self.rows = sum_rows(own.shape[1])
 
     def load(self):
-        block = self.column.chip_at(-1 - len(self.hops))
+        block = self.column.chip_at(-1 - self.sent)
         self.loading = [
             self.loads.copy(self.mine.at[block], self.own),
             self.loads.copy(self.twin.at[block], self.other),
         ]
 
-    def send(self, landed):
+    def send(self, landed, more=True):
         k, rows = self.column, self.rows
 
         def body(i, _):
@@ -183,35 +183,46 @@
             return 0
 
         lax.fori_loop(0, self.own.shape[0] // rows, body, 0)
-        self.hops.append(k.copy(self.staged, self.landing.at[len(self.hops)], k.right))
+        self.hop = k.copy(self.staged, self.landing.at[self.sent], k.right)
+        self.sent += 1
+        if more:
+            self.load()
+
+    def start(self, more=True):
+        wait_all(self.loading)
+        self.send(None, more)
+
+    def prepare(self, landed):
+        self.sent = 1
         self.load()
-
-    def start(self):
-        self.load()
+        self.loading.append(self.loads.copy(landed.at[0], self.landing.at[0]))
+
+    def resume(self):
         wait_all(self.loading)
-        self.send(None)
+        self.send(0)
 
     def advance(self):
-        self.hops[-1].wait()
+        self.hop.wait()
         wait_all(self.loading)
-        self.send(len(self.hops) - 1)
+        self.send(self.sent - 1)
 
     def finish(self):
         k, rows = self.column, self.rows
-        while len(self.hops) < k.chips - 1:
+        while self.sent < k.chips - 1:
             self.advance()
-        self.hops[-1].wait()
+        self.hop.wait()
         wait_all(self.loading)
         landed = k.chips - 2
+        slots = self.tile.shape[0]
 
         def body(i, _):
             here = pl.ds(pl.multiple_of(i * rows, rows), rows)
-            slot = lax.rem(i, 2)
+            slot = lax.rem(i, slots)
             copy = pltpu.make_async_copy(
                 self.tile.at[slot], self.target.at[here], self.tile_sems.at[slot]
             )
 
-            @pl.when(i >= 2)
+            @pl.when(i >= slots)
             def _():
                 copy.wait()
 
@@ -222,11 +233,15 @@
 
         count = self.own.shape[0] // rows
         lax.fori_loop(0, count, body, 0)
-        for i in range(max(count - 2, 0), count):
+        for i in range(max(count - slots, 0), count):
             here = pl.ds(i * rows, rows)
+            slot = i % slots
             pltpu.make_async_copy(
-                self.tile.at[i % 2], self.target.at[here], self.tile_sems.at[i % 2]
+                self.tile.at[slot], self.target.at[here], self.tile_sems.at[slot]
             ).wait()
+
+
+SUM_TILES = 4
 
 
 def sum_rows(width):
@@ -239,7 +254,7 @@
         ((rows, width), BF16),
         ((chips - 1, rows, width), BF16),
         ((rows, width), BF16),
-        ((2, sum_rows(width), width), F32),
+        ((SUM_TILES, sum_rows(width), width), F32),
     ]
 
 
@@ -437,42 +452,48 @@
     all_landed(column, twin, sems, twin_sem)
 
 
-def blocks_out(column, make, tile, mine, twin, sems, twin_sem):
-    def outs(i):
-        local = pltpu.make_async_copy(tile.at[0], mine.at[i], sems.at[0])
-        away = pltpu.make_async_remote_copy(
+def blocks_out(column, make, tile, mine, twin, sems, twin_sems, ring):
+    def local_copy(i):
+        chip = column.chip_at(-1 - i)
+        return pltpu.make_async_copy(tile.at[0], mine.at[chip], sems.at[0])
+
+    def away_copy(i):
+        return pltpu.make_async_remote_copy(
             src_ref=tile.at[1],
-            dst_ref=twin.at[i],
+            dst_ref=twin.at[column.chip_at(-1 - i)],
             send_sem=sems.at[1],
-            recv_sem=twin_sem.at[0],
+            recv_sem=twin_sems.at[i],
             device_id={"dp": column.twin},
             device_id_type=MESH,
         )
-        return local, away
 
     def body(i, _):
-        local, away = outs(i)
+        chip, local, away = column.chip_at(-1 - i), local_copy(i), away_copy(i)
 
         @pl.when(i > 0)
         def _():
             away.wait_send()
 
-        make(2 * i + 1 - column.core, tile.at[1])
+        make(2 * chip + 1 - column.core, tile.at[1])
         away.start()
 
-        @pl.when(i > 0)
+        @pl.when(i > 1)
         def _():
             local.wait()
 
-        make(2 * i + column.core, tile.at[0])
+        make(2 * chip + column.core, tile.at[0])
         local.start()
         return 0
 
-    lax.fori_loop(0, column.chips, body, 0)
-    local, away = outs(column.chips - 1)
-    local.wait()
-    away.wait_send()
-    all_landed(column, twin, sems, twin_sem)
+    lax.fori_loop(0, 1, body, 0)
+    local_copy(0).wait()
+    away_copy(0).wait_recv()
+    ring()
+    lax.fori_loop(1, column.chips, body, 0)
+    for i in range(1, column.chips):
+        away_copy(i).wait_recv()
+    local_copy(column.chips - 1).wait()
+    away_copy(column.chips - 1).wait_send()
 
 
 def all_landed(column, twin, sems, twin_sem):
@@ -547,8 +568,8 @@
     total = rows * size
     greet(*links.peers, *column.ring, *column.pair)
     rings = [
+        WeightRing(column, loads, merger, lambda i: out_out.at[i]),
         WeightRing(column, loads, mixer, lambda i: mix_out.at[i]),
-        WeightRing(column, loads, merger, lambda i: out_out.at[i]),
     ]
     for ring in rings:
         ring.start()
@@ -628,10 +649,13 @@
             return 0
 
         lax.fori_loop(0, total // chunk, table, 0)
+        if m == 0:
+            rings[0].advance()
     for g in gathers:
         g.middle()
-    for ring in rings:
-        ring.advance()
+    rings[1].advance()
+    if column.chips > 2:
+        rings[0].advance()
     outs = []
     usage[...] = jnp.zeros_like(usage)
     few = lax.broadcasted_iota(jnp.int32, (8, LANES), 1)
@@ -671,8 +695,8 @@
             value = jnp.where(lane_own == LIVE, live, value)
             own[m, pl.ds(where * half, half), :] = value
             usage[0:1, :] += jnp.sum(value * live, axis=0, keepdims=True)
-    for step in range(column.chips - 2):
-        for ring in rings:
+    for step in range(column.chips - 3):
+        for ring in reversed(rings):
             ring.advance()
     for ring in rings:
         ring.finish()
@@ -732,10 +756,10 @@
     mask_copy = loads.copy(mask_hbm, mask)
     out_copies = columns_in(loads, out_hbm, out)
     greet(*links.peers, *column.ring, *column.pair)
-    early = shrink.shape[0] // 2
+    early = shrink.shape[0] // 4
     rings = [
+        WeightRing(column, loads, shrink.at[pl.ds(0, early)], lambda i: down_out.at[i]),
         WeightRing(column, loads, expand, lambda i: up_out.at[i]),
-        WeightRing(column, loads, shrink.at[pl.ds(0, early)], lambda i: down_out.at[i]),
     ]
     for ring in rings:
         ring.start()
@@ -838,28 +862,27 @@
     for m in range(micro):
         row_copies[m].wait()
         project(m)
-        if m > 0:
-            scatters[m - 1].middle()
-            for ring in rings:
-                ring.advance()
         if m == 0:
             mask_copy.wait()
         attend(m)
         if m == 0:
             wait_all(out_copies)
+            rings[0].advance()
+        else:
+            scatters[m - 1].middle()
         merge(m)
         scatters[m].start()
+    rings[1].advance()
     for m in range(micro):
-        if m == micro - 1:
-            scatters[m].middle()
         scatters[m].finish()
         second_norm(m)
         gathers[m].start()
-        if m > 0:
-            gathers[m - 1].middle()
-        if m == 0:
-            for ring in rings:
-                ring.advance()
+        if m + 1 < micro:
+            scatters[m + 1].middle()
+            gathers[m].middle()
+            if column.chips > 2:
+                for ring in rings:
+                    ring.advance()
     saves.append(loads.copy(qkv, qkv_out))
     saves.append(loads.copy(head_rows, heads_out))
     gathers[micro - 1].middle()
@@ -920,8 +943,9 @@
                 )
             )
     greet(*links.peers, *column.ring, *column.pair)
-    late = shrink.shape[0] // 2
-    ring = WeightRing(column, loads, shrink.at[pl.ds(late, late)], lambda i: down_out.at[i])
+    late = down_out.shape[1]
+    rest = shrink.at[pl.ds(shrink.shape[0] - late, late)]
+    ring = WeightRing(column, loads, rest, lambda i: down_out.at[i])
     ring.start()
     wait_all(own_copies)
     gathers = [Gather(links, branch_buf, m * total) for m in range(micro)]
@@ -943,15 +967,16 @@
 
         lax.fori_loop(0, units // step, body, 0)
         gathers[m].middle()
-        if m < column.chips - 1:
-            ring.advance()
         here = pl.ds(m * total, total)
         saves.append(loads.copy(rect.at[here], rect_out.at[here]))
         saves.append(loads.copy(active.at[here], active_out.at[here]))
+    ring.advance()
     for m, g in enumerate(gathers):
         g.finish()
         here = pl.ds(m * total, total)
         saves.append(loads.copy(branch_buf.at[here], branch_out.at[here]))
+        if m == 0 and column.chips > 2:
+            ring.advance()
     block, wide = mine_out.shape[2], tile.shape[3]
 
     def make(c, put):
@@ -990,6 +1015,7 @@
     stats_out,
     gate_out,
     sum_out,
+    landed_out,
     down,
     up,
     active,
@@ -1034,9 +1060,10 @@
         sum_tile,
         sum_sems,
     )
+    ring.load()
     early = down_early.shape[1]
     down_copies = columns_in(loads, down_early, down.at[pl.ds(0, early)])
-    down_copies += columns_in(loads, down_late, down.at[pl.ds(early, early)])
+    down_copies += columns_in(loads, down_late, down.at[pl.ds(early, units - early)])
     active_copies = [loads.copy(active_hbm.at[h], active.at[h]) for h in here]
     branch_copies = [loads.copy(branch_hbm.at[h], shared_rows.at[h]) for h in here]
     rect_copy = loads.copy(rect_hbm.at[here[0]], rect)
@@ -1153,24 +1180,40 @@
 
         over_rows(half, body)
 
+    wait_all(second_copies)
+    block = mine_out.shape[1]
+
+    def make(c, ref):
+        ref[...] = dot_tn(
+            shared_rows[:, pl.ds(pl.multiple_of(c * block, block), block)], active[...]
+        ).astype(BF16)
+
+    early, other, staged_up = [up.at[pl.ds(i * block, block)] for i in range(3)]
+    up_ring = SumRing(
+        column, loads, mine_out, twin_out, None, early, other, landed_out, staged_up, None, None
+    )
+
+    def start_up():
+        up_ring.load()
+        up_ring.start(more=False)
+
+    blocks_out(column, make, tile, mine_out, twin_out, tile_sems, twin_sem, start_up)
     if column.chips > 3:
         ring.advance()
     for m in range(micro):
         finish_out(m)
-    wait_all(second_copies)
-    block = mine_out.shape[1]
-
-    def make(c, ref):
-        ref[...] = dot_tn(
-            shared_rows[:, pl.ds(pl.multiple_of(c * block, block), block)], active[...]
-        ).astype(BF16)
-
-    blocks_out(column, make, tile, mine_out, twin_out, tile_sems, twin_sem)
     for m in range(micro):
         backs[m].middle()
-    ring.finish()
     for m in range(micro):
         finish_back(m)
+    ring.finish()
+    up_ring.hop.wait()
+
+
+STATS_ONE = 6
+STATS_USE = 12
+STATS_ROWS = 16
+SEQ_COUNT = 4
 
 
 def attend_back_kernel(
@@ -1184,18 +1227,29 @@
     heads_hbm,
     rows_hbm,
     mask_hbm,
+    mix_hbm,
     cosine,
     sine,
     row_info,
     mine_hbm,
     twin_hbm,
-    mixed_out,
+    landed_hbm,
+    tokens,
+    hidden_back,
+    own,
+    seq_info,
+    params,
+    stats_two,
+    usage,
+    back_out,
+    up_sum,
+    mix_sum,
+    out_sum,
+    stats_out,
+    mix_mine,
+    mix_twin,
     out_mine,
     out_twin,
-    mix_mine,
-    mix_twin,
-    gate_out,
-    sum_out,
     buf,
     out,
     qkv,
@@ -1209,38 +1263,25 @@
     out_tile,
     mix_tile,
     gates,
-    sum_own,
-    sum_other,
-    sum_landing,
-    sum_staged,
-    sum_tile,
-    send,
-    recv,
-    load_sems,
-    out_sems,
-    out_twin_sem,
-    mix_sems,
-    mix_twin_sem,
-    sum_sems,
+    mix,
+    landing,
+    staged,
+    last,
+    *rest,
 ):
+    up_bufs, mix_bufs, out_bufs = rest[:5], rest[5:10], rest[10:15]
+    stats, share, pieces, sums, whole = rest[15:20]
+    send, recv, load_sems = rest[20:23]
+    out_sems, out_twin_sem, mix_sems, mix_twin_sem, up_sum_sems, mix_sum_sems, out_sum_sems = rest[23:]
     micro, rows, width = back.shape
     total = rows * size
     copies, loads = Copies(send, recv), Loads(load_sems)
     links, column = Links(size, rows, copies), Column(dp_size, copies)
     half = links.half
-    ring = SumRing(
-        column,
-        loads,
-        mine_hbm,
-        twin_hbm,
-        sum_out,
-        sum_own,
-        sum_other,
-        sum_landing,
-        sum_staged,
-        sum_tile,
-        sum_sems,
-    )
+    ring = SumRing(column, loads, mine_hbm, twin_hbm, up_sum, *up_bufs, up_sum_sems)
+    mix_ring = SumRing(column, loads, mix_mine, mix_twin, mix_sum, *mix_bufs, mix_sum_sems)
+    out_ring = SumRing(column, loads, out_mine, out_twin, out_sum, *out_bufs, out_sum_sems)
+    ring.prepare(landed_hbm)
     own_copies = []
     for m in range(micro):
         for where in range(2):
@@ -1255,26 +1296,35 @@
     mask_copy = loads.copy(mask_hbm, mask)
     heads_copy = loads.copy(heads_hbm, head_rows)
     rows_copy = loads.copy(rows_hbm, rows_buf)
+    mix_copy = loads.copy(mix_hbm, mix)
     gates[links.me] = gate[...]
-    others = [lax.rem(links.me + s, size) for s in range(1, size)]
-    greet(*[("tensor", to) for to in others], *column.ring, *column.pair)
+    near = [lax.rem(links.me + s, size) for s in range(1, size)]
+    far = [lax.rem(column.me + s, dp_size) for s in range(1, dp_size)]
+    greet(*[("tensor", to) for to in near], *[("dp", to) for to in far])
     wait_all(own_copies)
     gathers = [Gather(links, buf, m * total) for m in range(micro)]
-    for g in gathers:
-        g.start()
-    ring.start()
-    gate_copies = [links.copy(gate, gates.at[links.me], peer) for peer in others]
+    gathers[0].start()
+    ring.resume()
+    gate_copies = [links.copy(gate, gates.at[links.me], peer) for peer in near]
+    stats[...] = jnp.zeros_like(stats)
+    stats[0:8, :] = stats_two[...]
+    stats[STATS_USE : STATS_USE + 1, 0:LANES] = usage[0:1, :]
     wait_all(out_copies)
     qkv_copy.wait()
     mask_copy.wait()
     scale = HD ** (-0.5)
     chunk = min(128, total)
-    for g in gathers:
-        g.middle()
-    for m in range(micro):
-        gathers[m].finish()
-        if m + 2 < column.chips:
-            ring.advance()
+    gathers[0].middle()
+    for g in gathers[1:]:
+        g.start()
+    block, wide = out_mine.shape[2], out_tile.shape[3]
+    here_rows = [pl.ds(m * total, total) for m in range(micro)]
+    scatters = [
+        Scatter(links, buf, m * total, landing.at[m], staged.at[m], last.at[m], back_out.at[m])
+        for m in range(micro)
+    ]
+
+    def heads_part(m):
         base = m * total
         every = pl.ds(base, total)
         value = dot_nt(buf[every, :], out[...])
@@ -1307,133 +1357,89 @@
             mixed_back[every, pl.ds(col, HD)] = turned(query_back, cos, sin).astype(BF16)
             mixed_back[every, pl.ds(col + HD, HD)] = turned(keys_back, cos, sin).astype(BF16)
             mixed_back[every, pl.ds(col + 2 * HD, HD)] = values_back.astype(BF16)
-    mixed_save = loads.copy(mixed_back, mixed_out)
-    heads_copy.wait()
-    block, wide = out_mine.shape[2], out_tile.shape[3]
+            if m == 0 and h == 0:
+                for g in gathers[1:]:
+                    g.middle()
+                if column.chips > 3:
+                    ring.advance()
 
     def make_out(c, put):
         value = dot_tn(head_rows[:, pl.ds(pl.multiple_of(c * wide, wide), wide)], buf[...])
         for j in range(dp_size):
             put(j, value[:, j * block : (j + 1) * block].astype(BF16))
 
-    halves_out(
-        column, heads * HD // wide, make_out, out_tile, out_mine, out_twin, out_sems, out_twin_sem
-    )
-    rows_copy.wait()
-
     def make_mix(c, ref):
         ref[...] = dot_tn(
             rows_buf[:, pl.ds(pl.multiple_of(c * block, block), block)], mixed_back[...]
         ).astype(BF16)
 
-    blocks_out(column, make_mix, mix_tile, mix_mine, mix_twin, mix_sems, mix_twin_sem)
-    ring.finish()
+    tile = min(512, width)
+
+    def first_part(m):
+        def body(j, _):
+            cols = pl.ds(pl.multiple_of(j * tile, tile), tile)
+            buf[here_rows[m], cols] = dot_nt(mixed_back[here_rows[m], :], mix[cols, :]).astype(BF16)
+            return 0
+
+        lax.fori_loop(0, width // tile, body, 0)
+        scatters[m].start()
+
+    gathers[0].finish()
+    heads_part(0)
+    for g in gathers[1:]:
+        g.finish()
+    heads_copy.wait()
+    halves_out(
+        column,
+        heads * HD // wide,
+        make_out,
+        out_tile,
+        out_mine,
+        out_twin,
+        out_sems,
+        out_twin_sem,
+    )
+    out_ring.load()
+    out_ring.start()
+    mix_copy.wait()
+    first_part(0)
+    for m in range(1, micro):
+        heads_part(m)
+    scatters[0].middle()
+    if column.chips > 2:
+        out_ring.advance()
+    rows_copy.wait()
+
+    def start_mix():
+        mix_ring.load()
+        mix_ring.start(more=False)
+
+    blocks_out(column, make_mix, mix_tile, mix_mine, mix_twin, mix_sems, mix_twin_sem, start_mix)
+    mix_ring.load()
+    if column.chips > 3:
+        out_ring.advance()
+    for m in range(1, micro):
+        first_part(m)
     for made in gate_copies:
         made.wait()
     gate_sum = gates[0]
     for r in range(1, size):
         gate_sum = gate_sum + gates[r]
-    gate_out[...] = gate_sum
-    mixed_save.wait()
-
-
-STATS_ONE = 6
-STATS_USE = 12
-STATS_ROWS = 16
-SEQ_COUNT = 4
-
-
-def first_back_kernel(
-    dp_size,
-    size,
-    micro,
-    mixed_hbm,
-    mix_hbm,
-    mix_mine,
-    mix_twin,
-    out_mine,
-    out_twin,
-    tokens,
-    hidden_back,
-    own,
-    seq_info,
-    gates,
-    params,
-    stats_two,
-    usage,
-    back_out,
-    mix_sum,
-    out_sum,
-    stats_out,
-    mixed_back,
-    mix,
-    part,
-    landing,
-    staged,
-    last,
-    *rest,
-):
-    mix_bufs, out_bufs = rest[:5], rest[5:10]
-    stats, share, pieces, sums, whole = rest[10:15]
-    send, recv, load_sems, mix_sems, out_sems = rest[15:]
-    total = mixed_back.shape[0] // micro
-    rows = total // size
-    width = mix.shape[0]
-    copies, loads = Copies(send, recv), Loads(load_sems)
-    links, column = Links(size, rows, copies), Column(dp_size, copies)
-    here = [pl.ds(m * total, total) for m in range(micro)]
-    rings = [
-        SumRing(column, loads, mix_mine, mix_twin, mix_sum, *mix_bufs, mix_sems),
-        SumRing(column, loads, out_mine, out_twin, out_sum, *out_bufs, out_sems),
-    ]
-    mix_copy = loads.copy(mix_hbm, mix)
-    mixed_copies = [loads.copy(mixed_hbm.at[h], mixed_back.at[h]) for h in here]
-    near = [lax.rem(links.me + s, size) for s in range(1, size)]
-    far = [lax.rem(column.me + s, dp_size) for s in range(1, dp_size)]
-    greet(*[("tensor", to) for to in near], *[("dp", to) for to in far])
-    for ring in rings:
-        ring.start()
-    stats[...] = jnp.zeros_like(stats)
-    stats[0:8, :] = stats_two[...]
-    stats[STATS_USE : STATS_USE + 1, 0:LANES] = usage[0:1, :]
-    scatters = [
-        Scatter(links, part, m * total, landing.at[m], staged.at[m], last.at[m], back_out.at[m])
-        for m in range(micro)
-    ]
-    mix_copy.wait()
-    tile = min(512, width)
-    for m in range(micro):
-        mixed_copies[m].wait()
-
-        def body(j, _, m=m):
-            cols = pl.ds(pl.multiple_of(j * tile, tile), tile)
-            part[here[m], cols] = dot_nt(mixed_back[here[m], :], mix[cols, :]).astype(BF16)
-            return 0
-
-        lax.fori_loop(0, width // tile, body, 0)
-        scatters[m].start()
-    if column.chips > 2:
-        for ring in rings:
-            ring.advance()
-    for s in scatters:
-        s.middle()
-    if column.chips > 3:
-        for ring in rings:
-            ring.advance()
-    for m, s in enumerate(scatters):
+
+    def last_rows(m):
+        s = scatters[m]
         s.finish()
-
         count = SEQ_COUNT
         lane = lax.broadcasted_iota(jnp.int32, (8, LANES), 1)
         which = lax.broadcasted_iota(jnp.int32, (8, LANES), 0)
         info = seq_info[m]
-        gate_back = jnp.where(lane == SEQ + which, gates[m : m + 1, :], 0.0)
+        gate_back = jnp.where(lane == SEQ + which, gate_sum[m : m + 1, :], 0.0)
         gate_back = jnp.sum(gate_back, axis=-1, keepdims=True)
         chosen = jnp.where(lane == info[:, CHOSEN : CHOSEN + 1].astype(jnp.int32), 1.0, 0.0)
         logit_back = NHC * info[:, PICKED : PICKED + 1] * (chosen - info) * gate_back
         logit_back = logit_back / info[:, DIVISOR : DIVISOR + 1]
 
-        def body(where, i, row, m=m, s=s, logit_back=logit_back):
+        def body(where, i, row):
             back = s.chunk(where, i)
             normed, inverse = normalized(tokens[m, at(row), :].astype(F32))
             gain = params[ATTEND : ATTEND + 1, :]
@@ -1443,10 +1449,10 @@
             for q in range(count):
                 spread = spread + rows_info[:, SEQ + q : SEQ + q + 1] * logit_back[q : q + 1, :]
             for c in range(NHC):
-                column = spread[:, c : c + 1]
-                back = back + column * params[HEAD_ROUTER + c : HEAD_ROUTER + c + 1, :]
+                part = spread[:, c : c + 1]
+                back = back + part * params[HEAD_ROUTER + c : HEAD_ROUTER + c + 1, :]
                 at_row = STATS_ONE + 2 + c
-                stats[at_row : at_row + 1, :] += jnp.sum(column * low, axis=0, keepdims=True)
+                stats[at_row : at_row + 1, :] += jnp.sum(part * low, axis=0, keepdims=True)
             at_row = STATS_ONE
             stats[at_row : at_row + 1, :] += jnp.sum(back * normed, axis=0, keepdims=True)
             stats[at_row + 1 : at_row + 2, :] += jnp.sum(back, axis=0, keepdims=True)
@@ -1454,6 +1460,15 @@
             back_out[m, at(row), :] = hidden_back[m, at(row), :] + value
 
         over_rows(links.half, body)
+
+    last_rows(0)
+    if column.chips > 2:
+        mix_ring.advance()
+    for s in scatters[1:]:
+        s.middle()
+    ring.finish()
+    for m in range(1, micro):
+        last_rows(m)
 
     piece = width // size
     mine = pl.ds(pl.multiple_of(links.me * piece, piece), piece)
@@ -1470,7 +1485,11 @@
         value = value + pieces[r]
     share[0] = value
     sums[column.me] = value
-    wait_all([column.copy(share.at[0], sums.at[column.me], to) for to in far])
+    sent = [column.copy(share.at[0], sums.at[column.me], to) for to in far]
+    if column.chips > 3:
+        mix_ring.advance()
+    out_ring.finish()
+    wait_all(sent)
     value = sums[0]
     for r in range(1, dp_size):
         value = value + sums[r]
@@ -1479,8 +1498,7 @@
     wait_all([links.copy(share.at[1], whole.at[links.me], to) for to in near])
     for r in range(size):
         stats_out[:, r * piece : (r + 1) * piece] = whole[r]
-    for ring in rings:
-        ring.finish()
+    mix_ring.finish()
 
 
 ANY = pl.BlockSpec(memory_space=pl.ANY)
@@ -1536,9 +1554,9 @@
     few = transfers(size)
     ringed = ring_copies(dp_size)
 
-    vectors = jnp.stack([attend_gain, attend_bias, feed_gain, feed_bias])
+    vectors = jnp.concatenate([attend_gain, attend_bias, feed_gain, feed_bias]).reshape(4, width)
     params = jnp.concatenate(
-        [vectors, width_router.T, head_router.T, jnp.zeros((4, width), BF16)], axis=0
+        [vectors, jnp.concatenate([width_router, head_router], axis=1).T], axis=0
     ).astype(F32)
     rates = jnp.power(10000.0, -2.0 * jnp.arange(HD // 2, dtype=F32) / HD)
     rates = jnp.concatenate([rates, rates])[None]
@@ -1611,7 +1629,7 @@
             ((micro, rows, LANES), F32, True),
             ((micro, rows, width), BF16, True),
             ((dp_size,) + expand.shape, BF16, False),
-            ((dp_size, units // 2, block), BF16, False),
+            ((dp_size, units // 4, block), BF16, False),
         ],
         [
             ((every, width), BF16),
@@ -1645,7 +1663,7 @@
             ((every, units), BF16, False),
             ((every, units), BF16, False),
             ((every, width), BF16, False),
-            ((dp_size, units // 2, block), BF16, False),
+            ((dp_size, units - units // 4, block), BF16, False),
             ((chips, units, block), BF16, False),
             ((chips, units, block), BF16, False),
         ],
@@ -1663,7 +1681,7 @@
         flops=4 * every * width * units,
     )
 
-    block_output, up_mine, up_twin, hidden_back, back_own, stats_two, gate_part, down_sum = call(
+    narrowed = call(
         functools.partial(narrow_kernel, dp_size, size),
         4,
         [
@@ -1692,6 +1710,7 @@
             ((8, width), F32, True),
             ((8, LANES), F32, True),
             ((units, block), F32, False),
+            ((1, block, units), BF16, False),
         ],
         [
             ((units, width), BF16),
@@ -1708,15 +1727,17 @@
             ((2, block, units), BF16),
         ]
         + sum_scratch(chips, units, block),
-        2 * micro * few + chips - 1,
-        2 * dp_size + 4 * micro + 1 + 2 * chips,
-        (2, 1, 2),
+        2 * micro * few + chips,
+        2 * dp_size + 4 * micro + 1 + 2 * chips + 2,
+        (2, chips, SUM_TILES),
         flops=8 * every * width * units,
         limit=63,
     )
+    block_output, up_mine, up_twin, hidden_back, back_own, stats_two, gate_part = narrowed[:7]
+    down_sum, up_landed = narrowed[7:]
 
     out_tile = min(256, wide_heads)
-    mixed_back, out_mine, out_twin, mix_mine, mix_twin, gate_total, up_sum = call(
+    lasts = call(
         functools.partial(attend_back_kernel, dp_size, size, heads),
         5,
         [
@@ -1727,20 +1748,31 @@
             (head_rows, False),
             (first_rows, False),
             (mask, False),
+            (mix_weight, False),
             (cosine, True),
             (sine, True),
             (row_info, True),
             (up_mine, False),
             (up_twin, False),
+            (up_landed, False),
+            (tokens, True),
+            (hidden_back, True),
+            (own, True),
+            (seq_info, True),
+            (params, True),
+            (stats_two, True),
+            (usage, True),
         ],
         [
-            ((every, span), BF16, False),
+            ((micro, rows, width), F32, True),
+            ((block, units), F32, False),
+            ((block, span), F32, False),
+            ((wide_heads, block), F32, False),
+            ((STATS_ROWS, width), F32, True),
+            ((chips, block, span), BF16, False),
+            ((chips, block, span), BF16, False),
             ((chips, wide_heads, block), BF16, False),
             ((chips, wide_heads, block), BF16, False),
-            ((chips, block, span), BF16, False),
-            ((chips, block, span), BF16, False),
-            ((8, LANES), F32, True),
-            ((block, units), F32, False),
         ],
         [
             ((every, width), BF16),
@@ -1756,41 +1788,10 @@
             ((2, 2, chips, out_tile, block), BF16),
             ((2, block, span), BF16),
             ((size, 8, LANES), F32),
+            ((width, span), BF16),
         ]
-        + sum_scratch(chips, block, units),
-        micro * few + size - 1 + chips - 1,
-        2 * micro + dp_size + 5 + 2 * chips,
-        (4, 1, 2, 1, 2),
-        flops=2 * every * width * (2 * wide_heads + span) + 20 * heads * micro * total * total * HD,
-    )
-
-    tokens_gradient, mix_sum, out_sum, stats = call(
-        functools.partial(first_back_kernel, dp_size, size, micro),
-        6,
-        [
-            (mixed_back, False),
-            (mix_weight, False),
-            (mix_mine, False),
-            (mix_twin, False),
-            (out_mine, False),
-            (out_twin, False),
-            (tokens, True),
-            (hidden_back, True),
-            (own, True),
-            (seq_info, True),
-            (gate_total, True),
-            (params, True),
-            (stats_two, True),
-            (usage, True),
-        ],
-        [
-            ((micro, rows, width), F32, True),
-            ((block, span), F32, False),
-            ((wide_heads, block), F32, False),
-            ((STATS_ROWS, width), F32, True),
-        ],
-        [((every, span), BF16), ((width, span), BF16), ((every, width), BF16)]
         + buffers
+        + sum_scratch(chips, block, units)
         + sum_scratch(chips, block, span)
         + sum_scratch(chips, wide_heads, block)
         + [
@@ -1800,11 +1801,13 @@
             ((dp_size, STATS_ROWS, width // size), F32),
             ((size, STATS_ROWS, width // size), F32),
         ],
-        micro * few + 2 * (chips - 1) + 2 * (size - 1) + dp_size - 1,
-        1 + micro + 4 * chips,
-        (2, 2),
-        flops=2 * every * width * span,
+        2 * micro * few + 3 * (size - 1) + dp_size - 1 + 3 * (chips - 1),
+        2 * micro + dp_size + 6 + 6 * chips,
+        (4, 1, 2, chips, SUM_TILES, SUM_TILES, SUM_TILES),
+        flops=4 * every * width * (wide_heads + span) + 20 * heads * micro * total * total * HD,
+        limit=63,
     )
+    tokens_gradient, up_sum, mix_sum, out_sum, stats = lasts[:5]
     return (
         block_output,
         tokens_gradient,

time: 565 us -> 514 us (0.910)
  the two profiles are of different devices: /device:TPU:0 before, /device:TPU:1 now
where the time goes in v4:
time: 514 us; the launch traced here: 506 us
  Pallas kernels  489 us (95%)
  local copies, waits for them, and re-layouts  13.2 us (3%)
    pallas_call x5, Pallas kernels, call(): pl.pallas_call(kernel, out_shape=[jax.ShapeDtypeStruct(shape, kind) for s...  489 us

profile of v4, /device:TPU:1, one launch (start us, length us, event | category | flops | bytes accessed | tf_op | source)
XLA Modules:
  0.0 505.7 jit_solution(9110052504944813889)
XLA Ops:
  0.7 0.6 maximum_bitcast_fusion.1.rates
  1.2 0.8 pad_maximum_fusion
  2.0 0.8 maximum_bitcast_fusion
  2.8 0.7 maximum_convert_fusion.params
  3.5 80.7 %shard_map.254 = (bf16[1024,2048]{1,0:T(8,128)(2,1)}, bf16[8,256,1536]{2,1,0:T(8,128)(2,1)}, bf16[8,512,256]{2,1,0:T(8,128)(2,1)}, f32[2,512,512]{2,1,0:T(8,128)...) custom-call(bf16[2,128,2048]{2,1,0:T(8,128)(2,1)} %tokens.7, ...), custom_call_target="tpu_custom_call" | custom-call | bytes 2200128 | tf_op jit(solution)/shard_map/pallas_call | solution.py:1513
  84.1 98.9 %shard_map.255 = (bf16[2,3,512,512]{3,2,1,0:T(8,128)(2,1)}, bf16[1024,512]{1,0:T(8,128)(2,1)}, f32[2,128,2048]{2,1,0:T(8,128)}, bf16[1024,2048]{1,0:T(8,128)(2,1...) custom-call(bf16[1024,2048]{1,0:T(8,128)(2,1)} %get-tuple-element.52, ...), custom_call_target="tpu_custom_call" | custom-call | flops 10737418240 | bytes 20676608 | tf_op jit(solution)/shard_map/pallas_call | solution.py:1513
  183.1 59.4 %shard_map.256 = (bf16[1024,2048]{1,0:T(8,128)(2,1)}, bf16[1024,2048]{1,0:T(8,128)(2,1)}, bf16[1024,2048]{1,0:T(8,128)(2,1)}, bf16[8,1536,256]{2,1,0:T(8,128)(2,...) custom-call(bf16[1024,2048]{1,0:T(8,128)(2,1)} %get-tuple-element.61.second_hbm, ...), custom_call_target="tpu_custom_call" | custom-call | flops 17179869184 | bytes 15204352 | tf_op jit(solution)/shard_map/pallas_call | solution.py:1513
  242.5 105.4 %shard_map.257 = (bf16[2,128,2048]{2,1,0:T(8,128)(2,1)}, bf16[4,256,2048]{2,1,0:T(8,128)(2,1)}, bf16[4,256,2048]{2,1,0:T(8,128)(2,1)}, f32[2,128,2048]{2,1,0:T(8...) custom-call(bf16[8,512,256]{2,1,0:T(8,128)(2,1)} %get-tuple-element., ...), custom_call_target="tpu_custom_call" | custom-call | flops 34359738368 | bytes 46497792 | tf_op jit(solution)/shard_map/pallas_call | solution.py:1513
  347.9 144.1 %shard_map.258 = (f32[2,128,2048]{2,1,0:T(8,128)}, f32[256,2048]{1,0:T(8,128)}, f32[256,1536]{1,0:T(8,128)}, f32[512,256]{1,0:T(8,128)}, f32[16,2048]{1,0:T(8,12...) custom-call(bf16[2,128,2048]{2,1,0:T(8,128)(2,1)} %get-tuple-element, ...), custom_call_target="tpu_custom_call" | custom-call | flops 22548578304 | bytes 34390016 | tf_op jit(solution)/shard_map/pallas_call | solution.py:1513
  492.0 0.0 copy-start.2
  492.1 1.4 slice_bitcast_fusion.2
  493.5 1.6 fusion
  495.1 1.5 slice_bitcast_fusion
  496.6 0.0 copy-start.3
  496.6 2.4 copy.35
  499.0 0.0 copy-done.2
  499.0 0.0 copy-start.4
  499.0 1.3 copy.36
  500.4 0.0 copy-done.3
  500.4 0.0 copy-start.1
  500.4 1.1 copy.37
  501.5 0.0 copy-done.4
  501.5 0.0 copy-start
  501.5 0.8 copy.38
  502.3 0.3 copy-done.1
  502.6 1.3 copy.39
  503.9 0.0 copy-done
  503.9 1.3 copy.40
  (2 shorter events, 0.0 us)
Async XLA Ops:
  492.0 7.0 %copy-start.2 = (f32[2,128,2048]{2,1,0:T(8,128)S(1)}, f32[2,128,2048]{2,1,0:T(8,128)}, u32[]{:S(2)}) copy-start(f32[2,128,2048]{2,1,0:T(8,128)} %get-tuple-element.113) | copy-start | bytes 6291460
  496.6 3.8 copy-start.3
  499.0 2.5 copy-start.4
  500.4 2.2 copy-start.1
  501.5 2.4 copy-start

commit v5 on v4

--- a/solution.py
+++ b/solution.py
@@ -141,9 +141,12 @@
             self.hops.append(k.copy(here, here, k.right))
         self.twins.append(k.copy(here, here, k.twin))
 
-    def finish(self):
+    def advance_all(self):
         while len(self.twins) < self.column.chips:
             self.advance()
+
+    def finish(self):
+        self.advance_all()
         for made in self.twins:
             made.wait()
         for made in self.hops:
@@ -411,7 +414,7 @@
     return [loads.copy(blocks.at[j], flat.at[:, pl.ds(j * width, width)]) for j in range(count)]
 
 
-def halves_out(column, count, make, tile, mine, twin, sems, twin_sem):
+def halves_out(column, count, make, tile, mine, twin, sems, twin_sem, between=None):
     wide = tile.shape[3]
 
     def outs(c, slot):
@@ -444,7 +447,10 @@
         away.start()
         return 0
 
-    lax.fori_loop(0, count, body, 0)
+    lax.fori_loop(0, count // 2, body, 0)
+    if between is not None:
+        between()
+    lax.fori_loop(count // 2, count, body, 0)
     for c in range(max(count - 2, 0), count):
         local, away = outs(c, c % 2)
         local.wait()
@@ -530,12 +536,13 @@
     return value * cosine + pltpu.roll(value, HD // 2, 1) * sine
 
 
-def first_norm_kernel(
+def attend_kernel(
     dp_size,
     size,
     heads,
     units,
     tokens,
+    cotangent,
     params,
     rates,
     bucket,
@@ -543,6 +550,8 @@
     choices,
     mixer,
     merger,
+    expand,
+    shrink,
     rows_out,
     mix_out,
     out_out,
@@ -553,40 +562,72 @@
     own,
     seq_info,
     usage,
-    buf,
+    qkv_out,
+    heads_out,
+    attention_out,
+    second_out,
+    share_out,
+    up_out,
+    down_out,
+    rect_out,
+    active_out,
+    branch_out,
+    mine_out,
+    twin_out,
+    rows_buf,
     slot_col,
     member_col,
     bucket_col,
+    mix,
+    out,
+    qkv,
+    head_rows,
+    part,
+    landing,
+    staged,
+    last,
+    second_buf,
+    up,
+    branch_buf,
+    tile_out,
     send,
     recv,
     load_sems,
+    tile_sems,
+    twin_sem,
 ):
-    micro, rows, _ = tokens.shape
+    micro, rows, width = tokens.shape
     count = lengths.shape[1]
+    rect, active = rows_buf, part
+    total = rows * size
     copies, loads = Copies(send, recv), Loads(load_sems)
     links, column = Links(size, rows, copies), Column(dp_size, copies)
-    total = rows * size
+    half = links.half
+    block = mixer.shape[0]
     greet(*links.peers, *column.ring, *column.pair)
-    rings = [
-        WeightRing(column, loads, merger, lambda i: out_out.at[i]),
-        WeightRing(column, loads, mixer, lambda i: mix_out.at[i]),
-    ]
-    for ring in rings:
-        ring.start()
-    gathers = []
+    mix_ring = WeightRing(
+        column, loads, mixer, lambda i: mix.at[pl.ds(pl.multiple_of(i * block, block), block)]
+    )
+    out_ring = WeightRing(
+        column,
+        loads,
+        merger,
+        lambda i: out.at[:, pl.ds(pl.multiple_of(i * block, block), block)],
+    )
+    mix_ring.start()
+    first_gathers = []
     for m in range(micro):
 
         def body(where, i, row, m=m):
             value = tokens[m, at(row), :].astype(F32)
             low = normalized(value)[0] * params[ATTEND : ATTEND + 1, :]
             low = (low + params[ATTEND + 1 : ATTEND + 2, :]).astype(BF16)
-            buf[at(m * total + where * links.second + i * STEP), :] = low
+            rows_buf[at(m * total + where * links.second + i * STEP), :] = low
 
         over_rows(links.half, body)
-        gathers.append(Gather(links, buf, m * total))
-        gathers[m].start()
-
-    half = links.half
+        first_gathers.append(Gather(links, rows_buf, m * total))
+        first_gathers[m].start()
+
     starts = [r * rows for r in links.first_ranks] + [r * rows + half for r in links.second_ranks]
 
     def slots(shape, dimension):
@@ -649,28 +690,24 @@
             return 0
 
         lax.fori_loop(0, total // chunk, table, 0)
-        if m == 0:
-            rings[0].advance()
-    for g in gathers:
+    for g in first_gathers:
         g.middle()
-    rings[1].advance()
-    if column.chips > 2:
-        rings[0].advance()
-    outs = []
+    mix_ring.advance()
+    outs, rows_saves = [], []
     usage[...] = jnp.zeros_like(usage)
     few = lax.broadcasted_iota(jnp.int32, (8, LANES), 1)
     which = lax.broadcasted_iota(jnp.int32, (8, LANES), 0)
     lane_own = lax.broadcasted_iota(jnp.int32, (half, LANES), 1)
-    for m, g in enumerate(gathers):
+    for m, g in enumerate(first_gathers):
         g.finish()
         here = pl.ds(m * total, total)
-        outs.append(loads.copy(buf.at[here], rows_out.at[here]))
+        rows_saves.append(loads.copy(rows_buf.at[here], rows_out.at[here]))
         sequence = lax.broadcasted_iota(jnp.int32, (8, total), 0)
         hot = jnp.where(member_rows[m] == sequence, 1.0, 0.0).astype(BF16)
         divisor = jnp.maximum(by_member(which, [lengths[m, s] for s in range(count)], 0), 1)
         divisor = divisor.astype(F32)
         chosen = by_member(which, [choices[m, s] for s in range(count)], 0)
-        means = dot(hot, buf[here, :]) / divisor[:, :1]
+        means = dot(hot, rows_buf[here, :]) / divisor[:, :1]
         logits = jnp.full((8, LANES), MASKED)
         for c in range(NHC):
             router = params[HEAD_ROUTER + c : HEAD_ROUTER + c + 1, :]
@@ -695,80 +732,21 @@
             value = jnp.where(lane_own == LIVE, live, value)
             own[m, pl.ds(where * half, half), :] = value
             usage[0:1, :] += jnp.sum(value * live, axis=0, keepdims=True)
-    for step in range(column.chips - 3):
-        for ring in reversed(rings):
-            ring.advance()
-    for ring in rings:
-        ring.finish()
-    wait_all(outs)
-
-
-def attend_kernel(
-    dp_size,
-    size,
-    heads,
-    rows_hbm,
-    mix_hbm,
-    out_hbm,
-    mask_hbm,
-    cosine,
-    sine,
-    row_info,
-    own,
-    tokens,
-    cotangent,
-    params,
-    expand,
-    shrink,
-    qkv_out,
-    heads_out,
-    attention_out,
-    second_out,
-    share_out,
-    branch_out,
-    up_out,
-    down_out,
-    rows_buf,
-    mix,
-    out,
-    mask,
-    qkv,
-    head_rows,
-    part,
-    landing,
-    staged,
-    last,
-    second_buf,
-    send,
-    recv,
-    load_sems,
-):
-    micro, rows, width = tokens.shape
-    total = rows * size
-    copies, loads = Copies(send, recv), Loads(load_sems)
-    links, column = Links(size, rows, copies), Column(dp_size, copies)
-    half = links.half
-    mix_copy = loads.copy(mix_hbm, mix)
-    row_copies = [
-        loads.copy(rows_hbm.at[pl.ds(m * total, total)], rows_buf.at[pl.ds(m * total, total)])
-        for m in range(micro)
-    ]
-    mask_copy = loads.copy(mask_hbm, mask)
-    out_copies = columns_in(loads, out_hbm, out)
-    greet(*links.peers, *column.ring, *column.pair)
-    early = shrink.shape[0] // 4
-    rings = [
-        WeightRing(column, loads, shrink.at[pl.ds(0, early)], lambda i: down_out.at[i]),
-        WeightRing(column, loads, expand, lambda i: up_out.at[i]),
-    ]
-    for ring in rings:
-        ring.start()
-    mix_copy.wait()
+    if column.chips > 2:
+        mix_ring.advance()
+    out_ring.start()
+    mix_ring.advance_all()
+    out_ring.advance()
+    mix_ring.finish()
+    outs.append(loads.copy(mix, mix_out))
+    up_ring = WeightRing(
+        column, loads, expand, lambda i: up.at[pl.ds(pl.multiple_of(i * block, block), block)]
+    )
+    down_ring = WeightRing(column, loads, shrink, lambda i: down_out.at[i])
     scale = HD ** (-0.5)
     span = 3 * HD
-    chunk = min(128, total)
     tile = min(512, width)
-    saves = []
+    saves = outs
 
     def project(m):
         base = m * total
@@ -855,24 +833,28 @@
             share_out[m, at(row), :] = share
             gate = NB * jnp.sum(share * info, axis=-1, keepdims=True)
             outer = cotangent[m, at(row), :].astype(F32) * info[:, LIVE : LIVE + 1]
-            branch_out[m, at(row), :] = (gate * outer).astype(BF16)
+            branch_buf[at(m * total + where * links.second + i * STEP), :] = (gate * outer).astype(
+                BF16
+            )
 
         over_rows(half, body)
 
     for m in range(micro):
-        row_copies[m].wait()
         project(m)
         if m == 0:
-            mask_copy.wait()
+            if column.chips > 2:
+                out_ring.advance()
+            up_ring.start()
         attend(m)
         if m == 0:
-            wait_all(out_copies)
-            rings[0].advance()
+            out_ring.finish()
+            outs.append(loads.copy(out, out_out))
         else:
             scatters[m - 1].middle()
         merge(m)
         scatters[m].start()
-    rings[1].advance()
+    branch_gathers = [Gather(links, branch_buf, m * total) for m in range(micro)]
+    up_ring.advance()
     for m in range(micro):
         scatters[m].finish()
         second_norm(m)
@@ -881,119 +863,69 @@
             scatters[m + 1].middle()
             gathers[m].middle()
             if column.chips > 2:
-                for ring in rings:
-                    ring.advance()
+                up_ring.advance()
+    down_ring.start()
     saves.append(loads.copy(qkv, qkv_out))
     saves.append(loads.copy(head_rows, heads_out))
     gathers[micro - 1].middle()
+    for g in branch_gathers:
+        g.start()
     for m in range(micro):
         gathers[m].finish()
         here = pl.ds(m * total, total)
         saves.append(loads.copy(second_buf.at[here], second_out.at[here]))
-    for ring in rings:
-        ring.finish()
-    wait_all(saves)
-
-
-def widen_kernel(
-    dp_size,
-    size,
-    unit_lane,
-    second_hbm,
-    up_hbm,
-    branch,
-    row_info,
-    shrink,
-    rect_out,
-    active_out,
-    branch_out,
-    down_out,
-    mine_out,
-    twin_out,
-    second_rows,
-    up,
-    branch_buf,
-    rect,
-    active,
-    tile,
-    send,
-    recv,
-    load_sems,
-    tile_sems,
-    twin_sem,
-):
-    micro, rows, width = branch.shape
-    total = rows * size
-    units = up.shape[1]
-    copies, loads = Copies(send, recv), Loads(load_sems)
-    links, column = Links(size, rows, copies), Column(dp_size, copies)
-    up_copy = loads.copy(up_hbm, up)
-    second_copies = [
-        loads.copy(second_hbm.at[pl.ds(m * total, total)], second_rows.at[pl.ds(m * total, total)])
-        for m in range(micro)
-    ]
-    half = links.half
-    own_copies = []
+    up_ring.finish()
+    saves.append(loads.copy(up, up_out))
+    wait_all(rows_saves)
+    step = min(512, units)
     for m in range(micro):
-        for where in range(2):
-            own_copies.append(
-                loads.copy(
-                    branch.at[m, pl.ds(where * half, half)],
-                    branch_buf.at[pl.ds(m * total + where * links.second, half)],
-                )
-            )
-    greet(*links.peers, *column.ring, *column.pair)
-    late = down_out.shape[1]
-    rest = shrink.at[pl.ds(shrink.shape[0] - late, late)]
-    ring = WeightRing(column, loads, rest, lambda i: down_out.at[i])
-    ring.start()
-    wait_all(own_copies)
-    gathers = [Gather(links, branch_buf, m * total) for m in range(micro)]
-    for g in gathers:
-        g.start()
-    up_copy.wait()
-    step = min(512, units)
-    saves = []
-    for m in range(micro):
-        second_copies[m].wait()
-
-        def body(j, _, m=m):
+
+        def widen(j, _, m=m):
             here = pl.ds(pl.multiple_of(j * step, step), step)
-            before = dot(second_rows[pl.ds(m * total, total), :], up[:, here])
-            kept = jnp.maximum(before, 0.0) * row_info[m, :, unit_lane : unit_lane + 1]
+            before = dot(second_buf[pl.ds(m * total, total), :], up[:, here])
+            kept = jnp.maximum(before, 0.0) * row_info[m, :, heads : heads + 1]
             rect[pl.ds(m * total, total), here] = kept.astype(BF16)
             active[pl.ds(m * total, total), here] = (kept * kept).astype(BF16)
             return 0
 
-        lax.fori_loop(0, units // step, body, 0)
-        gathers[m].middle()
+        lax.fori_loop(0, units // step, widen, 0)
         here = pl.ds(m * total, total)
-        saves.append(loads.copy(rect.at[here], rect_out.at[here]))
-        saves.append(loads.copy(active.at[here], active_out.at[here]))
-    ring.advance()
-    for m, g in enumerate(gathers):
+        saves.append(loads.copy(rect.at[here, pl.ds(0, units)], rect_out.at[here]))
+        saves.append(loads.copy(active.at[here, pl.ds(0, units)], active_out.at[here]))
+        if m == 0:
+            for g in branch_gathers:
+                g.middle()
+            down_ring.advance()
+    for m, g in enumerate(branch_gathers):
         g.finish()
         here = pl.ds(m * total, total)
         saves.append(loads.copy(branch_buf.at[here], branch_out.at[here]))
-        if m == 0 and column.chips > 2:
-            ring.advance()
-    block, wide = mine_out.shape[2], tile.shape[3]
+    wide = tile_out.shape[3]
 
     def make(c, put):
         value = dot_tn(active[:, pl.ds(pl.multiple_of(c * wide, wide), wide)], branch_buf[...])
         for j in range(dp_size):
             put(j, value[:, j * block : (j + 1) * block].astype(BF16))
 
-    halves_out(column, units // wide, make, tile, mine_out, twin_out, tile_sems, twin_sem)
-    ring.finish()
+    halves_out(
+        column,
+        units // wide,
+        make,
+        tile_out,
+        mine_out,
+        twin_out,
+        tile_sems,
+        twin_sem,
+        down_ring.advance if column.chips > 2 else None,
+    )
+    down_ring.finish()
     wait_all(saves)
 
 
 def narrow_kernel(
     dp_size,
     size,
-    down_early,
-    down_late,
+    down_hbm,
     up_hbm,
     active_hbm,
     rect_hbm,
@@ -1061,9 +993,7 @@
         sum_sems,
     )
     ring.load()
-    early = down_early.shape[1]
-    down_copies = columns_in(loads, down_early, down.at[pl.ds(0, early)])
-    down_copies += columns_in(loads, down_late, down.at[pl.ds(early, units - early)])
+    down_copies = columns_in(loads, down_hbm, down)
     active_copies = [loads.copy(active_hbm.at[h], active.at[h]) for h in here]
     branch_copies = [loads.copy(branch_hbm.at[h], shared_rows.at[h]) for h in here]
     rect_copy = loads.copy(rect_hbm.at[here[0]], rect)
@@ -1291,7 +1221,7 @@
                     buf.at[pl.ds(m * total + where * links.second, half)],
                 )
             )
-    out_copies = columns_in(loads, out_hbm, out)
+    out_copies = [loads.copy(out_hbm, out)]
     qkv_copy = loads.copy(qkv_hbm, qkv)
     mask_copy = loads.copy(mask_hbm, mask)
     heads_copy = loads.copy(heads_hbm, head_rows)
@@ -1562,11 +1492,17 @@
     rates = jnp.concatenate([rates, rates])[None]
 
     tables = (micro, total, LANES)
-    first_rows, mix_weight, out_weight, mask, cosine, sine, row_info, own, seq_info, usage = call(
-        functools.partial(first_norm_kernel, dp_size, size, heads, units),
-        1,
+    lands = half * (2 * (high - 1) + high)
+    stages = half * high
+    wide_heads = heads * HD
+    span = 3 * wide_heads
+    buffers = [((micro, lands, width), BF16), ((micro, stages, width), BF16), ((micro, stages, width), BF16)]
+    attended = call(
+        functools.partial(attend_kernel, dp_size, size, heads, units),
+        2,
         [
             (tokens, True),
+            (cotangent, True),
             (params, True),
             (rates, True),
             (width_bucket, True),
@@ -1574,11 +1510,13 @@
             (head_choice, "s"),
             (mixer, False),
             (merger, False),
+            (expand, False),
+            (shrink, False),
         ],
         [
             ((every, width), BF16, False),
-            ((dp_size,) + mixer.shape, BF16, False),
-            ((dp_size,) + merger.shape, BF16, False),
+            ((width, span), BF16, False),
+            ((wide_heads, width), BF16, False),
             ((micro, total, total), F32, True),
             (tables, F32, True),
             (tables, F32, True),
@@ -1586,107 +1524,53 @@
             ((micro, rows, LANES), F32, True),
             ((micro, 8, LANES), F32, True),
             ((8, LANES), F32, True),
+            ((micro, 3, total, wide_heads), BF16, False),
+            ((every, wide_heads), BF16, False),
+            ((micro, rows, width), F32, True),
+            ((every, width), BF16, False),
+            ((micro, rows, LANES), F32, True),
+            ((width, units), BF16, False),
+            ((dp_size, units, block), BF16, False),
+            ((every, units), BF16, False),
+            ((every, units), BF16, False),
+            ((every, width), BF16, False),
+            ((chips, units, block), BF16, False),
+            ((chips, units, block), BF16, False),
         ],
         [
             ((every, width), BF16),
             ((total, LANES), jnp.int32),
             (tables, jnp.int32),
             (tables, F32),
-        ],
-        micro * few + 2 * ringed,
-        micro + 2,
-    )
-    mix_weight = mix_weight.reshape(width, -1)
-
-    lands = half * (2 * (high - 1) + high)
-    stages = half * high
-    wide_heads = heads * HD
-    span = 3 * wide_heads
-    buffers = [((micro, lands, width), BF16), ((micro, stages, width), BF16), ((micro, stages, width), BF16)]
-    qkv, head_rows, attention, second_rows, width_share, branch_own, up_weight, down_early = call(
-        functools.partial(attend_kernel, dp_size, size, heads),
-        2,
-        [
-            (first_rows, False),
-            (mix_weight, False),
-            (out_weight, False),
-            (mask, False),
-            (cosine, True),
-            (sine, True),
-            (row_info, True),
-            (own, True),
-            (tokens, True),
-            (cotangent, True),
-            (params, True),
-            (expand, False),
-            (shrink, False),
-        ],
-        [
-            ((micro, 3, total, wide_heads), BF16, False),
-            ((every, wide_heads), BF16, False),
-            ((micro, rows, width), F32, True),
-            ((every, width), BF16, False),
-            ((micro, rows, LANES), F32, True),
-            ((micro, rows, width), BF16, True),
-            ((dp_size,) + expand.shape, BF16, False),
-            ((dp_size, units // 4, block), BF16, False),
-        ],
-        [
-            ((every, width), BF16),
             ((width, span), BF16),
             ((wide_heads, width), BF16),
-            ((micro, total, total), F32),
             ((micro, 3, total, wide_heads), BF16),
             ((every, wide_heads), BF16),
             ((every, width), BF16),
         ]
         + buffers
-        + [((every, width), BF16)],
-        2 * micro * few + 2 * ringed,
-        2 + micro + dp_size + 2 + micro + 2,
-        flops=2 * every * width * (span + wide_heads) + 8 * heads * micro * total * total * HD,
-    )
-
-    up_weight = up_weight.reshape(width, -1)
-    unit_tile = 256
-    rect, active, branch_rows, down_late, down_mine, down_twin = call(
-        functools.partial(widen_kernel, dp_size, size, heads),
-        3,
-        [
-            (second_rows, False),
-            (up_weight, False),
-            (branch_own, False),
-            (row_info, True),
-            (shrink, False),
-        ],
-        [
-            ((every, units), BF16, False),
-            ((every, units), BF16, False),
-            ((every, width), BF16, False),
-            ((dp_size, units - units // 4, block), BF16, False),
-            ((chips, units, block), BF16, False),
-            ((chips, units, block), BF16, False),
-        ],
-        [
+        + [
             ((every, width), BF16),
             ((width, units), BF16),
             ((every, width), BF16),
-            ((every, units), BF16),
-            ((every, units), BF16),
-            ((2, 2, chips, unit_tile, block), BF16),
+            ((2, 2, chips, min(256, units), block), BF16),
         ],
-        micro * few + ringed,
-        2 + 6 * micro,
+        4 * micro * few + 4 * ringed,
+        4 + micro + 2 + 2 + micro + 1 + 3 * micro,
         (4, 1),
-        flops=4 * every * width * units,
+        flops=2 * every * width * (span + wide_heads + 2 * units),
+        limit=63,
     )
+    first_rows, mix_weight, out_weight, mask, cosine, sine, row_info = attended[:7]
+    own, seq_info, usage, qkv, head_rows, attention, second_rows = attended[7:14]
+    width_share, up_weight, down_weight, rect, active, branch_rows = attended[14:20]
+    down_mine, down_twin = attended[20:]
 
     narrowed = call(
         functools.partial(narrow_kernel, dp_size, size),
         4,
         [
-            (down_early, False),
-            (down_late, False),
+            (down_weight, False),
             (up_weight, False),
             (active, False),
             (rect, False),
@@ -1728,7 +1612,7 @@
         ]
         + sum_scratch(chips, units, block),
         2 * micro * few + chips,
-        2 * dp_size + 4 * micro + 1 + 2 * chips + 2,
+        dp_size + 4 * micro + 1 + 2 * chips + 2,
         (2, chips, SUM_TILES),
         flops=8 * every * width * units,
         limit=63,

time: 514 us -> 504 us (0.981)
  Pallas kernels: 489 us -> 478 us
    pallas_call x5 -> x3, Pallas kernels: 489 us -> 478 us  [call(): pl.pallas_call(kernel, out_shape=[jax.ShapeDtypeStruct(shape, kind) for s...]
where the time goes in v5:
time: 504 us; the launch traced here: 495 us
  Pallas kernels  478 us (95%)
  local copies, waits for them, and re-layouts  13.2 us (3%)
    pallas_call x3, Pallas kernels, call(): pl.pallas_call(kernel, out_shape=[jax.ShapeDtypeStruct(shape, kind) for s...  478 us

profile of v5, /device:TPU:1, one launch (start us, length us, event | category | flops | bytes accessed | tf_op | source)
XLA Modules:
  0.0 495.1 jit_solution(5718915120597087860)
XLA Ops:
  0.7 0.6 maximum_bitcast_fusion.1.rates
  1.2 0.8 pad_maximum_fusion
  2.0 0.8 maximum_bitcast_fusion
  2.8 0.7 maximum_convert_fusion.params
  3.5 228.5 %shard_map.254 = (bf16[1024,2048]{1,0:T(8,128)(2,1)}, bf16[2048,1536]{1,0:T(8,128)(2,1)}, bf16[512,2048]{1,0:T(8,128)(2,1)}, f32[2,512,512]{2,1,0:T(8,128)}, f32...) custom-call(bf16[2,128,2048]{2,1,0:T(8,128)(2,1)} %tokens.5, ...), custom_call_target="tpu_custom_call" | custom-call | flops 25769803776 | bytes 5345856 | tf_op jit(solution)/shard_map/pallas_call | solution.py:1443
  232.0 105.4 %shard_map.255 = (bf16[2,128,2048]{2,1,0:T(8,128)(2,1)}, bf16[4,256,2048]{2,1,0:T(8,128)(2,1)}, bf16[4,256,2048]{2,1,0:T(8,128)(2,1)}, f32[2,128,2048]{2,1,0:T(8...) custom-call(bf16[8,2048,256]{2,1,0:T(8,128)(2,1)} %get-tuple-element, ...), custom_call_target="tpu_custom_call" | custom-call | flops 34359738368 | bytes 46497792 | tf_op jit(solution)/shard_map/pallas_call | solution.py:1443
  337.4 144.0 %shard_map.256 = (f32[2,128,2048]{2,1,0:T(8,128)}, f32[256,2048]{1,0:T(8,128)}, f32[256,1536]{1,0:T(8,128)}, f32[512,256]{1,0:T(8,128)}, f32[16,2048]{1,0:T(8,12...) custom-call(bf16[2,128,2048]{2,1,0:T(8,128)(2,1)} %get-tuple-element, ...), custom_call_target="tpu_custom_call" | custom-call | flops 22548578304 | bytes 34390016 | tf_op jit(solution)/shard_map/pallas_call | solution.py:1443
  481.5 0.0 copy-start.2
  481.5 1.4 slice_bitcast_fusion.2
  482.9 1.6 fusion
  484.5 1.5 slice_bitcast_fusion
  486.0 0.0 copy-start.3
  486.0 2.4 copy.35
  488.4 0.0 copy-done.2
  488.4 0.0 copy-start.4
  488.4 1.3 copy.36
  489.8 0.0 copy-done.3
  489.8 0.0 copy-start.1
  489.8 1.1 copy.37
  490.9 0.0 copy-done.4
  490.9 0.0 copy-start
  490.9 0.8 copy.38
  491.7 0.3 copy-done.1
  492.0 1.3 copy.39
  493.3 0.0 copy-done
  493.3 1.3 copy.40
  (2 shorter events, 0.0 us)
Async XLA Ops:
  481.5 7.0 %copy-start.2 = (f32[2,128,2048]{2,1,0:T(8,128)S(1)}, f32[2,128,2048]{2,1,0:T(8,128)}, u32[]{:S(2)}) copy-start(f32[2,128,2048]{2,1,0:T(8,128)} %get-tuple-element.109) | copy-start | bytes 6291460
  486.0 3.8 copy-start.3
  488.4 2.5 copy-start.4
  489.8 2.2 copy-start.1
  490.9 2.4 copy-start

commit v6 on v5

--- a/solution.py
+++ b/solution.py
@@ -948,6 +948,7 @@
     gate_out,
     sum_out,
     landed_out,
+    gathered_out,
     down,
     up,
     active,
@@ -1104,7 +1105,11 @@
             stats_out[1:2, :] += jnp.sum(back, axis=0, keepdims=True)
             hidden_back = outer + norm_back(back, normed, inverse, gain)
             hidden_out[m, at(row), :] = hidden_back
-            back_out[m, at(row), :] = (info[:, GATE : GATE + 1] * hidden_back).astype(BF16)
+            attention_back = (info[:, GATE : GATE + 1] * hidden_back).astype(BF16)
+            if m == 0:
+                shared_rows[at(where * links.second + i * STEP), :] = attention_back
+            else:
+                back_out[m - 1, at(row), :] = attention_back
             gate_part = jnp.sum(hidden_back * attended, axis=-1, keepdims=True)
             gate_out[m : m + 1, :] += jnp.sum(info * gate_part, axis=0, keepdims=True)
 
@@ -1134,10 +1139,17 @@
         finish_out(m)
     for m in range(micro):
         backs[m].middle()
+    gather = Gather(links, shared_rows, 0)
     for m in range(micro):
         finish_back(m)
+        if m == 0:
+            gather.start()
+    gather.middle()
     ring.finish()
+    gather.finish()
+    save = loads.copy(shared_rows.at[pl.ds(0, total)], gathered_out)
     up_ring.hop.wait()
+    save.wait()
 
 
 STATS_ONE = 6
@@ -1151,6 +1163,7 @@
     size,
     heads,
     back,
+    gathered_hbm,
     gate,
     out_hbm,
     qkv_hbm,
@@ -1203,7 +1216,7 @@
     stats, share, pieces, sums, whole = rest[15:20]
     send, recv, load_sems = rest[20:23]
     out_sems, out_twin_sem, mix_sems, mix_twin_sem, up_sum_sems, mix_sum_sems, out_sum_sems = rest[23:]
-    micro, rows, width = back.shape
+    micro, rows, width = tokens.shape
     total = rows * size
     copies, loads = Copies(send, recv), Loads(load_sems)
     links, column = Links(size, rows, copies), Column(dp_size, copies)
@@ -1212,12 +1225,13 @@
     mix_ring = SumRing(column, loads, mix_mine, mix_twin, mix_sum, *mix_bufs, mix_sum_sems)
     out_ring = SumRing(column, loads, out_mine, out_twin, out_sum, *out_bufs, out_sum_sems)
     ring.prepare(landed_hbm)
+    first_copy = loads.copy(gathered_hbm, buf.at[pl.ds(0, total)])
     own_copies = []
-    for m in range(micro):
+    for m in range(1, micro):
         for where in range(2):
             own_copies.append(
                 loads.copy(
-                    back.at[m, pl.ds(where * half, half)],
+                    back.at[m - 1, pl.ds(where * half, half)],
                     buf.at[pl.ds(m * total + where * links.second, half)],
                 )
             )
@@ -1232,8 +1246,9 @@
     far = [lax.rem(column.me + s, dp_size) for s in range(1, dp_size)]
     greet(*[("tensor", to) for to in near], *[("dp", to) for to in far])
     wait_all(own_copies)
-    gathers = [Gather(links, buf, m * total) for m in range(micro)]
-    gathers[0].start()
+    gathers = [Gather(links, buf, m * total) for m in range(1, micro)]
+    for g in gathers:
+        g.start()
     ring.resume()
     gate_copies = [links.copy(gate, gates.at[links.me], peer) for peer in near]
     stats[...] = jnp.zeros_like(stats)
@@ -1244,9 +1259,6 @@
     mask_copy.wait()
     scale = HD ** (-0.5)
     chunk = min(128, total)
-    gathers[0].middle()
-    for g in gathers[1:]:
-        g.start()
     block, wide = out_mine.shape[2], out_tile.shape[3]
     here_rows = [pl.ds(m * total, total) for m in range(micro)]
     scatters = [
@@ -1288,10 +1300,8 @@
             mixed_back[every, pl.ds(col + HD, HD)] = turned(keys_back, cos, sin).astype(BF16)
             mixed_back[every, pl.ds(col + 2 * HD, HD)] = values_back.astype(BF16)
             if m == 0 and h == 0:
-                for g in gathers[1:]:
+                for g in gathers:
                     g.middle()
-                if column.chips > 3:
-                    ring.advance()
 
     def make_out(c, put):
         value = dot_tn(head_rows[:, pl.ds(pl.multiple_of(c * wide, wide), wide)], buf[...])
@@ -1314,9 +1324,9 @@
         lax.fori_loop(0, width // tile, body, 0)
         scatters[m].start()
 
-    gathers[0].finish()
+    first_copy.wait()
     heads_part(0)
-    for g in gathers[1:]:
+    for g in gathers:
         g.finish()
     heads_copy.wait()
     halves_out(
@@ -1329,6 +1339,8 @@
         out_sems,
         out_twin_sem,
     )
+    if column.chips > 3:
+        ring.advance()
     out_ring.load()
     out_ring.start()
     mix_copy.wait()
@@ -1336,8 +1348,6 @@
     for m in range(1, micro):
         heads_part(m)
     scatters[0].middle()
-    if column.chips > 2:
-        out_ring.advance()
     rows_copy.wait()
 
     def start_mix():
@@ -1346,7 +1356,7 @@
 
     blocks_out(column, make_mix, mix_tile, mix_mine, mix_twin, mix_sems, mix_twin_sem, start_mix)
     mix_ring.load()
-    if column.chips > 3:
+    if column.chips > 2:
         out_ring.advance()
     for m in range(1, micro):
         first_part(m)
@@ -1391,11 +1401,15 @@
 
         over_rows(links.half, body)
 
-    last_rows(0)
+    if column.chips > 3:
+        out_ring.advance()
     if column.chips > 2:
         mix_ring.advance()
+    last_rows(0)
     for s in scatters[1:]:
         s.middle()
+    if column.chips > 3:
+        mix_ring.advance()
     ring.finish()
     for m in range(1, micro):
         last_rows(m)
@@ -1416,9 +1430,8 @@
     share[0] = value
     sums[column.me] = value
     sent = [column.copy(share.at[0], sums.at[column.me], to) for to in far]
-    if column.chips > 3:
-        mix_ring.advance()
     out_ring.finish()
+    mix_ring.finish()
     wait_all(sent)
     value = sums[0]
     for r in range(1, dp_size):
@@ -1428,7 +1441,6 @@
     wait_all([links.copy(share.at[1], whole.at[links.me], to) for to in near])
     for r in range(size):
         stats_out[:, r * piece : (r + 1) * piece] = whole[r]
-    mix_ring.finish()
 
 
 ANY = pl.BlockSpec(memory_space=pl.ANY)
@@ -1590,11 +1602,12 @@
             ((chips, block, units), BF16, False),
             ((chips, block, units), BF16, False),
             ((micro, rows, width), F32, True),
-            ((micro, rows, width), BF16, True),
+            ((micro - 1, rows, width), BF16, True),
             ((8, width), F32, True),
             ((8, LANES), F32, True),
             ((units, block), F32, False),
             ((1, block, units), BF16, False),
+            ((total, width), BF16, False),
         ],
         [
             ((units, width), BF16),
@@ -1611,14 +1624,14 @@
             ((2, block, units), BF16),
         ]
         + sum_scratch(chips, units, block),
-        2 * micro * few + chips,
-        dp_size + 4 * micro + 1 + 2 * chips + 2,
+        2 * micro * few + few + chips,
+        dp_size + 4 * micro + 1 + 2 * chips + 3,
         (2, chips, SUM_TILES),
         flops=8 * every * width * units,
         limit=63,
     )
     block_output, up_mine, up_twin, hidden_back, back_own, stats_two, gate_part = narrowed[:7]
-    down_sum, up_landed = narrowed[7:]
+    down_sum, up_landed, back_rows = narrowed[7:]
 
     out_tile = min(256, wide_heads)
     lasts = call(
@@ -1626,6 +1639,7 @@
         5,
         [
             (back_own, False),
+            (back_rows, False),
             (gate_part, True),
             (out_weight, False),
             (qkv, False),

time: 504 us -> 498 us (0.988)
  the two profiles are of different devices: /device:TPU:1 before, /device:TPU:0 now
where the time goes in v6:
time: 498 us; the launch traced here: 488 us
  Pallas kernels  471 us (95%)
  local copies, waits for them, and re-layouts  13.2 us (3%)
    pallas_call x3, Pallas kernels, call(): pl.pallas_call(kernel, out_shape=[jax.ShapeDtypeStruct(shape, kind) for s...  471 us

profile of v6, /device:TPU:0, one launch (start us, length us, event | category | flops | bytes accessed | tf_op | source)
XLA Modules:
  0.0 488.4 jit_solution(12325541707764988446)
XLA Ops:
  0.7 0.6 maximum_bitcast_fusion.1.rates
  1.2 0.7 pad_maximum_fusion
  2.0 0.8 maximum_bitcast_fusion
  2.8 0.7 maximum_convert_fusion.params
  3.4 228.6 %shard_map.254 = (bf16[1024,2048]{1,0:T(8,128)(2,1)}, bf16[2048,1536]{1,0:T(8,128)(2,1)}, bf16[512,2048]{1,0:T(8,128)(2,1)}, f32[2,512,512]{2,1,0:T(8,128)}, f32...) custom-call(bf16[2,128,2048]{2,1,0:T(8,128)(2,1)} %tokens.5, ...), custom_call_target="tpu_custom_call" | custom-call | flops 25769803776 | bytes 5345856 | tf_op jit(solution)/shard_map/pallas_call | solution.py:1455
  232.0 107.2 %shard_map.255 = (bf16[2,128,2048]{2,1,0:T(8,128)(2,1)}, bf16[4,256,2048]{2,1,0:T(8,128)(2,1)}, bf16[4,256,2048]{2,1,0:T(8,128)(2,1)}, f32[2,128,2048]{2,1,0:T(8...) custom-call(bf16[8,2048,256]{2,1,0:T(8,128)(2,1)} %get-tuple-element, ...), custom_call_target="tpu_custom_call" | custom-call | flops 34359738368 | bytes 46497792 | tf_op jit(solution)/shard_map/pallas_call | solution.py:1455
  339.3 135.5 %shard_map.256 = (f32[2,128,2048]{2,1,0:T(8,128)}, f32[256,2048]{1,0:T(8,128)}, f32[256,1536]{1,0:T(8,128)}, f32[512,256]{1,0:T(8,128)}, f32[16,2048]{1,0:T(8,12...) custom-call(bf16[1,128,2048]{2,1,0:T(8,128)(2,1)} %get-tuple-element, ...), custom_call_target="tpu_custom_call" | custom-call | flops 22548578304 | bytes 35962880 | tf_op jit(solution)/shard_map/pallas_call | solution.py:1455
  474.8 0.0 copy-start.2
  474.8 1.4 slice_bitcast_fusion.2
  476.2 1.6 fusion
  477.8 1.5 slice_bitcast_fusion
  479.3 0.0 copy-start.3
  479.3 2.4 copy.35
  481.8 0.0 copy-done.2
  481.8 0.0 copy-start.4
  481.8 1.3 copy.36
  483.1 0.0 copy-done.3
  483.1 0.0 copy-start.1
  483.1 1.1 copy.37
  484.2 0.0 copy-done.4
  484.2 0.0 copy-start
  484.2 0.8 copy.38
  485.0 0.3 copy-done.1
  485.3 1.3 copy.39
  486.7 0.0 copy-done
  486.7 1.3 copy.40
  (2 shorter events, 0.0 us)
Async XLA Ops:
  474.8 7.0 %copy-start.2 = (f32[2,128,2048]{2,1,0:T(8,128)S(1)}, f32[2,128,2048]{2,1,0:T(8,128)}, u32[]{:S(2)}) copy-start(f32[2,128,2048]{2,1,0:T(8,128)} %get-tuple-element.111) | copy-start | bytes 6291460
  479.3 3.8 copy-start.3
  481.8 2.5 copy-start.4
  483.1 2.2 copy-start.1
  484.2 2.4 copy-start

commit v7 on v6

--- a/solution.py
+++ b/solution.py
@@ -555,16 +555,16 @@
     rows_out,
     mix_out,
     out_out,
-    mask,
-    cosine,
-    sine,
-    row_info,
+    mask_hbm,
+    cosine_hbm,
+    sine_hbm,
+    info_hbm,
     own,
     seq_info,
     usage,
     qkv_out,
     heads_out,
-    attention_out,
+    attention_hbm,
     second_out,
     share_out,
     up_out,
@@ -590,6 +590,11 @@
     up,
     branch_buf,
     tile_out,
+    mask,
+    cosine,
+    sine,
+    row_info,
+    attention_out,
     send,
     recv,
     load_sems,
@@ -865,6 +870,14 @@
             if column.chips > 2:
                 up_ring.advance()
     down_ring.start()
+    saves.append(loads.copy(attention_out, attention_hbm))
+    for here, there in (
+        (mask, mask_hbm),
+        (cosine, cosine_hbm),
+        (sine, sine_hbm),
+        (row_info, info_hbm),
+    ):
+        saves.append(loads.copy(here, there))
     saves.append(loads.copy(qkv, qkv_out))
     saves.append(loads.copy(head_rows, heads_out))
     gathers[micro - 1].middle()
@@ -1178,7 +1191,7 @@
     twin_hbm,
     landed_hbm,
     tokens,
-    hidden_back,
+    hidden_hbm,
     own,
     seq_info,
     params,
@@ -1210,6 +1223,7 @@
     landing,
     staged,
     last,
+    hidden_back,
     *rest,
 ):
     up_bufs, mix_bufs, out_bufs = rest[:5], rest[5:10], rest[10:15]
@@ -1241,6 +1255,7 @@
     heads_copy = loads.copy(heads_hbm, head_rows)
     rows_copy = loads.copy(rows_hbm, rows_buf)
     mix_copy = loads.copy(mix_hbm, mix)
+    hidden_copy = loads.copy(hidden_hbm, hidden_back)
     gates[links.me] = gate[...]
     near = [lax.rem(links.me + s, size) for s in range(1, size)]
     far = [lax.rem(column.me + s, dp_size) for s in range(1, dp_size)]
@@ -1344,6 +1359,7 @@
     out_ring.load()
     out_ring.start()
     mix_copy.wait()
+    hidden_copy.wait()
     first_part(0)
     for m in range(1, micro):
         heads_part(m)
@@ -1529,16 +1545,16 @@
             ((every, width), BF16, False),
             ((width, span), BF16, False),
             ((wide_heads, width), BF16, False),
-            ((micro, total, total), F32, True),
-            (tables, F32, True),
-            (tables, F32, True),
-            (tables, F32, True),
+            ((micro, total, total), F32, False),
+            (tables, F32, False),
+            (tables, F32, False),
+            (tables, F32, False),
             ((micro, rows, LANES), F32, True),
             ((micro, 8, LANES), F32, True),
             ((8, LANES), F32, True),
             ((micro, 3, total, wide_heads), BF16, False),
             ((every, wide_heads), BF16, False),
-            ((micro, rows, width), F32, True),
+            ((micro, rows, width), F32, False),
             ((every, width), BF16, False),
             ((micro, rows, LANES), F32, True),
             ((width, units), BF16, False),
@@ -1566,9 +1582,14 @@
             ((width, units), BF16),
             ((every, width), BF16),
             ((2, 2, chips, min(256, units), block), BF16),
+            ((micro, total, total), F32),
+            (tables, F32),
+            (tables, F32),
+            (tables, F32),
+            ((micro, rows, width), F32),
         ],
         4 * micro * few + 4 * ringed,
-        4 + micro + 2 + 2 + micro + 1 + 3 * micro,
+        4 + micro + 2 + 2 + micro + 1 + 3 * micro + 5,
         (4, 1),
         flops=2 * every * width * (span + wide_heads + 2 * units),
         limit=63,
@@ -1654,7 +1675,7 @@
             (up_twin, False),
             (up_landed, False),
             (tokens, True),
-            (hidden_back, True),
+            (hidden_back, False),
             (own, True),
             (seq_info, True),
             (params, True),
@@ -1689,6 +1710,7 @@
             ((width, span), BF16),
         ]
         + buffers
+        + [((micro, rows, width), F32)]
         + sum_scratch(chips, block, units)
         + sum_scratch(chips, block, span)
         + sum_scratch(chips, wide_heads, block)
@@ -1700,7 +1722,7 @@
             ((size, STATS_ROWS, width // size), F32),
         ],
         2 * micro * few + 3 * (size - 1) + dp_size - 1 + 3 * (chips - 1),
-        2 * micro + dp_size + 6 + 6 * chips,
+        2 * micro + dp_size + 7 + 6 * chips,
         (4, 1, 2, chips, SUM_TILES, SUM_TILES, SUM_TILES),
         flops=4 * every * width * (wide_heads + span) + 20 * heads * micro * total * total * HD,
         limit=63,

time: 498 us -> 496 us (level)
  no operation moved by 1% of the time
where the time goes in v7:
time: 496 us; the launch traced here: 486 us
  Pallas kernels  469 us (95%)
  local copies, waits for them, and re-layouts  13.2 us (3%)
    pallas_call x3, Pallas kernels, call(): pl.pallas_call(kernel, out_shape=[jax.ShapeDtypeStruct(shape, kind) for s...  469 us

profile of v7, /device:TPU:0, one launch (start us, length us, event | category | flops | bytes accessed | tf_op | source)
XLA Modules:
  0.0 486.1 jit_solution(11937830503962089313)
XLA Ops:
  0.7 0.6 maximum_bitcast_fusion.1.rates
  1.2 0.7 pad_maximum_fusion
  2.0 0.8 maximum_bitcast_fusion
  2.8 0.7 maximum_convert_fusion.params
  3.4 226.8 %shard_map.254 = (bf16[1024,2048]{1,0:T(8,128)(2,1)}, bf16[2048,1536]{1,0:T(8,128)(2,1)}, bf16[512,2048]{1,0:T(8,128)(2,1)}, f32[2,512,512]{2,1,0:T(8,128)}, f32...) custom-call(bf16[2,128,2048]{2,1,0:T(8,128)(2,1)} %tokens.5, ...), custom_call_target="tpu_custom_call" | custom-call | flops 25769803776 | bytes 5345856 | tf_op jit(solution)/shard_map/pallas_call | solution.py:1471
  230.2 107.2 %shard_map.255 = (bf16[2,128,2048]{2,1,0:T(8,128)(2,1)}, bf16[4,256,2048]{2,1,0:T(8,128)(2,1)}, bf16[4,256,2048]{2,1,0:T(8,128)(2,1)}, f32[2,128,2048]{2,1,0:T(8...) custom-call(bf16[8,2048,256]{2,1,0:T(8,128)(2,1)} %get-tuple-element, ...), custom_call_target="tpu_custom_call" | custom-call | flops 34359738368 | bytes 46497792 | tf_op jit(solution)/shard_map/pallas_call | solution.py:1471
  337.5 135.0 %shard_map.256 = (f32[2,128,2048]{2,1,0:T(8,128)}, f32[256,2048]{1,0:T(8,128)}, f32[256,1536]{1,0:T(8,128)}, f32[512,256]{1,0:T(8,128)}, f32[16,2048]{1,0:T(8,12...) custom-call(bf16[1,128,2048]{2,1,0:T(8,128)(2,1)} %get-tuple-element, ...), custom_call_target="tpu_custom_call" | custom-call | flops 22548578304 | bytes 35962880 | tf_op jit(solution)/shard_map/pallas_call | solution.py:1471
  472.5 0.0 copy-start.2
  472.5 1.4 slice_bitcast_fusion.2
  473.9 1.6 fusion
  475.5 1.5 slice_bitcast_fusion
  477.0 0.0 copy-start.3
  477.0 2.4 copy.35
  479.5 0.0 copy-done.2
  479.5 0.0 copy-start.4
  479.5 1.3 copy.36
  480.8 0.0 copy-done.3
  480.8 0.0 copy-start.1
  480.8 1.1 copy.37
  481.9 0.0 copy-done.4
  481.9 0.0 copy-start
  481.9 0.8 copy.38
  482.7 0.3 copy-done.1
  483.0 1.3 copy.39
  484.4 0.0 copy-done
  484.4 1.3 copy.40
  (2 shorter events, 0.0 us)
Async XLA Ops:
  472.5 7.0 %copy-start.2 = (f32[2,128,2048]{2,1,0:T(8,128)S(1)}, f32[2,128,2048]{2,1,0:T(8,128)}, u32[]{:S(2)}) copy-start(f32[2,128,2048]{2,1,0:T(8,128)} %get-tuple-element.111) | copy-start | bytes 6291460
  477.0 3.8 copy-start.3
  479.5 2.5 copy-start.4
  480.8 2.2 copy-start.1
  481.9 2.4 copy-start
